TPU v7x, 128 devices: a whole 4x4x4 slice. The times are simulated.
128 devices in a mesh: dp: 16 (over z, y_lo, core), rows: 8 (over x, y_hi).
Axes of the slice: x: 4, y: 4 (y_hi: 2, y_lo: 2; y = y_hi * 2 + y_lo), z: 4, core: 2. Of those that a mesh axis runs over, the one named last changes fastest.
Arguments:
- features: bfloat16 [16, 1, 16, 128, 384], P('dp', None, 'rows'), may hold values from -6 to 6
- past_frames: bfloat16 [16, 2, 16, 128, 384], P('dp', None, 'rows'), may hold values from -6 to 6
- upstream: bfloat16 [16, 1, 16, 128, 384], P('dp', None, 'rows'), may hold values from -6 to 6
- query_weight: bfloat16 [384, 384], replicated, may hold values from -8 to 8
- key_weight: bfloat16 [384, 384], replicated, may hold values from -8 to 8
- value_weight: bfloat16 [384, 384], replicated, may hold values from -0.3125 to 0.3125
- out_weight: bfloat16 [384, 384], replicated, may hold values from -0.3125 to 0.3125
- conv_weight: bfloat16 [384, 27, 384], P(('dp', 'rows')), may hold values from -0.0625 to 0.0625
Outputs:
- feature_grad: bfloat16 [16, 1, 16, 128, 384], P('dp', None, 'rows')
- proj_grads: float32 [384, 1536], P(('dp', 'rows'))
- conv_grad: float32 [384, 10368], P(('dp', 'rows'))
All inputs are finite; a program needn't handle non-finite values.
Results may differ from a plain program's by a relative error of at most 0.015.
Values may be sent and summed in bfloat16 or wider, within the bound.
No kernel may reach another device: no remote copies, remote signals or barrier semaphores. Data moves between devices by JAX's collectives and lax.ppermute only.
A program may use at most 128 MiB of HBM per device.

v0:
```python
import jax
import jax.numpy as jnp
from jax import lax
from jax.sharding import PartitionSpec as P


def extended(block, sides, width):
    for axis, dim in sides:
        count = lax.axis_size(axis)
        forward = [(i, i + 1) for i in range(count - 1)]
        backward = [(target, source) for source, target in forward]
        low = lax.ppermute(
            lax.slice_in_dim(block, block.shape[dim] - width, None, axis=dim), axis, forward
        )
        high = lax.ppermute(lax.slice_in_dim(block, 0, width, axis=dim), axis, backward)
        block = jnp.concatenate([low, block, high], axis=dim)
    return block


def shards(
    features, past_frames, upstream, query_weight, key_weight, value_weight, out_weight, conv_weight
):
    f32 = jnp.float32
    bf16 = jnp.bfloat16
    conv_whole = lax.all_gather(conv_weight, ("dp", "rows"), axis=0, tiled=True)
    feats = features[0]
    frames, rows_here, width, chans = feats.shape
    xf = feats.astype(f32)
    recip = lax.rsqrt(jnp.mean(xf * xf, -1, keepdims=True) + 1e-06)
    normed = (xf * recip).astype(bf16)
    tokens = normed.reshape(frames, rows_here * width, chans)

    def project(weight):
        return jnp.einsum("ftc,cd->ftd", tokens, weight, preferred_element_type=f32).astype(bf16)

    query, key, value = (project(query_weight), project(key_weight), project(value_weight))
    keys_all, values_all = (
        lax.all_gather(key, "rows", axis=1, tiled=True),
        lax.all_gather(value, "rows", axis=1, tiled=True),
    )
    scale = chans ** (-0.5)
    scores = jnp.einsum("fqd,fkd->fqk", query, keys_all, preferred_element_type=f32) * scale
    probs = jax.nn.softmax(scores, -1)
    probs_b = probs.astype(bf16)
    attended = jnp.einsum("fqk,fkd->fqd", probs_b, values_all, preferred_element_type=f32).astype(
        bf16
    )
    mixed = (
        xf.reshape(frames, -1, chans)
        + jnp.einsum("ftd,de->fte", attended, out_weight, preferred_element_type=f32)
    ).astype(bf16)
    mixed = mixed.reshape(frames, rows_here, width, chans)
    stacked = jnp.concatenate([past_frames[0], mixed], 0)
    grad_out = upstream[0]
    grad_rows = extended(grad_out, (("rows", 1),), 1)
    grad_pad = jnp.pad(grad_rows, ((0, 2), (0, 0), (1, 1), (0, 0)))
    grad_mixed = jnp.zeros((frames, rows_here, width, chans), f32)
    for tap in range(27):
        shift_t, shift_i, shift_j = (tap // 9, tap // 3 % 3, tap % 3)
        piece = grad_pad[
            2 - shift_t : 2 - shift_t + frames,
            2 - shift_i : 2 - shift_i + rows_here,
            2 - shift_j : 2 - shift_j + width,
        ]
        grad_mixed = grad_mixed + jnp.einsum(
            "fhwo,io->fhwi", piece, conv_whole[:, tap, :], preferred_element_type=f32
        )
    input_rows = extended(stacked, (("rows", 1),), 1)
    input_pad = jnp.pad(input_rows, ((0, 0), (0, 0), (1, 1), (0, 0)))
    grad_b = grad_mixed.astype(bf16).reshape(frames, -1, chans)
    grad_attended = jnp.einsum(
        "fte,de->ftd", grad_b, out_weight, preferred_element_type=f32
    ).astype(bf16)
    grad_probs = jnp.einsum("fqd,fkd->fqk", grad_attended, values_all, preferred_element_type=f32)
    totals = jnp.sum(probs * grad_probs, -1, keepdims=True)
    grad_scores = probs * (grad_probs - totals)
    scaled = (grad_scores * scale).astype(bf16)
    grad_query = jnp.einsum("fqk,fkd->fqd", scaled, keys_all, preferred_element_type=f32).astype(
        bf16
    )
    key_part = jnp.einsum("fqk,fqd->fkd", scaled, query, preferred_element_type=f32)
    value_part = jnp.einsum("fqk,fqd->fkd", probs_b, grad_attended, preferred_element_type=f32)
    grad_key, grad_value = (
        lax.psum_scatter(
            key_part.astype(jnp.bfloat16), "rows", scatter_dimension=1, tiled=True
        ).astype(jnp.float32),
        lax.psum_scatter(
            value_part.astype(jnp.bfloat16), "rows", scatter_dimension=1, tiled=True
        ).astype(jnp.float32),
    )
    grad_key = grad_key.astype(bf16)
    grad_value = grad_value.astype(bf16)
    grad_normed = (
        jnp.einsum("ftd,cd->ftc", grad_query, query_weight, preferred_element_type=f32)
        + jnp.einsum("ftd,cd->ftc", grad_key, key_weight, preferred_element_type=f32)
        + jnp.einsum("ftd,cd->ftc", grad_value, value_weight, preferred_element_type=f32)
    )
    grad_normed = grad_normed.reshape(frames, rows_here, width, chans)
    inner = jnp.mean(grad_normed * xf, -1, keepdims=True)
    feature_grad = (grad_mixed + recip * grad_normed - xf * recip**3 * inner).astype(bf16)
    data_count = lax.axis_size("dp")
    row_count = lax.axis_size("rows")
    pieces = [
        jnp.einsum("ftc,ftd->cd", tokens, grad_query, preferred_element_type=f32),
        jnp.einsum("ftc,ftd->cd", tokens, grad_key, preferred_element_type=f32),
        jnp.einsum("ftc,ftd->cd", tokens, grad_value, preferred_element_type=f32),
        jnp.einsum("ftc,ftd->cd", attended, grad_b, preferred_element_type=f32),
    ]
    conv_terms = []
    for tap in range(27):
        shift_t, shift_i, shift_j = (tap // 9, tap // 3 % 3, tap % 3)
        inputs = input_pad[
            shift_t : shift_t + frames, shift_i : shift_i + rows_here, shift_j : shift_j + width
        ]
        conv_terms.append(jnp.einsum("fhwc,fhwd->cd", inputs, grad_out, preferred_element_type=f32))
    conv_block = jnp.stack(conv_terms, 1).reshape(
        chans // (data_count * row_count) * lax.axis_size(("dp", "rows")), 27 * chans
    )
    summed = lax.psum_scatter(
        jnp.concatenate(pieces + [conv_block], 1), ("dp", "rows"), scatter_dimension=0, tiled=True
    )
    return (feature_grad[None], summed[:, : 4 * chans], summed[:, 4 * chans :])


def solution(mesh):
    placed = (
        P("dp", None, "rows", None, None),
        P("dp", None, "rows", None, None),
        P("dp", None, "rows", None, None),
        P(),
        P(),
        P(),
        P(),
        P(("dp", "rows"), None, None),
    )
    return jax.shard_map(
        shards,
        mesh=mesh,
        in_specs=placed,
        out_specs=(
            P("dp", None, "rows", None, None),
            P(("dp", "rows"), None),
            P(("dp", "rows"), None),
        ),
        check_vma=False,
    )
```

profile of v0, /device:TPU:1, one launch (start us, length us, event | category | flops | bytes accessed | tf_op | source)
XLA Modules:
  0.0 866.6 jit_solution(16209071115758195999)
XLA Ops:
  9.4 1.9 convolution_convert_fusion.6
  13.9 1.3 collective-permute-start.1
  15.2 6.3 collective-permute-start
  22.6 42.3 %all-gather.8.cloned.1.call-done = bf16[2048,384]{1,0:T(8,128)(2,1)} async-done(((bf16[256,384]{1,0:T(8,128)(2,1)}), bf16[2048,384]{1,0:T(8,128)(2,1)}) %all-gather.8.cloned.1.call-update) | async-done | bytes 1572880 | tf_op jit(solution)/shard_map/all_gather | solution.py:38
  64.8 2.2 fusion.187
  67.5 49.7 %all-gather.10.cloned.1.call-done = bf16[2048,384]{1,0:T(8,128)(2,1)} async-done(((bf16[256,384]{1,0:T(8,128)(2,1)}), bf16[2048,384]{1,0:T(8,128)(2,1)}) %all-gather.10.cloned.1.call-update) | async-done | bytes 1572880 | tf_op jit(solution)/shard_map/all_gather | solution.py:39
  117.2 2.2 convolution_convert_fusion.2
  119.8 1.3 collective-permute-start.3
  121.1 5.5 collective-permute-start.2
  126.6 2.1 fusion.12
  129.4 6.1 collective-permute-done.2
  135.9 1.3 fusion.44
  138.3 1.1 fusion.42
  140.5 1.1 fusion.40
  141.6 290.7 %all-gather.6.cloned.1.call-done = bf16[384,27,384]{2,1,0:T(8,128)(2,1)} async-done(((bf16[3,27,384]{2,1,0:T(8,128)(2,1)}), bf16[384,27,384]{2,1,0:T(8,128)(2,1)}) %all-gather.6.cloned.1.call-update) | async-done | bytes 7962640 | tf_op jit(solution)/shard_map/all_gather | solution.py:25
  432.4 11.9 %fusion.184 = (bf16[384,1,384]{2,1,0:T(2,128)(2,1)}, bf16[384,1,384]{2,1,0:T(2,128)(2,1)}, bf16[384,1,384]{2,1,0:T(2,128)(2,1)}, bf16[384,1,384]{2,1,0:T(2,128)(...) fusion(bf16[384,27,384]{2,1,0:T(8,128)(2,1)} %all-gather.6.clon, ...), kind=kLoop, calls=%fused_computation.322 | loop fusion | bytes 4718592 | tf_op jit(solution)/shard_map/slice | solution.py:66
  444.3 1.2 fusion.63
  445.5 10.3 %fusion.183 = (bf16[384,1,384]{2,1,0:T(2,128)(2,1)}, bf16[384,1,384]{2,1,0:T(2,128)(2,1)}, bf16[384,1,384]{2,1,0:T(2,128)(2,1)S(1)}, bf16[384,1,384]{2,1,0:T(2,1...) fusion(bf16[384,27,384]{2,1,0:T(8,128)(2,1)S(1)} %copy-done.3), kind=kLoop, calls=%fused_computation.321 | loop fusion | bytes 11206656 | tf_op jit(solution)/shard_map/slice | solution.py:66
  462.8 1.2 fusion.69
  469.1 1.9 fusion.3
  471.1 2.2 fusion.39
  473.3 2.1 fusion.38
  477.6 1.2 fusion.35
  478.8 1.1 fusion.34
  479.9 1.1 fusion.33
  481.1 1.1 fusion.32
  482.2 1.2 fusion.31
  483.4 1.2 fusion.30
  484.5 1.2 fusion.29
  485.7 1.1 fusion.28
  486.9 2.1 fusion.4
  489.3 2.3 fusion.27
  493.8 1.1 fusion.24
  494.9 1.1 fusion.23
  496.1 1.1 fusion.22
  500.6 1.1 fusion.18
  501.7 16.4 %copy.102 = f32[384,10368]{1,0:T(8,128)} copy(f32[384,10368]{0,1:T(8,128)} %bitcast.159) | data formatting | bytes 31850496 | tf_op jit(solution)/shard_map/reshape | solution.py:116
  518.2 2.2 convolution_convert_fusion.3
  520.4 1.2 convolution_dynamic-update-slice_fusion.3
  521.5 23.7 %reduce-scatter.3.cloned.1.call-done = bf16[1,256,384]{2,1,0:T(8,128)(2,1)} async-done(((bf16[1,2048,384]{2,1,0:T(8,128)(2,1)}), bf16[1,256,384]{2,1,0:T(8,128)(2,1)}) %reduce-scatter.3.cloned.1.call-update) | async-done | bytes 196624 | tf_op jit(solution)/shard_map/reduce_scatter | solution.py:84
  545.3 2.1 convolution_dynamic-update-slice_fusion.2
  547.3 74.6 %reduce-scatter.5.cloned.1.call-done = bf16[1,256,384]{2,1,0:T(8,128)(2,1)} async-done(((bf16[1,2048,384]{2,1,0:T(8,128)(2,1)}), bf16[1,256,384]{2,1,0:T(8,128)(2,1)}) %reduce-scatter.5.cloned.1.call-update) | async-done | bytes 196624 | tf_op jit(solution)/shard_map/reduce_scatter | solution.py:87
  621.9 2.1 convolution_dynamic-update-slice_fusion.1
  624.0 1.2 convolution_dynamic-update-slice_fusion
  625.2 11.0 %constant_dynamic-update-slice_fusion = f32[384,11904]{1,0:T(8,128)} fusion(f32[384,11904]{1,0:T(8,128)} %convolution_dynamic-update-slice_fusion, f32[384,10368]{1,0:T(8,128)} %copy.102), kind=kLoop, calls=%fused_computation.289 | loop fusion | bytes 31850496 | tf_op jit(solution)/shard_map/concatenate | solution.py:120
  639.0 217.3 %all-reduce.5.cloned.1.call-done = f32[384,11904]{1,0:T(8,128)} async-done(((f32[384,11904]{1,0:T(8,128)}), f32[384,11904]{1,0:T(8,128)}) %all-reduce.5.cloned.1.call-update) | async-done | bytes 18284560
  856.3 1.5 constant_dynamic-slice_fusion
  857.8 1.9 dynamic-slice.2
  (182 shorter events, 32.2 us)
Async XLA Ops:
  7.2 4.3 copy-start
  7.2 14.3 %copy-start.7 = (bf16[1,1,2,128,384]{4,3,2,1,0:T(8,128)(2,1)S(1)}, bf16[1,1,2,128,384]{4,3,2,1,0:T(8,128)(2,1)}, u32[]{:S(2)}) copy-start(bf16[1,1,2,128,384]{4,3,2,1,0:T(8,128)(2,1)} %param.8) | copy-start | bytes 589828
  7.2 6.0 copy-start.1
  7.2 15.1 %copy-start.47 = (bf16[384,384]{1,0:T(8,128)(2,1)S(1)}, bf16[384,384]{1,0:T(8,128)(2,1)}, u32[]{:S(2)}) copy-start(bf16[384,384]{1,0:T(8,128)(2,1)} %param.11) | copy-start | bytes 884740
  7.2 57.6 %all-gather.8.cloned.1.call-start = ((), (), s32[]{:S(2)}) async-start(), calls=%async_computation.5 | async-start | bytes 1769472 | tf_op jit(solution)/shard_map/all_gather | solution.py:38
  11.4 105.8 %all-gather.10.cloned.1.call-start = ((), (), s32[]{:S(2)}) async-start(), calls=%async_computation.6 | async-start | bytes 1769472 | tf_op jit(solution)/shard_map/all_gather | solution.py:39
  12.4 420.0 %all-gather.6.cloned.1.call-start = ((), (), s32[]{:S(2)}) async-start(), calls=%async_computation.2 | async-start | bytes 9510912 | tf_op jit(solution)/shard_map/all_gather | solution.py:25
  13.1 532.1 %reduce-scatter.3.cloned.1.call-start = ((), (), s32[]{:S(2)}) async-start(), calls=%async_computation.3 | async-start | bytes 1769472 | tf_op jit(solution)/shard_map/reduce_scatter | solution.py:84
  13.9 112.7 %collective-permute-start.1 = (bf16[1,1,128,384]{3,2,1,0:T(8,128)(2,1)}, bf16[1,1,128,384]{3,2,1,0:T(8,128)(2,1)}, u32[]{:S(2)}, u32[]{:S(2)}) collective-permute-start(bf16[1,1,128,384]{3,2,1,0:T(8,128)(2,1)} %get-tuple-element.33), channel_id=1, source_target_pairs={{1,0},{2,1},{3,2},{4,3},{5,4},{6,5},{7,6},{9,8},{10,9},{11,10},{12... | collective-permute-start | bytes 294920 | tf_op jit(solution)/shard_map/ppermute | solution.py:15
  15.2 111.4 %collective-permute-start = (bf16[1,1,128,384]{3,2,1,0:T(8,128)(2,1)}, bf16[1,1,128,384]{3,2,1,0:T(8,128)(2,1)S(1)}, u32[]{:S(2)}, u32[]{:S(2)}) collective-permute-start(bf16[1,1,128,384]{3,2,1,0:T(8,128)(2,1)} %get-tuple-element.32), channel_id=1, source_target_pairs={{0,1},{1,2},{2,3},{3,4},{4,5},{5,6},{6,7},{8,9},{9,10},{10,11},{11... | collective-permute-start | bytes 294920 | tf_op jit(solution)/shard_map/ppermute | solution.py:12
  22.5 44.5 %copy-start.18 = (bf16[256,384]{1,0:T(8,128)(2,1)}, bf16[256,384]{1,0:T(8,128)(2,1)S(1)}, u32[]{:S(2)}) copy-start(bf16[256,384]{1,0:T(8,128)(2,1)S(1)} %convolution_convert_fusion.7) | copy-start | bytes 589828
  67.5 52.2 %copy-start.2 = (bf16[1,2,2,128,384]{4,3,2,1,0:T(8,128)(2,1)S(1)}, bf16[1,2,2,128,384]{4,3,2,1,0:T(8,128)(2,1)}, u32[]{:S(2)}) copy-start(bf16[1,2,2,128,384]{4,3,2,1,0:T(8,128)(2,1)} %param.9) | copy-start | bytes 1179652
  117.2 2.2 copy-start.45
  119.4 10.0 %copy-start.50 = (bf16[256,384]{1,0:T(8,128)(2,1)}, bf16[256,384]{1,0:T(8,128)(2,1)S(1)}, u32[]{:S(2)}) copy-start(bf16[256,384]{1,0:T(8,128)(2,1)S(1)} %convolution_convert_fusion.2) | copy-start | bytes 589828
  119.8 9.7 %collective-permute-start.3 = (bf16[3,1,128,384]{3,2,1,0:T(8,128)(2,1)S(1)}, bf16[3,1,128,384]{3,2,1,0:T(8,128)(2,1)S(1)}, u32[]{:S(2)}, u32[]{:S(2)}) collective-permute-start(bf16[3,1,128,384]{3,2,1,0:T(8,128)(2,1)S(1)} %get-tuple-element.31), channel_id=1, source_target_pairs={{1,0},{2,1},{3,2},{4,3},{5,4},{6,5},{7,6},{9,8},{10,9},{11,10},{12... | collective-permute-start | bytes 884744 | tf_op jit(solution)/shard_map/ppermute | solution.py:15
  121.1 14.4 %collective-permute-start.2 = (bf16[3,1,128,384]{3,2,1,0:T(8,128)(2,1)S(1)}, bf16[3,1,128,384]{3,2,1,0:T(8,128)(2,1)S(1)}, u32[]{:S(2)}, u32[]{:S(2)}) collective-permute-start(bf16[3,1,128,384]{3,2,1,0:T(8,128)(2,1)S(1)} %get-tuple-element.30), channel_id=1, source_target_pairs={{0,1},{1,2},{2,3},{3,4},{4,5},{5,6},{6,7},{8,9},{9,10},{10,11},{11... | collective-permute-start | bytes 884744 | tf_op jit(solution)/shard_map/ppermute | solution.py:12
  129.4 8.8 %copy-start.9 = (bf16[3,1,128,384]{3,2,1,0:T(8,128)(2,1)}, bf16[3,1,128,384]{3,2,1,0:T(8,128)(2,1)S(1)}, u32[]{:S(2)}) copy-start(bf16[3,1,128,384]{3,2,1,0:T(8,128)(2,1)S(1)} %collective-permute-done.3) | copy-start | bytes 884740
  135.5 2.7 copy-start.12
  135.9 4.6 copy-start.4
  432.4 13.1 %copy-start.3 = (bf16[384,27,384]{2,1,0:T(8,128)(2,1)S(1)}, bf16[384,27,384]{2,1,0:T(8,128)(2,1)}, u32[]{:S(2)}) copy-start(bf16[384,27,384]{2,1,0:T(8,128)(2,1)} %all-gather.6.cloned.1.call-done) | copy-start | bytes 23887876
  445.5 10.3 %copy-start.8 = (bf16[3,4,130,384]{3,2,1,0:T(8,128)(2,1)S(1)}, bf16[3,4,130,384]{3,2,1,0:T(8,128)(2,1)}, u32[]{:S(2)}) copy-start(bf16[3,4,130,384]{3,2,1,0:T(8,128)(2,1)} %fusion.12) | copy-start | bytes 3594244
  455.8 1.5 copy-start.43
  456.1 1.6 copy-start.42
  456.5 1.6 copy-start.41
  457.1 1.3 copy-start.39
  457.4 1.3 copy-start.37
  458.0 1.3 copy-start.40
  459.0 1.3 copy-start.34
  461.9 2.2 copy-start.25
  462.8 1.6 copy-start.24
  464.4 1.8 copy-start.46
  464.5 2.0 copy-start.56
  467.4 1.7 copy-start.19
  471.0 150.9 %reduce-scatter.5.cloned.1.call-start = ((), (), s32[]{:S(2)}) async-start(), calls=%async_computation.4 | async-start | bytes 1769472 | tf_op jit(solution)/shard_map/reduce_scatter | solution.py:87
  471.1 4.3 copy-start.10
  471.1 5.4 copy-start.5
  473.3 5.5 copy-start.13
  482.2 4.7 copy-start.55
  489.0 2.6 copy-start.6
  489.0 3.7 copy-start.14
  489.0 367.3 %all-reduce.5.cloned.1.call-start = ((), (), s32[]{:S(2)}) async-start(), calls=%async_computation.7 | async-start | bytes 36569088
  494.9 4.5 copy-start.11
  501.7 16.4 %copy-start.16 = (bf16[256,2048]{1,0:T(8,128)(2,1)S(1)}, bf16[256,2048]{1,0:T(8,128)(2,1)}, u32[]{:S(2)}) copy-start(bf16[256,2048]{1,0:T(8,128)(2,1)} %copy-done.15) | copy-start | bytes 3145732
  518.2 2.2 copy-start.17
  520.3 103.7 %copy-start.21 = (bf16[2,128,384]{2,1,0:T(8,128)(2,1)S(1)}, bf16[2,128,384]{2,1,0:T(8,128)(2,1)}, u32[]{:S(2)}) copy-start(bf16[2,128,384]{2,1,0:T(8,128)(2,1)} %copy-done.20) | copy-start | bytes 589828
  520.3 103.7 %copy-start.51 = (bf16[256,384]{1,0:T(8,128)(2,1)S(1)}, bf16[256,384]{1,0:T(8,128)(2,1)}, u32[]{:S(2)}) copy-start(bf16[256,384]{1,0:T(8,128)(2,1)} %copy-done.50) | copy-start | bytes 589828
  636.2 1.5 copy-start.53
  636.2 1.9 copy-start.22
  (19 other events, 22.9 us)
Sparse Core Ops, SparseCore 0:
  11.5 53.2 all-gather.7
  67.1 49.9 all-gather.9
  118.9 313.4 all-gather.5
  471.1 74.0 reduce-scatter.2
  548.9 73.0 reduce-scatter.4
  636.3 219.8 all-reduce.4
where the time goes:
time: 867 us
  waiting for transfers between devices  706 us (81%)
  matrix products  67.1 us (8%)
  local copies, waits for them, and re-layouts  56.2 us (6%)
  between operations  15.1 us (2%)
  starting transfers between devices  14.8 us (2%)
    all_gather x1, waiting for transfers between devices, shards(): conv_whole = lax.all_gather(conv_weight, ('dp', 'rows'), axis=0, tiled=True)  291 us
    unnamed x7, waiting for transfers between devices  218 us
    reduce_scatter x1, waiting for transfers between devices, shards(): lax.psum_scatter(value_part.astype(jnp.bfloat16), 'rows', scatter_dimensi...  74.6 us
    all_gather x1, waiting for transfers between devices, shards(): lax.all_gather(value, 'rows', axis=1, tiled=True)  49.7 us
    all_gather x1, waiting for transfers between devices, shards(): lax.all_gather(key, 'rows', axis=1, tiled=True)  42.3 us
    dot_general x27, matrix products, shards(): jnp.einsum('fhwc,fhwd->cd', inputs, grad_out, preferred_element_type=f32)  33.9 us
    reduce_scatter x1, waiting for transfers between devices, shards(): lax.psum_scatter(key_part.astype(jnp.bfloat16), 'rows', scatter_dimension...  23.7 us
    slice x2, local copies, waits for them, and re-layouts, shards(): conv_whole[:, tap, :]  22.2 us
  transfers between devices with their start and end apart: 10, of which 8 were waited for; matrix products, arithmetic and copies ran while one was open for 8% of the time, Pallas kernels for 0%

commit v1 on v0

v1 whole, which is shorter than its diff:
```python
import jax
import jax.numpy as jnp
import numpy as np
from jax import lax
from jax.experimental import pallas as pl
from jax.experimental.pallas import tpu as pltpu
from jax.sharding import PartitionSpec as P

F32 = jnp.float32
BF16 = jnp.bfloat16
VMEM_BYTES = 56 * 1024 * 1024


def nn(a, b):
    return lax.dot_general(a, b, (((1,), (0,)), ((), ())), preferred_element_type=F32)


def nt(a, b):
    return lax.dot_general(a, b, (((1,), (1,)), ((), ())), preferred_element_type=F32)


def whole(count):
    return [pl.BlockSpec(memory_space=pltpu.VMEM)] * count


def params():
    return pltpu.CompilerParams(vmem_limit_bytes=VMEM_BYTES)


def cost(macs, size):
    return pl.CostEstimate(flops=2 * macs, bytes_accessed=size, transcendentals=0)


def eye_of(n):
    rows = lax.broadcasted_iota(jnp.int32, (n, n), 0)
    cols = lax.broadcasted_iota(jnp.int32, (n, n), 1)
    return jnp.where(rows == cols, 1.0, 0.0).astype(BF16)


def pack_kernel(x_ref, u_ref, past_ref, order_ref, out_ref):
    chans, cells = x_ref.shape[1], x_ref.shape[0]
    groups = out_ref.shape[0]
    part = chans // groups
    eye = eye_of(chans)
    x_t = nt(eye, x_ref[...]).astype(BF16)
    u_t = nt(eye, u_ref[...]).astype(BF16)
    for r in range(groups):
        out_ref[r, 0:chans, :] = x_t
        out_ref[r, chans : 2 * chans, :] = u_t
    for f in range(2):
        p_t = nt(order_ref[...], past_ref[f]).astype(BF16)
        for r in range(groups):
            at = 2 * chans + f * part
            out_ref[r, at : at + part, :] = p_t[r * part : (r + 1) * part]


def conv_input_kernel(width, got_ref, w_ref, out_ref, wide_ref, w32_ref, wcat_ref):
    groups = got_ref.shape[0]
    cells = got_ref.shape[2]
    part, total = out_ref.shape
    chans = w_ref.shape[2]
    slots, padded = w_ref.shape[0], w_ref.shape[1]
    per = part // slots
    for c in range(chans // 128):
        lanes = slice(c * 128, (c + 1) * 128)
        for d in range(slots):
            w32_ref[c, d * padded : (d + 1) * padded, :] = w_ref[d, :, lanes].astype(F32)
        for tap in range(9):
            for k in range(per):
                rows = w32_ref[c, pl.ds(k * 9 + tap, slots, stride=padded), :]
                at = tap * part + k * slots
                wcat_ref[at : at + slots, lanes] = rows.astype(BF16)
    wide_ref[:, 0:width] = jnp.zeros((9 * part, width), F32)
    wide_ref[:, width + total :] = jnp.zeros((9 * part, width), F32)
    for r in range(groups):
        wide_ref[:, width + r * cells : width + (r + 1) * cells] = nn(
            wcat_ref[...], got_ref[r, chans : 2 * chans, :]
        )
    lane = lax.broadcasted_iota(jnp.int32, (part, total), 1) % width
    sums = []
    for j in range(3):
        piece = None
        for i in range(3):
            tap = 3 * i + j
            at = (2 - i) * width
            term = wide_ref[tap * part : (tap + 1) * part, at : at + total]
            piece = term if piece is None else piece + term
        sums.append(piece)
    first = jnp.where(lane == width - 1, 0.0, pltpu.roll(sums[0], total - 1, 1))
    last = jnp.where(lane == 0, 0.0, pltpu.roll(sums[2], 1, 1))
    out_ref[...] = (first + sums[1] + last).astype(BF16)


def forward_kernel(
    width,
    got_ref,
    wq_ref,
    wk_ref,
    wv_ref,
    wo_ref,
    pick_ref,
    qt_ref,
    kt_ref,
    key_ref,
    value_ref,
    att_ref,
    top_ref,
    inv_ref,
    terms_ref,
    vt_ref,
    side_ref,
    ut_ref,
    acc_ref,
):
    groups, cells = got_ref.shape[0], got_ref.shape[2]
    chans = wq_ref.shape[0]
    total = groups * cells
    part = pick_ref.shape[0]
    scale = chans ** (-0.5)
    eye = eye_of(chans)
    eye_cells = eye_of(cells)
    wq_t = nt(eye, wq_ref[...]).astype(BF16)
    wk_t = nt(eye, wk_ref[...]).astype(BF16)
    wv_t = nt(eye, wv_ref[...]).astype(BF16)
    wo_t = nt(eye, wo_ref[...]).astype(BF16)
    wo_pick = nn(pick_ref[...], wo_t).astype(BF16)

    def project(r, carry):
        x = got_ref[r, 0:chans, :].astype(F32)
        recip = lax.rsqrt(jnp.mean(x * x, 0, keepdims=True) + 1e-06)
        normed = (x * recip).astype(BF16)
        qt_ref[r] = nn(wq_t, normed).astype(BF16)
        k_t = nn(wk_t, normed).astype(BF16)
        kt_ref[r] = k_t
        v_t = nn(wv_t, normed).astype(BF16)
        vt_ref[r] = v_t
        at = pl.ds(pl.multiple_of(r * cells, cells), cells)
        key_ref[at, :] = nt(eye_cells, k_t).astype(BF16)
        value_ref[at, :] = nt(eye_cells, v_t).astype(BF16)
        return carry

    lax.fori_loop(0, groups, project, 0)
    for r in range(groups):
        ut_ref[:, r * cells : (r + 1) * cells] = got_ref[r, chans : 2 * chans, :]

    for n in range(9):
        rows = slice(n * part, (n + 1) * part)
        side_ref[rows, 0:width] = jnp.zeros((part, width), BF16)
        side_ref[rows, width + total :] = jnp.zeros((part, width), BF16)

    lane = lax.broadcasted_iota(jnp.int32, (part, cells), 1) % width

    def place(t, r, block):
        at = pl.ds(pl.multiple_of(width + r * cells, width), cells)
        block32 = block.astype(F32)
        left = jnp.where(lane == 0, 0.0, pltpu.roll(block32, 1, 1))
        right = jnp.where(lane == width - 1, 0.0, pltpu.roll(block32, cells - 1, 1))
        side_ref[(3 * t) * part : (3 * t + 1) * part, at] = left.astype(BF16)
        side_ref[(3 * t + 1) * part : (3 * t + 2) * part, at] = block
        side_ref[(3 * t + 2) * part : (3 * t + 3) * part, at] = right.astype(BF16)

    def attend(r, carry):
        scores = nn(key_ref[...], qt_ref[r]) * scale
        top = jnp.max(scores, 0, keepdims=True)
        raised = jnp.exp(scores - top)
        inv = 1.0 / jnp.sum(raised, 0, keepdims=True)
        raised_b = raised.astype(BF16)
        att = jnp.zeros((chans, cells), F32)
        for b in range(groups):
            att = att + nn(vt_ref[b], raised_b[b * cells : (b + 1) * cells])
        att = att * inv
        att_ref[r] = att
        top_ref[r] = top
        inv_ref[r] = inv
        x_pick = nn(pick_ref[...], got_ref[r, 0:chans, :])
        mixed = (x_pick + nn(wo_pick, att.astype(BF16))).astype(BF16)
        place(2, r, mixed)
        for f in range(2):
            place(f, r, got_ref[r, 2 * chans + f * part : 2 * chans + (f + 1) * part, :])
        return carry

    lax.fori_loop(0, groups, attend, 0)

    lane_tiles = chans // 128
    acc_ref[:, 27 * part :, :] = jnp.zeros((lane_tiles, 5 * part, 128), F32)
    for i in range(3):
        block = nt(side_ref[:, i * width : i * width + total], ut_ref[...])
        for t in range(3):
            for j in range(3):
                tap, at = 9 * t + 3 * i + j, (3 * t + j) * part
                for c in range(lane_tiles):
                    acc_ref[c, tap * part : (tap + 1) * part, :] = block[
                        at : at + part, c * 128 : (c + 1) * 128
                    ]
    slots = terms_ref.shape[0]
    for d in range(slots):
        for k in range(part // slots):
            for c in range(lane_tiles):
                rows = acc_ref[c, pl.ds(k * slots + d, 32, stride=part), :]
                terms_ref[d, k * 32 : (k + 1) * 32, c * 128 : (c + 1) * 128] = rows.astype(BF16)


def backward_kernel(
    me_ref,
    got_ref,
    grad_ref,
    qt_ref,
    kt_ref,
    key_ref,
    value_ref,
    att_ref,
    top_ref,
    inv_ref,
    wq_ref,
    wk_ref,
    wv_ref,
    wo_ref,
    order_ref,
    back_ref,
    out_ref,
    terms_ref,
    ga_ref,
    tot_ref,
    gq_ref,
    gk_ref,
    gv_ref,
):
    groups, cells = got_ref.shape[0], got_ref.shape[2]
    chans = wq_ref.shape[0]
    scale = chans ** (-0.5)
    me = me_ref[0]
    wo_order = nt(wo_ref[...], order_ref[...]).astype(BF16)

    def spread(r, carry):
        at = pl.ds(pl.multiple_of(r * cells, cells), cells)
        ga = nn(wo_order, grad_ref[:, at]).astype(BF16)
        ga_ref[r] = ga
        tot_ref[r] = jnp.sum(att_ref[r] * ga.astype(F32), 0, keepdims=True)
        return carry

    lax.fori_loop(0, groups, spread, 0)

    mine = pl.ds(pl.multiple_of(me * cells, cells), cells)
    key_mine = key_ref[mine, :]
    value_mine = value_ref[mine, :]
    q_mine = qt_ref[me]
    ga_mine = ga_ref[me]
    top_mine = top_ref[me]
    inv_mine = inv_ref[me]
    tot_mine = tot_ref[me]
    gq_ref[...] = jnp.zeros((chans, cells), F32)
    gk_ref[...] = jnp.zeros((chans, cells), F32)
    gv_ref[...] = jnp.zeros((chans, cells), F32)

    def step(r, carry):
        at = pl.ds(pl.multiple_of(r * cells, cells), cells)
        probs = jnp.exp(nn(key_ref[at, :], q_mine) * scale - top_mine) * inv_mine
        grad_probs = nn(value_ref[at, :], ga_mine)
        scaled = (probs * (grad_probs - tot_mine) * scale).astype(BF16)
        gq_ref[...] += nn(kt_ref[r], scaled)
        probs = jnp.exp(nn(key_mine, qt_ref[r]) * scale - top_ref[r]) * inv_ref[r]
        grad_probs = nn(value_mine, ga_ref[r])
        scaled = (probs * (grad_probs - tot_ref[r]) * scale).astype(BF16)
        gk_ref[...] += nt(qt_ref[r], scaled)
        gv_ref[...] += nt(ga_ref[r], probs.astype(BF16))
        return carry

    lax.fori_loop(0, groups, step, 0)

    gq = gq_ref[...].astype(BF16)
    gk = gk_ref[...].astype(BF16)
    gv = gv_ref[...].astype(BF16)
    x = got_ref[me, 0:chans, :].astype(F32)
    recip = lax.rsqrt(jnp.mean(x * x, 0, keepdims=True) + 1e-06)
    normed = (x * recip).astype(BF16)
    grad_b = nn(back_ref[...], grad_ref[:, mine])
    grad_normed = nn(wq_ref[...], gq) + nn(wk_ref[...], gk) + nn(wv_ref[...], gv)
    inner = jnp.mean(grad_normed * x, 0, keepdims=True)
    out = grad_b + recip * grad_normed - x * (recip * recip * recip) * inner
    out_ref[...] = nt(eye_of(cells), out.astype(BF16)).astype(BF16)
    slots = terms_ref.shape[0]
    each = chans // slots
    pairs = [(normed, gq), (normed, gk), (normed, gv), (att_ref[me].astype(BF16), grad_b.astype(BF16))]
    for n, (left, right) in enumerate(pairs):
        term = nt(left, right).astype(BF16)
        for d in range(slots):
            terms_ref[d, n * each : (n + 1) * each, :] = term[d * each : (d + 1) * each]


def spread_over(block, axis):
    count = lax.axis_size(axis)
    return lax.all_to_all(jnp.broadcast_to(block[None], (count, *block.shape)), axis, 0, 0)


def shards(
    features, past_frames, upstream, query_weight, key_weight, value_weight, out_weight, conv_weight
):
    slots, groups = lax.axis_size("dp"), lax.axis_size("rows")
    _, _, rows_here, width, chans = features.shape
    cells = rows_here * width
    total = cells * groups
    part = chans // groups
    per = part // slots
    me = lax.axis_index("rows")

    order = np.zeros((chans, chans), np.float32)
    for r in range(groups):
        for k in range(per):
            for d in range(slots):
                order[r * part + k * slots + d, d * per * groups + per * r + k] = 1.0
    order_b = jnp.asarray(order, BF16)
    back_b = jnp.asarray(order.T, BF16)
    pick = lax.dynamic_slice_in_dim(order_b, me * part, part, axis=0)

    x = features.reshape(cells, chans)
    u = upstream.reshape(cells, chans)
    past = past_frames.reshape(2, cells, chans)
    depth = 2 * chans + 2 * part
    packed = pl.pallas_call(
        pack_kernel,
        out_shape=jax.ShapeDtypeStruct((groups, depth, cells), BF16),
        in_specs=whole(4),
        out_specs=pl.BlockSpec(memory_space=pltpu.VMEM),
        compiler_params=params(),
        name="pack",
    )(x, u, past, order_b)
    got = lax.all_to_all(packed, "rows", 0, 0)

    w_local = conv_weight[:, 18:27, :].reshape(per * 9, chans)
    w_local = jnp.pad(w_local, ((0, 32 - per * 9), (0, 0)))
    w_all = spread_over(w_local, "dp")

    grad_part = pl.pallas_call(
        lambda *refs: conv_input_kernel(width, *refs),
        out_shape=jax.ShapeDtypeStruct((part, total), BF16),
        in_specs=whole(2),
        out_specs=pl.BlockSpec(memory_space=pltpu.VMEM),
        scratch_shapes=[
            pltpu.VMEM((9 * part, total + 2 * width), F32),
            pltpu.VMEM((chans // 128, slots * 32, 128), F32),
            pltpu.VMEM((9 * part, chans), BF16),
        ],
        compiler_params=params(),
        name="conv_input",
    )(got, w_all)
    grad_all = spread_over(grad_part, "rows").reshape(chans, total)

    qt, kt, key, value, att, top, inv, conv_terms = pl.pallas_call(
        lambda *refs: forward_kernel(width, *refs),
        out_shape=(
            jax.ShapeDtypeStruct((groups, chans, cells), BF16),
            jax.ShapeDtypeStruct((groups, chans, cells), BF16),
            jax.ShapeDtypeStruct((total, chans), BF16),
            jax.ShapeDtypeStruct((total, chans), BF16),
            jax.ShapeDtypeStruct((groups, chans, cells), F32),
            jax.ShapeDtypeStruct((groups, 1, cells), F32),
            jax.ShapeDtypeStruct((groups, 1, cells), F32),
            jax.ShapeDtypeStruct((slots, per * 32, chans), BF16),
        ),
        in_specs=whole(6),
        out_specs=tuple(whole(8)),
        scratch_shapes=[
            pltpu.VMEM((groups, chans, cells), BF16),
            pltpu.VMEM((9 * part, total + 2 * width), BF16),
            pltpu.VMEM((chans, total), BF16),
            pltpu.VMEM((chans // 128, 32 * part, 128), F32),
        ],
        compiler_params=params(),
        name="forward",
    )(got, query_weight, key_weight, value_weight, out_weight, pick)

    feature_grad, proj_terms = pl.pallas_call(
        backward_kernel,
        out_shape=(
            jax.ShapeDtypeStruct((cells, chans), BF16),
            jax.ShapeDtypeStruct((slots, 4 * chans // slots, chans), BF16),
        ),
        in_specs=[pl.BlockSpec(memory_space=pltpu.SMEM)] + whole(15),
        out_specs=tuple(whole(2)),
        scratch_shapes=[
            pltpu.VMEM((groups, chans, cells), BF16),
            pltpu.VMEM((groups, 1, cells), F32),
            pltpu.VMEM((chans, cells), F32),
            pltpu.VMEM((chans, cells), F32),
            pltpu.VMEM((chans, cells), F32),
        ],
        compiler_params=params(),
        name="backward",
    )(
        me.reshape(1),
        got,
        grad_all,
        qt,
        kt,
        key,
        value,
        att,
        top,
        inv,
        query_weight,
        key_weight,
        value_weight,
        out_weight,
        order_b,
        back_b,
    )

    conv_sum = jnp.sum(lax.all_to_all(conv_terms, "dp", 0, 0).astype(F32), 0)
    conv_grad = conv_sum.reshape(per, 32, chans)[:, :27].reshape(per, 27 * chans)
    proj_sum = jnp.sum(lax.all_to_all(proj_terms, "dp", 0, 0).astype(F32), 0)
    proj_sum = proj_sum.reshape(4, groups, per, chans).transpose(1, 2, 0, 3)
    proj_sum = proj_sum.reshape(groups, per, 4 * chans)
    proj_grads = jnp.sum(lax.all_to_all(proj_sum, "rows", 0, 0), 0)
    return feature_grad.reshape(features.shape), proj_grads, conv_grad


def solution(mesh):
    placed = (
        P("dp", None, "rows", None, None),
        P("dp", None, "rows", None, None),
        P("dp", None, "rows", None, None),
        P(),
        P(),
        P(),
        P(),
        P(("dp", "rows"), None, None),
    )
    return jax.shard_map(
        shards,
        mesh=mesh,
        in_specs=placed,
        out_specs=(
            P("dp", None, "rows", None, None),
            P(("dp", "rows"), None),
            P(("dp", "rows"), None),
        ),
        check_vma=False,
    )
```

time: 867 us -> 179 us (0.21)
  waiting for transfers between devices: 706 us -> 27.9 us
  matrix products: 67.1 us -> 0 us
  Pallas kernels: 0 us -> 62.2 us
  local copies, waits for them, and re-layouts: 56.2 us -> 6.94 us
  blocking collectives: 0 us -> 48.2 us
  starting transfers between devices: 14.8 us -> 30.5 us
  between operations: 15.1 us -> 0.7 us
    all_gather x3 -> x0, waiting for transfers between devices: 383 us -> none  [the longest x1 291 us: shards(): conv_whole = lax.all_gather(conv_weight, ('dp', 'rows'), axis=0, tiled=True)]
    unnamed x7 -> x0, waiting for transfers between devices: 218 us -> none
    reduce_scatter x2 -> x0, waiting for transfers between devices: 98.4 us -> none  [the longest x1 74.6 us: shards(): lax.psum_scatter(value_part.astype(jnp.bfloat16), 'rows', scatter_dimensi...]
    dot_general x72 -> x0, matrix products: 67.1 us -> none  [the longest x27 33.9 us: shards(): jnp.einsum('fhwc,fhwd->cd', inputs, grad_out, preferred_element_type=f32)]
    pallas_call x0 -> x4, Pallas kernels: none -> 62.2 us  [the longest x1 35.5 us: shards(): pl.pallas_call(lambda *refs: forward_kernel(width, *refs), out_shape=(jax...]
    all_to_all x0 -> x1, blocking collectives: none -> 48.2 us  [shards(): got = lax.all_to_all(packed, 'rows', 0, 0)]
    all_to_all x0 -> x5, starting transfers between devices: none -> 30.5 us  [the longest x2 11.4 us: spread_over(): lax.all_to_all(jnp.broadcast_to(block[None], (count, *block.shape)), axis...]
    all_to_all x0 -> x5, waiting for transfers between devices: none -> 27.9 us  [the longest x1 17.1 us: shards(): proj_sum = jnp.sum(lax.all_to_all(proj_terms, 'dp', 0, 0).astype(F32), 0)]
  transfers between devices with their start and end apart: 10 -> 5, of which waited for: 8 -> 3; matrix products, arithmetic and copies ran while one was open for 8% -> 1% of each run, Pallas kernels for 0% -> 33%
where the time goes in v1:
time: 179 us; the launch traced here: 177 us
  Pallas kernels  62.2 us (35%)
  blocking collectives  48.2 us (27%)
  starting transfers between devices  30.5 us (17%)
  waiting for transfers between devices  27.9 us (16%)
  local copies, waits for them, and re-layouts  6.94 us (4%)
    all_to_all x1, blocking collectives, shards(): got = lax.all_to_all(packed, 'rows', 0, 0)  48.2 us
    pallas_call x1, Pallas kernels, shards(): pl.pallas_call(lambda *refs: forward_kernel(width, *refs), out_shape=(jax...  35.5 us
    pallas_call x1, Pallas kernels, shards(): pl.pallas_call(backward_kernel, out_shape=(jax.ShapeDtypeStruct((cells, c...  18.7 us
    all_to_all x1, waiting for transfers between devices, shards(): proj_sum = jnp.sum(lax.all_to_all(proj_terms, 'dp', 0, 0).astype(F32), 0)  17.1 us
    all_to_all x2, starting transfers between devices, spread_over(): lax.all_to_all(jnp.broadcast_to(block[None], (count, *block.shape)), axis...  11.4 us
    all_to_all x1, starting transfers between devices, shards(): proj_grads = jnp.sum(lax.all_to_all(proj_sum, 'rows', 0, 0), 0)  6.85 us
    all_to_all x1, starting transfers between devices, shards(): conv_sum = jnp.sum(lax.all_to_all(conv_terms, 'dp', 0, 0).astype(F32), 0)  6.41 us
    all_to_all x1, waiting for transfers between devices, shards(): proj_grads = jnp.sum(lax.all_to_all(proj_sum, 'rows', 0, 0), 0)  6.26 us
  transfers between devices with their start and end apart: 5, of which 3 were waited for; matrix products, arithmetic and copies ran while one was open for 1% of the time, Pallas kernels for 33%

profile of v1, /device:TPU:1, one launch (start us, length us, event | category | flops | bytes accessed | tf_op | source)
XLA Modules:
  0.0 177.4 jit_solution(9520939382265700779)
XLA Ops:
  0.6 0.8 slice.6
  1.5 0.8 broadcast_in_dim.4
  2.2 7.8 %all-to-all-start.1 = ((bf16[16,32,384]{2,1,0:T(8,128)(2,1)}), bf16[16,32,384]{2,1,0:T(8,128)(2,1)S(1)}, u32[]{:S(2)}, u32[]{:S(2)}) async-start(bf16[16,32,384]{2,1,0:T(8,128)(2,1)} %broadcast_in_dim.4), calls=%async_computation.1 | async-start | bytes 786432 | tf_op jit(solution)/shard_map/all_to_all | solution.py:292
  10.1 3.9 %pack.1 = bf16[8,864,256]{2,1,0:T(8,128)(2,1)} custom-call(bf16[256,384]{1,0:T(8,128)(2,1)} %bitcast.15, bf16[256,384]{1,0:T(8,128)(2,1)} %bitcast.16, bf16[2,256,384]{2,1,0:T(8,128)(2,1)} %bitcast.14, bf16[384,384]{1,0:T(8,128)(2,1)} %constant.18.clone.order_ref), custom_call_target="tpu_custom_call" | custom-call | tf_op jit(solution)/shard_map/pack/pallas_call | solution.py:319
  13.9 4.5 %all-to-all-done.1.refs_1_ = bf16[16,32,384]{2,1,0:T(8,128)(2,1)S(1)} async-done(((bf16[16,32,384]{2,1,0:T(8,128)(2,1)}), bf16[16,32,384]{2,1,0:T(8,128)(2,1)S(1)}, u32[]{:S(2)}, u32[]{:S(2)}) %all-to-all-start.1) | async-done | bytes 393248 | tf_op jit(solution)/shard_map/all_to_all | solution.py:292
  18.5 0.0 copy-start.1
  18.5 48.2 %all_to_all.30.refs_0_.got_ref = bf16[8,864,256]{2,1,0:T(8,128)(2,1)} all-to-all(bf16[8,864,256]{2,1,0:T(8,128)(2,1)} %pack.1), channel_id=1, replica_groups=mesh['dp'=16,'rows'=8] {'rows'}, dimensions={0} | all-to-all | bytes 7077888 | tf_op jit(solution)/shard_map/all_to_all | solution.py:327
  66.7 0.0 copy-done.1
  66.7 4.2 %conv_input.1 = bf16[48,2048]{1,0:T(8,128)(2,1)} custom-call(bf16[8,864,256]{2,1,0:T(8,128)(2,1)} %all_to_all.30.refs_0_.got_ref, bf16[16,32,384]{2,1,0:T(8,128)(2,1)} %copy-done.1), custom_call_target="tpu_custom_call" | custom-call | tf_op jit(solution)/shard_map/conv_input/pallas_call | solution.py:333
  70.9 2.3 %broadcast_in_dim.5 = bf16[8,48,2048]{2,1,0:T(8,128)(2,1)} broadcast(bf16[48,2048]{1,0:T(8,128)(2,1)} %conv_input.1), dimensions={1,2} | broadcast | bytes 1769472 | tf_op jit(solution)/shard_map/broadcast_in_dim | solution.py:292
  73.2 3.6 %all-to-all-start.2 = ((bf16[8,48,2048]{2,1,0:T(8,128)(2,1)}), bf16[8,48,2048]{2,1,0:T(8,128)(2,1)S(1)}, u32[]{:S(2)}, u32[]{:S(2)}) async-start(bf16[8,48,2048]{2,1,0:T(8,128)(2,1)} %broadcast_in_dim.5), calls=%async_computation.2 | async-start | bytes 3145728 | tf_op jit(solution)/shard_map/all_to_all | solution.py:292
  76.8 1.4 constant_dynamic-slice_fusion.refs_5_
  78.1 35.5 %forward.1 = (bf16[8,384,256]{2,1,0:T(8,128)(2,1)}, bf16[8,384,256]{2,1,0:T(8,128)(2,1)}, bf16[2048,384]{1,0:T(8,128)(2,1)}, bf16[2048,384]{1,0:T(8,128)(2,1)}, ...) custom-call(bf16[8,864,256]{2,1,0:T(8,128)(2,1)} %all_to_all.30.refs_0_.got_, ...), custom_call_target="tpu_custom_call" | custom-call | tf_op jit(solution)/shard_map/forward/pallas_call | solution.py:348
  113.6 0.0 all-to-all-done.2
  113.6 0.0 copy-start
  113.6 6.4 %all-to-all-start.5 = ((bf16[16,96,384]{2,1,0:T(8,128)(2,1)}), bf16[16,96,384]{2,1,0:T(8,128)(2,1)S(1)}, u32[]{:S(2)}, u32[]{:S(2)}) async-start(bf16[16,96,384]{2,1,0:T(8,128)(2,1)} %get-tuple-element.22), calls=%async_computation.5 | async-start | bytes 2359296 | tf_op jit(solution)/shard_map/all_to_all | solution.py:408
  120.0 0.0 copy-done
  120.0 18.7 %backward.1 = (bf16[256,384]{1,0:T(8,128)(2,1)}, bf16[16,96,384]{2,1,0:T(8,128)(2,1)}) custom-call(s32[1]{0:T(128)} %bitcast.me_ref, bf16[8,864,256]{2,1,0:T(8,128)(2,1)} %all_to_all.30.refs_0_.got_ref, bf16[384,2048]{1,0:T(8,128)(2,1)} %bitcast.11, bf16[8,384,256]{2,1,0:T(8,128)(2,1)} %get-tuple-element.13.qt_ref, ...), custom_call_target="tpu_custom_call" | custom-call | tf_op jit(solution)/shard_map/backward/pallas_call | solution.py:372
  138.7 0.0 all-to-all-done.5
  138.7 5.8 %all-to-all-start.3 = ((bf16[16,96,384]{2,1,0:T(8,128)(2,1)}), bf16[16,96,384]{2,1,0:T(8,128)(2,1)S(1)}, u32[]{:S(2)}, u32[]{:S(2)}) async-start(bf16[16,96,384]{2,1,0:T(8,128)(2,1)} %get-tuple-element.21), calls=%async_computation.3 | async-start | bytes 2359296 | tf_op jit(solution)/shard_map/all_to_all | solution.py:410
  144.5 0.2 convert_reduce_fusion
  144.7 17.1 %all-to-all-done.3 = bf16[16,96,384]{2,1,0:T(8,128)(2,1)S(1)} async-done(((bf16[16,96,384]{2,1,0:T(8,128)(2,1)}), bf16[16,96,384]{2,1,0:T(8,128)(2,1)S(1)}, u32[]{:S(2)}, u32[]{:S(2)}) %all-to-all-start.3) | async-done | bytes 1179680 | tf_op jit(solution)/shard_map/all_to_all | solution.py:410
  161.8 0.2 convert_reduce_fusion.1
  162.0 0.1 reshape.48
  162.0 0.1 copy.16
  162.1 0.8 reshape.52
  162.9 6.8 %all-to-all-start.4 = ((f32[8,3,1536]{2,1,0:T(4,128)}), f32[8,3,1536]{2,1,0:T(4,128)S(1)}, u32[]{:S(2)}, u32[]{:S(2)}) async-start(f32[8,3,1536]{2,1,0:T(4,128)} %reshape.52), calls=%async_computation.4 | async-start | bytes 393216 | tf_op jit(solution)/shard_map/all_to_all | solution.py:413
  169.8 0.8 copy.18
  170.5 6.3 %all-to-all-done.4 = f32[8,3,1536]{2,1,0:T(4,128)S(1)} async-done(((f32[8,3,1536]{2,1,0:T(4,128)}), f32[8,3,1536]{2,1,0:T(4,128)S(1)}, u32[]{:S(2)}, u32[]{:S(2)}) %all-to-all-start.4) | async-done | bytes 147488 | tf_op jit(solution)/shard_map/all_to_all | solution.py:413
  176.8 0.6 reduce_sum.28
  (3 shorter events, 0.0 us)
Async XLA Ops:
  2.2 16.2 %all-to-all-start.1 = ((bf16[16,32,384]{2,1,0:T(8,128)(2,1)}), bf16[16,32,384]{2,1,0:T(8,128)(2,1)S(1)}, u32[]{:S(2)}, u32[]{:S(2)}) async-start(bf16[16,32,384]{2,1,0:T(8,128)(2,1)} %broadcast_in_dim.4), calls=%async_computation.1 | async-start | bytes 786432 | tf_op jit(solution)/shard_map/all_to_all | solution.py:292
  18.5 48.2 %copy-start.1 = (bf16[16,32,384]{2,1,0:T(8,128)(2,1)}, bf16[16,32,384]{2,1,0:T(8,128)(2,1)S(1)}, u32[]{:S(2)}) copy-start(bf16[16,32,384]{2,1,0:T(8,128)(2,1)S(1)} %all-to-all-done.1.refs_1_) | copy-start | bytes 1179652
  73.2 40.5 %all-to-all-start.2 = ((bf16[8,48,2048]{2,1,0:T(8,128)(2,1)}), bf16[8,48,2048]{2,1,0:T(8,128)(2,1)S(1)}, u32[]{:S(2)}, u32[]{:S(2)}) async-start(bf16[8,48,2048]{2,1,0:T(8,128)(2,1)} %broadcast_in_dim.5), calls=%async_computation.2 | async-start | bytes 3145728 | tf_op jit(solution)/shard_map/all_to_all | solution.py:292
  113.6 6.4 %copy-start = (bf16[8,48,2048]{2,1,0:T(8,128)(2,1)}, bf16[8,48,2048]{2,1,0:T(8,128)(2,1)S(1)}, u32[]{:S(2)}) copy-start(bf16[8,48,2048]{2,1,0:T(8,128)(2,1)S(1)} %all-to-all-done.2) | copy-start | bytes 4718596
  113.6 25.1 %all-to-all-start.5 = ((bf16[16,96,384]{2,1,0:T(8,128)(2,1)}), bf16[16,96,384]{2,1,0:T(8,128)(2,1)S(1)}, u32[]{:S(2)}, u32[]{:S(2)}) async-start(bf16[16,96,384]{2,1,0:T(8,128)(2,1)} %get-tuple-element.22), calls=%async_computation.5 | async-start | bytes 2359296 | tf_op jit(solution)/shard_map/all_to_all | solution.py:408
  138.7 23.1 %all-to-all-start.3 = ((bf16[16,96,384]{2,1,0:T(8,128)(2,1)}), bf16[16,96,384]{2,1,0:T(8,128)(2,1)S(1)}, u32[]{:S(2)}, u32[]{:S(2)}) async-start(bf16[16,96,384]{2,1,0:T(8,128)(2,1)} %get-tuple-element.21), calls=%async_computation.3 | async-start | bytes 2359296 | tf_op jit(solution)/shard_map/all_to_all | solution.py:410
  162.9 13.9 %all-to-all-start.4 = ((f32[8,3,1536]{2,1,0:T(4,128)}), f32[8,3,1536]{2,1,0:T(4,128)S(1)}, u32[]{:S(2)}, u32[]{:S(2)}) async-start(f32[8,3,1536]{2,1,0:T(4,128)} %reshape.52), calls=%async_computation.4 | async-start | bytes 393216 | tf_op jit(solution)/shard_map/all_to_all | solution.py:413

commit v2 on v1

v2 whole, which is shorter than its diff:
```python
import jax
import jax.numpy as jnp
import numpy as np
from jax import lax
from jax.experimental import pallas as pl
from jax.experimental.pallas import tpu as pltpu
from jax.sharding import PartitionSpec as P

F32 = jnp.float32
BF16 = jnp.bfloat16
LOG2E = 1.4426950408889634
VMEM_BYTES = 56 * 1024 * 1024


def nn(a, b):
    return lax.dot_general(a, b, (((1,), (0,)), ((), ())), preferred_element_type=F32)


def nt(a, b):
    return lax.dot_general(a, b, (((1,), (1,)), ((), ())), preferred_element_type=F32)


def whole(count):
    return [pl.BlockSpec(memory_space=pltpu.VMEM)] * count


def params():
    return pltpu.CompilerParams(vmem_limit_bytes=VMEM_BYTES)


def cost(macs, size):
    return pl.CostEstimate(flops=2 * macs, bytes_accessed=size, transcendentals=0)


def eye_of(n):
    rows = lax.broadcasted_iota(jnp.int32, (n, n), 0)
    cols = lax.broadcasted_iota(jnp.int32, (n, n), 1)
    return jnp.where(rows == cols, 1.0, 0.0).astype(BF16)


def pack_kernel(x_ref, u_ref, past_ref, order_ref, out_ref):
    chans = x_ref.shape[1]
    groups = out_ref.shape[0]
    part = chans // groups
    eye = eye_of(chans)
    x_t = nt(eye, x_ref[...]).astype(BF16)
    u_t = nt(eye, u_ref[...]).astype(BF16)
    for r in range(groups):
        out_ref[r, 0:chans, :] = x_t
        out_ref[r, chans : 2 * chans, :] = u_t
    for f in range(2):
        p_t = nt(order_ref[...], past_ref[f]).astype(BF16)
        for r in range(groups):
            at = 2 * chans + f * part
            out_ref[r, at : at + part, :] = p_t[r * part : (r + 1) * part]


def conv_input_kernel(width, me_ref, got_ref, w0_ref, w1_ref, w2_ref, w3_ref, out_ref, wide_ref, w32_ref, wcat_ref):
    groups = got_ref.shape[0]
    cells = got_ref.shape[2]
    part, total = out_ref.shape[1:]
    w_refs = (w0_ref, w1_ref, w2_ref, w3_ref)
    near, padded, chans = w0_ref.shape
    slots = 4 * near
    per = part // slots
    me = me_ref[0]
    for back in range(4):
        for n in range(near):
            plane = lax.rem(lax.div(me, near) + 4 - back, 4)
            inner = lax.rem(me, near)
            apart = [(inner // 2 + n // 2) % 2, (inner + n) % 2]
            at = (plane * near + apart[0] * 2 + apart[1]) * padded
            at = pl.ds(pl.multiple_of(at, padded), padded)
            for c in range(chans // 128):
                w32_ref[c, at, :] = w_refs[back][n, :, c * 128 : (c + 1) * 128].astype(F32)
    for c in range(chans // 128):
        lanes = slice(c * 128, (c + 1) * 128)
        for tap in range(9):
            for k in range(per):
                rows = w32_ref[c, pl.ds(k * 9 + tap, slots, stride=padded), :]
                at = tap * part + k * slots
                wcat_ref[at : at + slots, lanes] = rows.astype(BF16)
    wide_ref[:, 0:width] = jnp.zeros((9 * part, width), F32)
    wide_ref[:, width + total :] = jnp.zeros((9 * part, width), F32)
    for r in range(groups):
        wide_ref[:, width + r * cells : width + (r + 1) * cells] = nn(
            wcat_ref[...], got_ref[r, chans : 2 * chans, :]
        )
    lane = lax.broadcasted_iota(jnp.int32, (part, total), 1) % width
    sums = []
    for j in range(3):
        piece = None
        for i in range(3):
            tap = 3 * i + j
            at = (2 - i) * width
            term = wide_ref[tap * part : (tap + 1) * part, at : at + total]
            piece = term if piece is None else piece + term
        sums.append(piece)
    first = jnp.where(lane == width - 1, 0.0, pltpu.roll(sums[0], total - 1, 1))
    last = jnp.where(lane == 0, 0.0, pltpu.roll(sums[2], 1, 1))
    grad = (first + sums[1] + last).astype(BF16)
    for r in range(groups):
        out_ref[r] = grad


def forward_kernel(
    width,
    me_ref,
    got_ref,
    wq_ref,
    wk_ref,
    wv_ref,
    wo_ref,
    order_ref,
    qt_ref,
    kt_ref,
    key_ref,
    value_ref,
    att_ref,
    top_ref,
    inv_ref,
    terms_ref,
    vt_ref,
    side_ref,
    ut_ref,
    acc_ref,
    even_ref,
    odd_ref,
    raised_ref,
):
    groups, cells = got_ref.shape[0], got_ref.shape[2]
    chans = wq_ref.shape[0]
    total = groups * cells
    part = chans // groups
    pick = order_ref[pl.ds(pl.multiple_of(me_ref[0] * part, part), part), :]
    scale = chans ** (-0.5)
    eye = eye_of(chans)
    eye_cells = eye_of(cells)
    wqkv_t = jnp.concatenate(
        [nt(eye, ref[...]).astype(BF16) for ref in (wq_ref, wk_ref, wv_ref)], 0
    )
    wkv = jnp.concatenate([wk_ref[...], wv_ref[...]], 1)
    wo_t = nt(eye, wo_ref[...]).astype(BF16)
    wo_pick = nn(pick, wo_t).astype(BF16)

    def project(r, carry):
        x = got_ref[r, 0:chans, :].astype(F32)
        recip = lax.rsqrt(jnp.mean(x * x, 0, keepdims=True) + 1e-06)
        normed = (x * recip).astype(BF16)
        at = pl.ds(pl.multiple_of(r * cells, cells), cells)
        qkv_t = nn(wqkv_t, normed).astype(BF16)
        qt_ref[:, at] = qkv_t[0:chans]
        kt_ref[:, at] = qkv_t[chans : 2 * chans]
        vt_ref[:, at] = qkv_t[2 * chans :]
        kv = nn(nt(eye_cells, normed).astype(BF16), wkv).astype(BF16)
        key_ref[at, :] = kv[:, 0:chans]
        value_ref[at, :] = kv[:, chans:]
        return carry

    lax.fori_loop(0, groups, project, 0, unroll=2)
    for r in range(groups):
        ut_ref[:, r * cells : (r + 1) * cells] = got_ref[r, chans : 2 * chans, :]

    for n in range(9):
        rows = slice(n * part, (n + 1) * part)
        side_ref[rows, 0:width] = jnp.zeros((part, width), BF16)
        side_ref[rows, width + total :] = jnp.zeros((part, width), BF16)

    lane = lax.broadcasted_iota(jnp.int32, (part, cells), 1) % width

    def place(t, r, block):
        at = pl.ds(pl.multiple_of(width + r * cells, width), cells)
        block32 = block.astype(F32)
        left = jnp.where(lane == 0, 0.0, pltpu.roll(block32, 1, 1))
        right = jnp.where(lane == width - 1, 0.0, pltpu.roll(block32, cells - 1, 1))
        side_ref[(3 * t) * part : (3 * t + 1) * part, at] = left.astype(BF16)
        side_ref[(3 * t + 1) * part : (3 * t + 2) * part, at] = block
        side_ref[(3 * t + 2) * part : (3 * t + 3) * part, at] = right.astype(BF16)

    even_ref[...] = nn(key_ref[...], qt_ref[:, 0:cells])
    chunk = total // 4

    def attend(r, now_ref, later_ref):
        later = jnp.minimum(r + 1, groups - 1)
        at = pl.ds(pl.multiple_of(r * cells, cells), cells)
        later = pl.ds(pl.multiple_of(later * cells, cells), cells)
        top = jnp.max(now_ref[...], 0, keepdims=True)
        count = jnp.zeros((1, cells), F32)
        for b in range(4):
            rows = slice(b * chunk, (b + 1) * chunk)
            later_ref[rows] = nn(key_ref[rows], qt_ref[:, later])
            raised = jnp.exp2((now_ref[rows] - top) * (scale * LOG2E))
            count = count + jnp.sum(raised, 0, keepdims=True)
            raised_ref[rows] = raised.astype(BF16)
        inv = 1.0 / count
        att = nn(vt_ref[...], raised_ref[...]) * inv
        att_ref[:, at] = att
        top_ref[:, at] = top
        inv_ref[:, at] = inv
        x_pick = nn(pick, got_ref[r, 0:chans, :])
        mixed = (x_pick + nn(wo_pick, att.astype(BF16))).astype(BF16)
        place(2, r, mixed)
        for f in range(2):
            place(f, r, got_ref[r, 2 * chans + f * part : 2 * chans + (f + 1) * part, :])

    def attend_two(n, carry):
        attend(2 * n, even_ref, odd_ref)
        attend(2 * n + 1, odd_ref, even_ref)
        return carry

    lax.fori_loop(0, groups // 2, attend_two, 0)

    lane_tiles = chans // 128
    acc_ref[:, 27 * part :, :] = jnp.zeros((lane_tiles, 5 * part, 128), F32)
    for i in range(3):
        block = nt(side_ref[:, i * width : i * width + total], ut_ref[...])
        for t in range(3):
            for j in range(3):
                tap, at = 9 * t + 3 * i + j, (3 * t + j) * part
                for c in range(lane_tiles):
                    acc_ref[c, tap * part : (tap + 1) * part, :] = block[
                        at : at + part, c * 128 : (c + 1) * 128
                    ]
    slots = terms_ref.shape[0]
    for d in range(slots):
        for k in range(part // slots):
            for c in range(lane_tiles):
                rows = acc_ref[c, pl.ds(k * slots + d, 32, stride=part), :]
                terms_ref[d, k * 32 : (k + 1) * 32, c * 128 : (c + 1) * 128] = rows.astype(BF16)


def backward_kernel(
    place_ref,
    x_ref,
    grad_ref,
    qt_ref,
    kt_ref,
    key_ref,
    value_ref,
    att_ref,
    top_ref,
    inv_ref,
    wq_ref,
    wk_ref,
    wv_ref,
    wo_ref,
    order_ref,
    back_ref,
    rows_ref,
    out_ref,
    give_ref,
    keep_ref,
    ga_ref,
    tot_ref,
    sq_ref,
    sk_ref,
    pb_ref,
):
    cells = x_ref.shape[0]
    chans, total = qt_ref.shape
    scale = chans ** (-0.5)
    mine = pl.ds(pl.multiple_of(place_ref[0] * cells, cells), cells)
    core = place_ref[1]
    wo_order = nt(wo_ref[...], order_ref[...]).astype(BF16)
    chunk = total // 4
    chunks = [slice(b * chunk, (b + 1) * chunk) for b in range(4)]
    for at in chunks:
        ga = nn(wo_order, grad_ref[:, at]).astype(BF16)
        ga_ref[:, at] = ga
        tot_ref[:, at] = jnp.sum(att_ref[:, at] * ga.astype(F32), 0, keepdims=True)

    key_mine = key_ref[mine, :]
    value_mine = value_ref[mine, :]
    q_mine = qt_ref[:, mine]
    ga_mine = ga_ref[:, mine]
    top_mine = top_ref[:, mine]
    inv_mine = inv_ref[:, mine]
    tot_mine = tot_ref[:, mine]

    def probs_of(scores, top, inv):
        return jnp.exp2((scores - top) * (scale * LOG2E)) * inv

    for at in chunks:
        probs = probs_of(nn(key_ref[at, :], q_mine), top_mine, inv_mine)
        grad_probs = nn(value_ref[at, :], ga_mine)
        sq_ref[at, :] = (probs * (grad_probs - tot_mine) * scale).astype(BF16)
        probs = probs_of(nn(key_mine, qt_ref[:, at]), top_ref[:, at], inv_ref[:, at])
        grad_probs = nn(value_mine, ga_ref[:, at])
        pb_ref[:, at] = probs.astype(BF16)
        sk_ref[:, at] = (probs * (grad_probs - tot_ref[:, at]) * scale).astype(BF16)

    gq = nn(kt_ref[...], sq_ref[...]).astype(BF16)
    gk = nt(qt_ref[...], sk_ref[...]).astype(BF16)
    gv = nt(ga_ref[...], pb_ref[...]).astype(BF16)
    x = nt(eye_of(chans), x_ref[...])
    recip = lax.rsqrt(jnp.mean(x * x, 0, keepdims=True) + 1e-06)
    normed = (x * recip).astype(BF16)
    grad_b = nn(back_ref[...], grad_ref[:, mine])
    grad_normed = nn(wq_ref[...], gq) + nn(wk_ref[...], gk) + nn(wv_ref[...], gv)
    inner = jnp.mean(grad_normed * x, 0, keepdims=True)
    out = grad_b + recip * grad_normed - x * (recip * recip * recip) * inner
    out_ref[...] = nt(eye_of(cells), out.astype(BF16)).astype(BF16)
    att = att_ref[:, mine].astype(BF16)
    gq_gv = jnp.concatenate([nt(eye_of(cells), gq), nt(eye_of(cells), gv)], 0).astype(BF16)
    gk_gb = jnp.concatenate(
        [nt(eye_of(cells), gk), nt(eye_of(cells), grad_b.astype(BF16))], 0
    ).astype(BF16)
    for half, to_ref in ((1 - core, give_ref), (core, keep_ref)):
        upper = nn(rows_ref[half, 0], normed).astype(BF16)
        lower = nn(rows_ref[half, 1], normed).astype(BF16)
        lower_att = nn(rows_ref[half, 1], att).astype(BF16)
        to_ref[:, 0:chans] = nn(jnp.concatenate([upper, lower], 1), gq_gv).astype(BF16)
        to_ref[:, chans:] = nn(jnp.concatenate([upper, lower_att], 1), gk_gb).astype(BF16)


def shards(
    features, past_frames, upstream, query_weight, key_weight, value_weight, out_weight, conv_weight
):
    slots, groups = lax.axis_size("dp"), lax.axis_size("rows")
    _, _, rows_here, width, chans = features.shape
    cells = rows_here * width
    total = cells * groups
    part = chans // groups
    per = part // slots
    me = lax.axis_index("rows")

    order = np.zeros((chans, chans), np.float32)
    for r in range(groups):
        for k in range(per):
            for d in range(slots):
                order[r * part + k * slots + d, d * per * groups + per * r + k] = 1.0
    order_b = jnp.asarray(order, BF16)
    back_b = jnp.asarray(order.T, BF16)

    pairs = slots // 2
    by_core = np.zeros((2, 2, pairs * groups * 8, chans), np.float32)
    for core in range(2):
        for pair in range(pairs):
            for r in range(groups):
                for k in range(per):
                    row = (pair * groups + r) * 8 + k
                    chan = (2 * pair + core) * per * groups + per * r + k
                    by_core[core, 0, row, chan] = 1.0
                    by_core[core, 1, row + 4, chan] = 1.0
    by_core = jnp.asarray(by_core, BF16)
    core = lax.rem(lax.axis_index("dp"), 2)

    x = features.reshape(cells, chans)
    u = upstream.reshape(cells, chans)
    past = past_frames.reshape(2, cells, chans)
    packed = pl.pallas_call(
        pack_kernel,
        out_shape=jax.ShapeDtypeStruct((groups, 2 * chans + 2 * part, cells), BF16),
        in_specs=whole(4),
        out_specs=pl.BlockSpec(memory_space=pltpu.VMEM),
        compiler_params=params(),
        name="pack",
    )(x, u, past, order_b)
    got = lax.all_to_all(packed, "rows", 0, 0)

    w_local = conv_weight[:, 18:27, :].reshape(per * 9, chans)
    w_local = jnp.pad(w_local, ((0, 32 - per * 9), (0, 0)))
    w_local, packed = lax.optimization_barrier((w_local, packed))
    w_near = w_local[None]
    w_near = jnp.concatenate([w_near, lax.ppermute(w_near, "dp", [(d, d ^ 1) for d in range(slots)])], 0)
    w_near = jnp.concatenate([w_near, lax.ppermute(w_near, "dp", [(d, d ^ 2) for d in range(slots)])], 0)
    w_all = [w_near]
    for back in (1, 2, 3):
        w_all.append(lax.ppermute(w_near, "dp", [(d, (d + 4 * back) % slots) for d in range(slots)]))

    grad_sent = pl.pallas_call(
        lambda *refs: conv_input_kernel(width, *refs),
        out_shape=jax.ShapeDtypeStruct((groups, part, total), BF16),
        in_specs=[pl.BlockSpec(memory_space=pltpu.SMEM)] + whole(5),
        out_specs=pl.BlockSpec(memory_space=pltpu.VMEM),
        scratch_shapes=[
            pltpu.VMEM((9 * part, total + 2 * width), F32),
            pltpu.VMEM((chans // 128, slots * 32, 128), F32),
            pltpu.VMEM((9 * part, chans), BF16),
        ],
        compiler_params=params(),
        name="conv_input",
    )(lax.axis_index("dp").reshape(1), got, *w_all)
    grad_all = lax.all_to_all(grad_sent, "rows", 0, 0).reshape(chans, total)

    qt, kt, key, value, att, top, inv, conv_terms = pl.pallas_call(
        lambda *refs: forward_kernel(width, *refs),
        out_shape=(
            jax.ShapeDtypeStruct((chans, total), BF16),
            jax.ShapeDtypeStruct((chans, total), BF16),
            jax.ShapeDtypeStruct((total, chans), BF16),
            jax.ShapeDtypeStruct((total, chans), BF16),
            jax.ShapeDtypeStruct((chans, total), F32),
            jax.ShapeDtypeStruct((1, total), F32),
            jax.ShapeDtypeStruct((1, total), F32),
            jax.ShapeDtypeStruct((slots, per * 32, chans), BF16),
        ),
        in_specs=[pl.BlockSpec(memory_space=pltpu.SMEM)] + whole(6),
        out_specs=tuple(whole(8)),
        scratch_shapes=[
            pltpu.VMEM((chans, total), BF16),
            pltpu.VMEM((9 * part, total + 2 * width), BF16),
            pltpu.VMEM((chans, total), BF16),
            pltpu.VMEM((chans // 128, 32 * part, 128), F32),
            pltpu.VMEM((total, cells), F32),
            pltpu.VMEM((total, cells), F32),
            pltpu.VMEM((total, cells), BF16),
        ],
        compiler_params=params(),
        name="forward",
    )(me.reshape(1), got, query_weight, key_weight, value_weight, out_weight, order_b)

    feature_grad, give, keep = pl.pallas_call(
        backward_kernel,
        out_shape=(
            jax.ShapeDtypeStruct((cells, chans), BF16),
            jax.ShapeDtypeStruct((pairs * groups * 8, 2 * chans), BF16),
            jax.ShapeDtypeStruct((pairs * groups * 8, 2 * chans), BF16),
        ),
        in_specs=[pl.BlockSpec(memory_space=pltpu.SMEM)] + whole(16),
        out_specs=tuple(whole(3)),
        scratch_shapes=[
            pltpu.VMEM((chans, total), BF16),
            pltpu.VMEM((1, total), F32),
            pltpu.VMEM((total, cells), BF16),
            pltpu.VMEM((cells, total), BF16),
            pltpu.VMEM((cells, total), BF16),
        ],
        compiler_params=params(),
        name="backward",
    )(
        jnp.stack([me, core]),
        x,
        grad_all,
        qt,
        kt,
        key,
        value,
        att,
        top,
        inv,
        query_weight,
        key_weight,
        value_weight,
        out_weight,
        order_b,
        back_b,
        by_core,
    )

    conv_sum = jnp.sum(lax.all_to_all(conv_terms, "dp", 0, 0).astype(F32), 0)
    conv_grad = conv_sum.reshape(per, 32, chans)[:, :27].reshape(per, 27 * chans)
    taken = lax.ppermute(give, "dp", [(d, d ^ 1) for d in range(slots)])
    chip = (keep.astype(F32) + taken.astype(F32)).astype(BF16)
    chip = chip.reshape(pairs * groups, 8, 2 * chans)
    same_core = [[d * groups + r for d in range(c, slots, 2) for r in range(groups)] for c in range(2)]
    chip = lax.all_to_all(chip, ("dp", "rows"), 0, 0, axis_index_groups=same_core)
    proj = jnp.sum(chip.astype(F32), 0).reshape(2, 4, 2, chans)[:, :per]
    proj_grads = proj.transpose(1, 0, 2, 3).reshape(per, 4 * chans)
    return feature_grad.reshape(features.shape), proj_grads, conv_grad


def solution(mesh):
    placed = (
        P("dp", None, "rows", None, None),
        P("dp", None, "rows", None, None),
        P("dp", None, "rows", None, None),
        P(),
        P(),
        P(),
        P(),
        P(("dp", "rows"), None, None),
    )
    return jax.shard_map(
        shards,
        mesh=mesh,
        in_specs=placed,
        out_specs=(
            P("dp", None, "rows", None, None),
            P(("dp", "rows"), None),
            P(("dp", "rows"), None),
        ),
        check_vma=False,
    )
```

time: 179 us -> 161 us (0.90)
  blocking collectives: 48.2 us -> 0 us
  waiting for transfers between devices: 27.9 us -> 56.3 us
  Pallas kernels: 62.2 us -> 53.2 us
  starting transfers between devices: 30.5 us -> 38.9 us
  other arithmetic: 0.96 us -> 3.78 us
    all_to_all x1 -> x0, blocking collectives: 48.2 us -> none  [shards(): got = lax.all_to_all(packed, 'rows', 0, 0)]
    ppermute x0 -> x6, waiting for transfers between devices: none -> 32.9 us  [the longest x1 24.4 us: shards(): lax.ppermute(w_near, 'dp', [(d, d ^ 2) for d in range(slots)])]
    ppermute x0 -> x6, starting transfers between devices: none -> 6.32 us  [the longest x3 4.45 us: shards(): lax.ppermute(w_near, 'dp', [(d, (d + 4 * back) % slots) for d in range(sl...]
    pallas_call x1, Pallas kernels: 35.5 us -> 30.2 us  [shards(): pl.pallas_call(lambda *refs: forward_kernel(width, *refs), out_shape=(jax...]
    all_to_all x4 -> x3, waiting for transfers between devices: 27.9 us -> 23.4 us  [the longest x1 14.2 us: shards(): lax.all_to_all(chip, ('dp', 'rows'), 0, 0, axis_index_groups=same_core)]
    pallas_call x1, Pallas kernels: 18.7 us -> 14.3 us  [shards(): pl.pallas_call(backward_kernel, out_shape=(jax.ShapeDtypeStruct((cells, c...]
    all_to_all x4 -> x3, starting transfers between devices: 24.1 us -> 27.9 us  [the longest x1 10.5 us: shards(): lax.all_to_all(chip, ('dp', 'rows'), 0, 0, axis_index_groups=same_core)]
    broadcast_in_dim x2 -> x0, local copies, waits for them, and re-layouts: 3.05 us -> none  [spread_over(): jnp.broadcast_to(block[None], (count, *block.shape))]
  transfers between devices with their start and end apart: 5 -> 10, of which waited for: 3 -> 8; matrix products, arithmetic and copies ran while one was open for 1% -> 5% of each run, Pallas kernels for 33% -> 28%
where the time goes in v2:
time: 161 us; the launch traced here: 160 us
  waiting for transfers between devices  56.3 us (35%)
  Pallas kernels  53.2 us (33%)
  starting transfers between devices  38.9 us (24%)
  local copies, waits for them, and re-layouts  6.71 us (4%)
  other arithmetic  3.78 us (2%)
    pallas_call x1, Pallas kernels, shards(): pl.pallas_call(lambda *refs: forward_kernel(width, *refs), out_shape=(jax...  30.2 us
    ppermute x1, waiting for transfers between devices, shards(): lax.ppermute(w_near, 'dp', [(d, d ^ 2) for d in range(slots)])  24.4 us
    pallas_call x1, Pallas kernels, shards(): pl.pallas_call(backward_kernel, out_shape=(jax.ShapeDtypeStruct((cells, c...  14.3 us
    all_to_all x1, waiting for transfers between devices, shards(): lax.all_to_all(chip, ('dp', 'rows'), 0, 0, axis_index_groups=same_core)  14.2 us
    all_to_all x1, starting transfers between devices, shards(): lax.all_to_all(chip, ('dp', 'rows'), 0, 0, axis_index_groups=same_core)  10.5 us
    all_to_all x1, starting transfers between devices, shards(): grad_all = lax.all_to_all(grad_sent, 'rows', 0, 0).reshape(chans, total)  9.92 us
    all_to_all x1, waiting for transfers between devices, shards(): got = lax.all_to_all(packed, 'rows', 0, 0)  9.21 us
    all_to_all x1, starting transfers between devices, shards(): got = lax.all_to_all(packed, 'rows', 0, 0)  7.48 us
  transfers between devices with their start and end apart: 10, of which 8 were waited for; matrix products, arithmetic and copies ran while one was open for 5% of the time, Pallas kernels for 28%

profile of v2, /device:TPU:1, one launch (start us, length us, event | category | flops | bytes accessed | tf_op | source)
XLA Modules:
  0.0 159.5 jit_solution(804567010118258078)
XLA Ops:
  0.6 3.8 %pack.1 = bf16[8,864,256]{2,1,0:T(8,128)(2,1)} custom-call(bf16[256,384]{1,0:T(8,128)(2,1)} %bitcast.18, bf16[256,384]{1,0:T(8,128)(2,1)} %bitcast.25, bf16[2,256,384]{2,1,0:T(8,128)(2,1)} %bitcast.21, bf16[384,384]{1,0:T(8,128)(2,1)} %constant.25.clone.order_ref.refs_6_), custom_call_target="tpu_custom_call" | custom-call | tf_op jit(solution)/shard_map/pack/pallas_call | solution.py:351
  4.4 7.5 %all-to-all-start = ((bf16[8,864,256]{2,1,0:T(8,128)(2,1)}), bf16[8,864,256]{2,1,0:T(8,128)(2,1)S(1)}, u32[]{:S(2)}, u32[]{:S(2)}) async-start(bf16[8,864,256]{2,1,0:T(8,128)(2,1)} %pack.1), calls=%async_computation | async-start | bytes 7077888 | tf_op jit(solution)/shard_map/all_to_all | solution.py:359
  11.9 1.4 slice.9
  13.3 1.4 reshape.47
  14.7 0.7 pad.4
  15.4 1.0 collective-permute-start
  16.4 0.8 collective-permute-done
  17.3 0.5 collective-permute-start.1
  17.7 24.4 %collective-permute-done.1 = bf16[2,32,384]{2,1,0:T(8,128)(2,1)S(1)} collective-permute-done((bf16[2,32,384]{2,1,0:T(8,128)(2,1)S(1)}, bf16[2,32,384]{2,1,0:T(8,128)(2,1)S(1)}, u32[]{:S(2)}, u32[]{:S(2)}) %collective-permute-start.1) | collective-permute-done | bytes 49184 | tf_op jit(solution)/shard_map/ppermute | solution.py:366
  42.1 0.7 pad_maximum_fusion.refs_2_
  42.8 3.8 %collective-permute-start.4 = (bf16[4,32,384]{2,1,0:T(8,128)(2,1)}, bf16[4,32,384]{2,1,0:T(8,128)(2,1)}, u32[]{:S(2)}, u32[]{:S(2)}) collective-permute-start(bf16[4,32,384]{2,1,0:T(8,128)(2,1)} %pad_maximum_fusion.refs_2_), channel_id=1, source_target_pairs={{0,96},{8,104},{16,112},{24,120},{32,0},{40,8},{48,16},{56,24},{64... | collective-permute-start | bytes 294920 | tf_op jit(solution)/shard_map/ppermute | solution.py:369
  46.5 0.0 collective-permute-start.3
  46.5 0.7 collective-permute-start.2
  47.2 2.3 %collective-permute-done.4.refs_5_ = bf16[4,32,384]{2,1,0:T(8,128)(2,1)} collective-permute-done((bf16[4,32,384]{2,1,0:T(8,128)(2,1)}, bf16[4,32,384]{2,1,0:T(8,128)(2,1)}, u32[]{:S(2)}, u32[]{:S(2)}) %collective-permute-start.4) | collective-permute-done | bytes 98336 | tf_op jit(solution)/shard_map/ppermute | solution.py:369
  49.5 2.6 %collective-permute-done.3.refs_4_ = bf16[4,32,384]{2,1,0:T(8,128)(2,1)} collective-permute-done((bf16[4,32,384]{2,1,0:T(8,128)(2,1)}, bf16[4,32,384]{2,1,0:T(8,128)(2,1)}, u32[]{:S(2)}, u32[]{:S(2)}) %collective-permute-start.3) | collective-permute-done | bytes 98336 | tf_op jit(solution)/shard_map/ppermute | solution.py:369
  52.0 0.7 collective-permute-done.2.refs_3_
  52.8 9.2 %all-to-all-done.refs_1_ = bf16[8,864,256]{2,1,0:T(8,128)(2,1)S(1)} async-done(((bf16[8,864,256]{2,1,0:T(8,128)(2,1)}), bf16[8,864,256]{2,1,0:T(8,128)(2,1)S(1)}, u32[]{:S(2)}, u32[]{:S(2)}) %all-to-all-start) | async-done | bytes 3538976 | tf_op jit(solution)/shard_map/all_to_all | solution.py:359
  62.0 0.0 copy-start
  62.0 1.7 %copy-done = bf16[8,864,256]{2,1,0:T(8,128)(2,1)} copy-done((bf16[8,864,256]{2,1,0:T(8,128)(2,1)}, bf16[8,864,256]{2,1,0:T(8,128)(2,1)S(1)}, u32[]{:S(2)}) %copy-start) | copy-done | bytes 3538968
  63.7 4.8 %conv_input.1 = bf16[8,48,2048]{2,1,0:T(8,128)(2,1)} custom-call(s32[1]{0:T(128)} %bitcast.3.refs_0_, bf16[8,864,256]{2,1,0:T(8,128)(2,1)} %copy-done, bf16[4,32,384]{2,1,0:T(8,128)(2,1)} %pad_maximum_fusion.refs_2_, bf16[4,32,384]{2,1,0:T(8,128)(2,1)} %collective-permute-done.2.refs_3_, bf16[4,32,384]{2,1,0:T(8,128)(2,1)} %collective-permute-done.3.refs_4_, ...), custom_call_target="tpu_custom_call" | custom-call | tf_op jit(solution)/shard_map/conv_input/pallas_call | solution.py:371
  68.6 9.9 %all-to-all-start.1 = ((bf16[8,48,2048]{2,1,0:T(8,128)(2,1)}), bf16[8,48,2048]{2,1,0:T(8,128)(2,1)S(1)}, u32[]{:S(2)}, u32[]{:S(2)}) async-start(bf16[8,48,2048]{2,1,0:T(8,128)(2,1)} %conv_input.1), calls=%async_computation.1 | async-start | bytes 3145728 | tf_op jit(solution)/shard_map/all_to_all | solution.py:384
  78.5 30.2 %forward.1 = (bf16[384,2048]{1,0:T(8,128)(2,1)}, bf16[384,2048]{1,0:T(8,128)(2,1)}, bf16[2048,384]{1,0:T(8,128)(2,1)}, bf16[2048,384]{1,0:T(8,128)(2,1)}, f32[38...) custom-call(s32[1]{0:T(128)} %bitcast.refs_0_, ...), custom_call_target="tpu_custom_call" | custom-call | tf_op jit(solution)/shard_map/forward/pallas_call | solution.py:386
  108.7 0.0 all-to-all-done.1
  108.7 0.0 copy-start.1
  108.7 4.6 %all-to-all-start.3 = ((bf16[16,96,384]{2,1,0:T(8,128)(2,1)}), bf16[16,96,384]{2,1,0:T(8,128)(2,1)S(1)}, u32[]{:S(2)}, u32[]{:S(2)}) async-start(bf16[16,96,384]{2,1,0:T(8,128)(2,1)} %get-tuple-element.26), calls=%async_computation.3 | async-start | bytes 2359296 | tf_op jit(solution)/shard_map/all_to_all | solution.py:451
  113.3 0.6 pad_add_fusion.place_ref
  113.9 0.0 copy-done.1
  113.9 14.3 %backward.1 = (bf16[256,384]{1,0:T(8,128)(2,1)}, bf16[512,768]{1,0:T(8,128)(2,1)}, bf16[512,768]{1,0:T(8,128)(2,1)}) custom-call(s32[2]{0:T(128)} %pad_add_fusion.place_ref, bf16[256,384]{1,0:T(8,128)(2,1)} %bitcast.19, bf16[384,2048]{1,0:T(8,128)(2,1)} %bitcast.17, bf16[384,2048]{1,0:T(8,128)(2,1)} %get-tuple-element.16.qt_ref, ...), custom_call_target="tpu_custom_call" | custom-call | tf_op jit(solution)/shard_map/backward/pallas_call | solution.py:413
  128.3 0.4 collective-permute-start.5
  128.7 2.1 %collective-permute-done.5 = bf16[512,768]{1,0:T(8,128)(2,1)S(1)} collective-permute-done((bf16[512,768]{1,0:T(8,128)(2,1)}, bf16[512,768]{1,0:T(8,128)(2,1)S(1)}, u32[]{:S(2)}, u32[]{:S(2)}) %collective-permute-start.5) | collective-permute-done | bytes 786464 | tf_op jit(solution)/shard_map/ppermute | solution.py:453
  130.8 2.2 %fusion = bf16[64,8,768]{2,1,0:T(8,128)(2,1)} fusion(bf16[512,768]{1,0:T(8,128)(2,1)S(1)} %collective-permute-done.5, bf16[512,768]{1,0:T(8,128)(2,1)} %get-tuple-element.24), kind=kLoop, calls=%fused_computation.3 | loop fusion | flops 1572864 | bytes 2359296 | tf_op jit(solution)/shard_map/reshape | solution.py:455
  133.0 0.0 all-to-all-done.3
  133.0 10.5 %all-to-all-start.2 = ((bf16[64,8,768]{2,1,0:T(8,128)(2,1)}), bf16[64,8,768]{2,1,0:T(8,128)(2,1)S(1)}, u32[]{:S(2)}, u32[]{:S(2)}) async-start(bf16[64,8,768]{2,1,0:T(8,128)(2,1)} %fusion), calls=%async_computation.2 | async-start | bytes 1572864 | tf_op jit(solution)/shard_map/all_to_all | solution.py:457
  143.6 0.2 convert_reduce_fusion
  143.8 0.8 copy.15
  144.5 14.2 %all-to-all-done.2 = bf16[64,8,768]{2,1,0:T(8,128)(2,1)S(1)} async-done(((bf16[64,8,768]{2,1,0:T(8,128)(2,1)}), bf16[64,8,768]{2,1,0:T(8,128)(2,1)S(1)}, u32[]{:S(2)}, u32[]{:S(2)}) %all-to-all-start.2) | async-done | bytes 786464 | tf_op jit(solution)/shard_map/all_to_all | solution.py:457
  158.7 0.1 convert_reduce_fusion.1
  158.9 0.6 reshape.52
  (5 shorter events, 0.1 us)
Async XLA Ops:
  4.4 57.5 %all-to-all-start = ((bf16[8,864,256]{2,1,0:T(8,128)(2,1)}), bf16[8,864,256]{2,1,0:T(8,128)(2,1)S(1)}, u32[]{:S(2)}, u32[]{:S(2)}) async-start(bf16[8,864,256]{2,1,0:T(8,128)(2,1)} %pack.1), calls=%async_computation | async-start | bytes 7077888 | tf_op jit(solution)/shard_map/all_to_all | solution.py:359
  15.4 1.8 %collective-permute-start = (bf16[1,32,384]{2,1,0:T(8,128)(2,1)S(1)}, bf16[1,32,384]{2,1,0:T(8,128)(2,1)S(1)}, u32[]{:S(2)}, u32[]{:S(2)}) collective-permute-start(bf16[1,32,384]{2,1,0:T(8,128)(2,1)S(1)} %bitcast.22), channel_id=1, source_target_pairs={{0,8},{8,0},{16,24},{24,16},{32,40},{40,32},{48,56},{56,48},{64,72... | collective-permute-start | bytes 73736 | tf_op jit(solution)/shard_map/ppermute | solution.py:365
  17.3 24.8 %collective-permute-start.1 = (bf16[2,32,384]{2,1,0:T(8,128)(2,1)S(1)}, bf16[2,32,384]{2,1,0:T(8,128)(2,1)S(1)}, u32[]{:S(2)}, u32[]{:S(2)}) collective-permute-start(bf16[2,32,384]{2,1,0:T(8,128)(2,1)S(1)} %pad_maximum_fusion.1), channel_id=1, source_target_pairs={{0,16},{8,24},{16,0},{24,8},{32,48},{40,56},{48,32},{56,40},{64,80... | collective-permute-start | bytes 147464 | tf_op jit(solution)/shard_map/ppermute | solution.py:366
  42.8 6.7 %collective-permute-start.4 = (bf16[4,32,384]{2,1,0:T(8,128)(2,1)}, bf16[4,32,384]{2,1,0:T(8,128)(2,1)}, u32[]{:S(2)}, u32[]{:S(2)}) collective-permute-start(bf16[4,32,384]{2,1,0:T(8,128)(2,1)} %pad_maximum_fusion.refs_2_), channel_id=1, source_target_pairs={{0,96},{8,104},{16,112},{24,120},{32,0},{40,8},{48,16},{56,24},{64... | collective-permute-start | bytes 294920 | tf_op jit(solution)/shard_map/ppermute | solution.py:369
  46.5 5.5 %collective-permute-start.3 = (bf16[4,32,384]{2,1,0:T(8,128)(2,1)}, bf16[4,32,384]{2,1,0:T(8,128)(2,1)}, u32[]{:S(2)}, u32[]{:S(2)}) collective-permute-start(bf16[4,32,384]{2,1,0:T(8,128)(2,1)} %pad_maximum_fusion.refs_2_), channel_id=1, source_target_pairs={{0,64},{8,72},{16,80},{24,88},{32,96},{40,104},{48,112},{56,120},{... | collective-permute-start | bytes 294920 | tf_op jit(solution)/shard_map/ppermute | solution.py:369
  46.5 6.2 %collective-permute-start.2 = (bf16[4,32,384]{2,1,0:T(8,128)(2,1)}, bf16[4,32,384]{2,1,0:T(8,128)(2,1)}, u32[]{:S(2)}, u32[]{:S(2)}) collective-permute-start(bf16[4,32,384]{2,1,0:T(8,128)(2,1)} %pad_maximum_fusion.refs_2_), channel_id=1, source_target_pairs={{0,32},{8,40},{16,48},{24,56},{32,64},{40,72},{48,80},{56,88},{64,... | collective-permute-start | bytes 294920 | tf_op jit(solution)/shard_map/ppermute | solution.py:369
  62.0 1.8 %copy-start = (bf16[8,864,256]{2,1,0:T(8,128)(2,1)}, bf16[8,864,256]{2,1,0:T(8,128)(2,1)S(1)}, u32[]{:S(2)}) copy-start(bf16[8,864,256]{2,1,0:T(8,128)(2,1)S(1)} %all-to-all-done.refs_1_) | copy-start | bytes 10616836
  68.6 40.1 %all-to-all-start.1 = ((bf16[8,48,2048]{2,1,0:T(8,128)(2,1)}), bf16[8,48,2048]{2,1,0:T(8,128)(2,1)S(1)}, u32[]{:S(2)}, u32[]{:S(2)}) async-start(bf16[8,48,2048]{2,1,0:T(8,128)(2,1)} %conv_input.1), calls=%async_computation.1 | async-start | bytes 3145728 | tf_op jit(solution)/shard_map/all_to_all | solution.py:384
  108.7 5.2 %copy-start.1 = (bf16[8,48,2048]{2,1,0:T(8,128)(2,1)}, bf16[8,48,2048]{2,1,0:T(8,128)(2,1)S(1)}, u32[]{:S(2)}) copy-start(bf16[8,48,2048]{2,1,0:T(8,128)(2,1)S(1)} %all-to-all-done.1) | copy-start | bytes 4718596
  108.7 24.3 %all-to-all-start.3 = ((bf16[16,96,384]{2,1,0:T(8,128)(2,1)}), bf16[16,96,384]{2,1,0:T(8,128)(2,1)S(1)}, u32[]{:S(2)}, u32[]{:S(2)}) async-start(bf16[16,96,384]{2,1,0:T(8,128)(2,1)} %get-tuple-element.26), calls=%async_computation.3 | async-start | bytes 2359296 | tf_op jit(solution)/shard_map/all_to_all | solution.py:451
  128.3 2.6 %collective-permute-start.5 = (bf16[512,768]{1,0:T(8,128)(2,1)}, bf16[512,768]{1,0:T(8,128)(2,1)S(1)}, u32[]{:S(2)}, u32[]{:S(2)}) collective-permute-start(bf16[512,768]{1,0:T(8,128)(2,1)} %get-tuple-element.25), channel_id=1, source_target_pairs={{0,8},{8,0},{16,24},{24,16},{32,40},{40,32},{48,56},{56,48},{64,72... | collective-permute-start | bytes 2359304 | tf_op jit(solution)/shard_map/ppermute | solution.py:453
  133.0 25.7 %all-to-all-start.2 = ((bf16[64,8,768]{2,1,0:T(8,128)(2,1)}), bf16[64,8,768]{2,1,0:T(8,128)(2,1)S(1)}, u32[]{:S(2)}, u32[]{:S(2)}) async-start(bf16[64,8,768]{2,1,0:T(8,128)(2,1)} %fusion), calls=%async_computation.2 | async-start | bytes 1572864 | tf_op jit(solution)/shard_map/all_to_all | solution.py:457

commit v3 on v2

v3 whole, which is shorter than its diff:
```python
import jax
import jax.numpy as jnp
import numpy as np
from jax import lax
from jax.experimental import pallas as pl
from jax.experimental.pallas import tpu as pltpu
from jax.sharding import PartitionSpec as P

F32 = jnp.float32
BF16 = jnp.bfloat16
LOG2E = 1.4426950408889634


def nn(a, b):
    return lax.dot_general(a, b, (((1,), (0,)), ((), ())), preferred_element_type=F32)


def nt(a, b):
    return lax.dot_general(a, b, (((1,), (1,)), ((), ())), preferred_element_type=F32)


def whole(count):
    return [pl.BlockSpec(memory_space=pltpu.VMEM)] * count


def anywhere(count):
    return [pl.BlockSpec(memory_space=pl.ANY)] * count


def in_hbm(count):
    return [pl.BlockSpec(memory_space=pltpu.HBM)] * count


def params(mib):
    return pltpu.CompilerParams(vmem_limit_bytes=mib * 1024 * 1024)


def cost(macs, size):
    return pl.CostEstimate(flops=2 * macs, bytes_accessed=size, transcendentals=0)


def eye_of(n):
    rows = lax.broadcasted_iota(jnp.int32, (n, n), 0)
    cols = lax.broadcasted_iota(jnp.int32, (n, n), 1)
    return jnp.where(rows == cols, 1.0, 0.0).astype(BF16)


def pack_kernel(u_ref, past_ref, order_ref, conv_ref, out_ref, w_ref):
    chans = u_ref.shape[1]
    groups = out_ref.shape[0]
    part = chans // groups
    w_ref[...] = jnp.zeros(w_ref.shape, BF16)
    for k in range(w_ref.shape[0]):
        w_ref[k, 0:11, :] = conv_ref[k, 16:27, :]
    u_t = nt(eye_of(chans), u_ref[...]).astype(BF16)
    for r in range(groups):
        out_ref[r, 0:chans, :] = u_t
    for f in range(2):
        p_t = nt(order_ref[...], past_ref[f]).astype(BF16)
        for r in range(groups):
            at = chans + f * part
            out_ref[r, at : at + part, :] = p_t[r * part : (r + 1) * part]


def prepare_kernel(me_ref, wq_ref, wk_ref, wv_ref, wo_ref, order_ref, wqkv_t_ref, wkv_ref, pick_ref, wo_pick_ref, wo_order_ref):
    chans = wq_ref.shape[0]
    part = pick_ref.shape[0]
    eye = eye_of(chans)
    for n, ref in enumerate((wq_ref, wk_ref, wv_ref)):
        wqkv_t_ref[n * chans : (n + 1) * chans, :] = nt(eye, ref[...]).astype(BF16)
    wkv_ref[:, 0:chans] = wk_ref[...]
    wkv_ref[:, chans:] = wv_ref[...]
    pick = order_ref[pl.ds(pl.multiple_of(me_ref[0] * part, part), part), :]
    pick_ref[...] = pick
    wo_pick_ref[...] = nn(pick, nt(eye, wo_ref[...]).astype(BF16)).astype(BF16)
    wo_order_ref[...] = nt(wo_ref[...], order_ref[...]).astype(BF16)


def conv_input_kernel(width, me_ref, got_ref, w_mine_ref, w_other_ref, *refs):
    out_ref, wide_ref, w32_ref, wcat_ref, grad_ref, sems = refs[-6:]
    groups = got_ref.shape[0]
    cells = got_ref.shape[2]
    part, total = out_ref.shape[1:]
    near, padded, chans = w_mine_ref.shape
    slots = 2 * near
    per = part // slots
    z, y, core = lax.div(me_ref[0], 4), lax.rem(lax.div(me_ref[0], 2), 2), lax.rem(me_ref[0], 2)
    for apart, w_ref in enumerate((w_mine_ref, w_other_ref)):
        for n in range(near):
            at = lax.rem(z + 4 - n // 2, 4) * 4 + lax.rem(y + n % 2, 2) * 2 + lax.rem(core + apart, 2)
            at = pl.ds(pl.multiple_of(at * padded, padded), padded)
            for c in range(chans // 128):
                w32_ref[c, at, :] = w_ref[n, :, c * 128 : (c + 1) * 128].astype(F32)
    for c in range(chans // 128):
        lanes = slice(c * 128, (c + 1) * 128)
        for tap in range(9):
            for k in range(per):
                rows = w32_ref[c, pl.ds(k * 16 + 2 + tap, slots, stride=padded), :]
                at = tap * part + k * slots
                wcat_ref[at : at + slots, lanes] = rows.astype(BF16)
    wide_ref[:, 0:width] = jnp.zeros((9 * part, width), F32)
    wide_ref[:, width + total :] = jnp.zeros((9 * part, width), F32)
    for r in range(groups):
        wide_ref[:, width + r * cells : width + (r + 1) * cells] = nn(
            wcat_ref[...], got_ref[r, 0:chans, :]
        )
    lane = lax.broadcasted_iota(jnp.int32, (part, total), 1) % width
    sums = []
    for j in range(3):
        piece = None
        for i in range(3):
            tap = 3 * i + j
            at = (2 - i) * width
            term = wide_ref[tap * part : (tap + 1) * part, at : at + total]
            piece = term if piece is None else piece + term
        sums.append(piece)
    first = jnp.where(lane == width - 1, 0.0, pltpu.roll(sums[0], total - 1, 1))
    last = jnp.where(lane == 0, 0.0, pltpu.roll(sums[2], 1, 1))
    grad_ref[...] = (first + sums[1] + last).astype(BF16)
    copies = [pltpu.make_async_copy(grad_ref, out_ref.at[r], sems.at[r]) for r in range(groups)]
    for copy in copies:
        copy.start()
    for copy in copies:
        copy.wait()


def forward_kernel(
    width,
    place_ref,
    got_in,
    x0_in,
    x1_in,
    x2_in,
    x3_in,
    x4_in,
    x5_in,
    x6_in,
    x7_in,
    wqkv_t_ref,
    wkv_ref,
    pick_ref,
    wo_pick_ref,
    qt_out,
    kt_out,
    key_out,
    value_out,
    att_out,
    top_ref,
    inv_ref,
    give_ref,
    keep_ref,
    got_ref,
    x_ref,
    qt_ref,
    kt_ref,
    key_ref,
    value_ref,
    att_ref,
    in_sems,
    x_sems,
    out_sems,
    att_sems,
    vt_ref,
    side_ref,
    ut_ref,
    acc_ref,
    even_ref,
    odd_ref,
    raised_ref,
):
    groups, cells = got_ref.shape[0], got_ref.shape[2]
    chans = wkv_ref.shape[0]
    total = groups * cells
    part = chans // groups

    me = place_ref[0]
    fetches = []
    for n, ref in enumerate((x0_in, x1_in, x2_in, x3_in, x4_in, x5_in, x6_in, x7_in)):
        plane = lax.rem(lax.div(me, 2) + (0, 3, 1, 2)[n // 2], 4)
        at = plane * 2 + lax.rem(me + n % 2, 2)
        fetches.append(pltpu.make_async_copy(ref, x_ref.at[at], x_sems.at[n]))
    for r in range(groups):
        fetches.append(pltpu.make_async_copy(got_in.at[r], got_ref.at[r], in_sems.at[r]))
    for fetch in fetches:
        fetch.start()
    kept = [(qt_ref, qt_out), (kt_ref, kt_out), (key_ref, key_out), (value_ref, value_out)]
    keeps = [pltpu.make_async_copy(a, b, out_sems.at[n]) for n, (a, b) in enumerate(kept)]

    def keep_att(r):
        at = pl.ds(pl.multiple_of(r * cells, cells), cells)
        return pltpu.make_async_copy(att_ref.at[:, at], att_out.at[:, at], att_sems.at[r])

    scale = chans ** (-0.5)
    def project(r, carry):
        x = x_ref[r].astype(F32)
        recip = lax.rsqrt(jnp.mean(x * x, 1, keepdims=True) + 1e-06)
        normed = (x * recip).astype(BF16)
        at = pl.ds(pl.multiple_of(r * cells, cells), cells)
        qkv_t = nt(wqkv_t_ref[...], normed).astype(BF16)
        qt_ref[:, at] = qkv_t[0:chans]
        kt_ref[:, at] = qkv_t[chans : 2 * chans]
        vt_ref[:, at] = qkv_t[2 * chans :]
        kv = nn(normed, wkv_ref[...]).astype(BF16)
        key_ref[at, :] = kv[:, 0:chans]
        value_ref[at, :] = kv[:, chans:]
        return carry

    for fetch in fetches[:groups]:
        fetch.wait()
    lax.fori_loop(0, groups, project, 0, unroll=2)
    for fetch in fetches[groups:]:
        fetch.wait()
    for copy in keeps:
        copy.start()
    for r in range(groups):
        ut_ref[:, r * cells : (r + 1) * cells] = got_ref[r, 0:chans, :]

    for n in range(9):
        rows = slice(n * part, (n + 1) * part)
        side_ref[rows, 0:width] = jnp.zeros((part, width), BF16)
        side_ref[rows, width + total :] = jnp.zeros((part, width), BF16)

    lane = lax.broadcasted_iota(jnp.int32, (part, width), 1)

    def place(t, at, block):
        for n in range(0, cells, width):
            one = block[:, n : n + width]
            one32 = one.astype(F32)
            left = jnp.where(lane == 0, 0.0, pltpu.roll(one32, 1, 1))
            right = jnp.where(lane == width - 1, 0.0, pltpu.roll(one32, width - 1, 1))
            for j, moved in enumerate((left.astype(BF16), one, right.astype(BF16))):
                rows = slice((3 * t + j) * part, (3 * t + j + 1) * part)
                side_ref[rows, width + at + n : 2 * width + at + n] = moved

    for r in range(groups):
        for f in range(2):
            at = chans + f * part
            place(f, r * cells, got_ref[r, at : at + part, :])

    even_ref[...] = nn(key_ref[...], qt_ref[:, 0:cells])
    chunk = total // 4

    def attend(r, now_ref, later_ref):
        later = jnp.minimum(r + 1, groups - 1)
        at = pl.ds(pl.multiple_of(r * cells, cells), cells)
        later = pl.ds(pl.multiple_of(later * cells, cells), cells)
        top = jnp.max(now_ref[...], 0, keepdims=True)
        count = jnp.zeros((1, cells), F32)
        for b in range(4):
            rows = slice(b * chunk, (b + 1) * chunk)
            later_ref[rows] = nn(key_ref[rows], qt_ref[:, later])
            raised = jnp.exp2((now_ref[rows] - top) * (scale * LOG2E))
            count = count + jnp.sum(raised, 0, keepdims=True)
            raised_ref[rows] = raised.astype(BF16)
        inv = 1.0 / count
        att = nn(vt_ref[...], raised_ref[...]) * inv
        att_ref[:, at] = att
        keep_att(r).start()
        top_ref[:, at] = top
        inv_ref[:, at] = inv

    def attend_two(n, carry):
        attend(2 * n, even_ref, odd_ref)
        attend(2 * n + 1, odd_ref, even_ref)
        return carry

    lax.fori_loop(0, groups // 2, attend_two, 0)
    for r in range(groups):
        x_pick = nt(pick_ref[...], x_ref[r])
        att = att_ref[:, r * cells : (r + 1) * cells].astype(BF16)
        place(2, r * cells, (x_pick + nn(wo_pick_ref[...], att)).astype(BF16))

    lane_tiles = chans // 128
    acc_ref[:, 27 * part :, :] = jnp.zeros((lane_tiles, 5 * part, 128), F32)
    for i in range(3):
        block = nt(side_ref[:, i * width : i * width + total], ut_ref[...])
        for t in range(3):
            for j in range(3):
                tap, at = 9 * t + 3 * i + j, (3 * t + j) * part
                for c in range(lane_tiles):
                    acc_ref[c, tap * part : (tap + 1) * part, :] = block[
                        at : at + part, c * 128 : (c + 1) * 128
                    ]
    near = give_ref.shape[0]
    for core, to_ref in ((1 - place_ref[1], give_ref), (place_ref[1], keep_ref)):
        for n in range(near):
            first = (n % 4) * 4 + (n // 4) * 2 + core
            for k in range(part // (2 * near)):
                for c in range(lane_tiles):
                    rows = acc_ref[c, pl.ds(k * 2 * near + first, 32, stride=part), :]
                    to_ref[n, k * 32 : (k + 1) * 32, c * 128 : (c + 1) * 128] = rows.astype(BF16)
    for copy in keeps:
        copy.wait()
    for r in range(groups):
        keep_att(r).wait()


def backward_kernel(
    place_ref,
    x_ref,
    grad_in,
    qt_in,
    kt_in,
    key_in,
    value_in,
    att_in,
    rows_in,
    top_ref,
    inv_ref,
    wq_ref,
    wk_ref,
    wv_ref,
    wo_order_ref,
    back_ref,
    out_ref,
    give_ref,
    keep_ref,
    grad_ref,
    qt_ref,
    kt_ref,
    key_ref,
    value_ref,
    att_ref,
    rows_ref,
    sems,
    ga_ref,
    tot_ref,
    sq_ref,
    sk_ref,
    pb_ref,
    pq_ref,
    pk_ref,
):
    cells = x_ref.shape[0]
    chans, total = qt_ref.shape
    moves = [
        (key_in, key_ref),
        (qt_in, qt_ref),
        (grad_in, grad_ref),
        (att_in, att_ref),
        (value_in, value_ref),
        (kt_in, kt_ref),
        (rows_in, rows_ref),
    ]
    moves = [pltpu.make_async_copy(a, b, sems.at[n]) for n, (a, b) in enumerate(moves)]
    for copy in moves:
        copy.start()
    scale = chans ** (-0.5)
    mine = pl.ds(pl.multiple_of(place_ref[0] * cells, cells), cells)
    core = place_ref[1]
    chunk = total // 4
    chunks = [slice(b * chunk, (b + 1) * chunk) for b in range(4)]

    def probs_of(scores, top, inv):
        return jnp.exp2((scores - top) * (scale * LOG2E)) * inv

    for copy in moves[0:2]:
        copy.wait()
    key_mine = key_ref[mine, :]
    q_mine = qt_ref[:, mine]
    top_mine = top_ref[:, mine]
    inv_mine = inv_ref[:, mine]
    for at in chunks:
        pq_ref[at, :] = probs_of(nn(key_ref[at, :], q_mine), top_mine, inv_mine)
        pk_ref[:, at] = probs_of(nn(key_mine, qt_ref[:, at]), top_ref[:, at], inv_ref[:, at])
    for copy in moves[2:4]:
        copy.wait()
    for at in chunks:
        ga = nn(wo_order_ref[...], grad_ref[:, at]).astype(BF16)
        ga_ref[:, at] = ga
        tot_ref[:, at] = jnp.sum(att_ref[:, at] * ga.astype(F32), 0, keepdims=True)
    moves[4].wait()
    value_mine = value_ref[mine, :]
    ga_mine = ga_ref[:, mine]
    tot_mine = tot_ref[:, mine]
    for at in chunks:
        grad_probs = nn(value_ref[at, :], ga_mine)
        sq_ref[at, :] = (pq_ref[at, :] * (grad_probs - tot_mine) * scale).astype(BF16)
        probs = pk_ref[:, at]
        grad_probs = nn(value_mine, ga_ref[:, at])
        pb_ref[:, at] = probs.astype(BF16)
        sk_ref[:, at] = (probs * (grad_probs - tot_ref[:, at]) * scale).astype(BF16)

    moves[5].wait()
    gq = nn(kt_ref[...], sq_ref[...]).astype(BF16)
    gk = nt(qt_ref[...], sk_ref[...]).astype(BF16)
    gv = nt(ga_ref[...], pb_ref[...]).astype(BF16)
    x = nt(eye_of(chans), x_ref[...])
    recip = lax.rsqrt(jnp.mean(x * x, 0, keepdims=True) + 1e-06)
    normed = (x * recip).astype(BF16)
    grad_b = nn(back_ref[...], grad_ref[:, mine])
    grad_normed = nn(wq_ref[...], gq) + nn(wk_ref[...], gk) + nn(wv_ref[...], gv)
    inner = jnp.mean(grad_normed * x, 0, keepdims=True)
    out = grad_b + recip * grad_normed - x * (recip * recip * recip) * inner
    out_ref[...] = nt(eye_of(cells), out.astype(BF16)).astype(BF16)
    moves[6].wait()
    att = att_ref[:, mine].astype(BF16)
    gq_gv = jnp.concatenate([nt(eye_of(cells), gq), nt(eye_of(cells), gv)], 0).astype(BF16)
    gk_gb = jnp.concatenate(
        [nt(eye_of(cells), gk), nt(eye_of(cells), grad_b.astype(BF16))], 0
    ).astype(BF16)
    for half, to_ref in ((1 - core, give_ref), (core, keep_ref)):
        upper = nn(rows_ref[half, 0], normed).astype(BF16)
        lower = nn(rows_ref[half, 1], normed).astype(BF16)
        lower_att = nn(rows_ref[half, 1], att).astype(BF16)
        to_ref[:, 0:chans] = nn(jnp.concatenate([upper, lower], 1), gq_gv).astype(BF16)
        to_ref[:, chans:] = nn(jnp.concatenate([upper, lower_att], 1), gk_gb).astype(BF16)


def shards(
    features, past_frames, upstream, query_weight, key_weight, value_weight, out_weight, conv_weight
):
    slots, groups = lax.axis_size("dp"), lax.axis_size("rows")
    _, _, rows_here, width, chans = features.shape
    cells = rows_here * width
    total = cells * groups
    part = chans // groups
    per = part // slots
    me = lax.axis_index("rows")

    order = np.zeros((chans, chans), np.float32)
    for r in range(groups):
        for k in range(per):
            for d in range(slots):
                order[r * part + k * slots + d, d * per * groups + per * r + k] = 1.0
    order_b = jnp.asarray(order, BF16)
    back_b = jnp.asarray(order.T, BF16)

    pairs = slots // 2
    by_core = np.zeros((2, 2, pairs * groups * 8, chans), np.float32)
    for core in range(2):
        for pair in range(pairs):
            for r in range(groups):
                for k in range(per):
                    row = (pair * groups + r) * 8 + k
                    chan = (2 * pair + core) * per * groups + per * r + k
                    by_core[core, 0, row, chan] = 1.0
                    by_core[core, 1, row + 4, chan] = 1.0
    by_core = jnp.asarray(by_core, BF16)
    core = lax.rem(lax.axis_index("dp"), 2)

    x = features.reshape(cells, chans)
    u = upstream.reshape(cells, chans)
    past = past_frames.reshape(2, cells, chans)
    def across(block):
        return lax.ppermute(block, "rows", [(r, r ^ 1) for r in range(groups)])

    def along(block, step):
        return lax.ppermute(block, "rows", [(r, (r + 2 * step) % groups) for r in range(groups)])

    x_across = across(x)
    x_low, x_high = along(x, 1), along(x, -1)

    packed, w_local = pl.pallas_call(
        pack_kernel,
        out_shape=(
            jax.ShapeDtypeStruct((groups, chans + 2 * part, cells), BF16),
            jax.ShapeDtypeStruct((per, 16, chans), BF16),
        ),
        in_specs=whole(4),
        out_specs=tuple(whole(2)),
        compiler_params=params(56),
        name="pack",
    )(u, past, order_b, conv_weight)

    w_near = w_local.reshape(1, per * 16, chans)
    w_across = lax.ppermute(w_near, "dp", [(d, d ^ 2) for d in range(slots)])
    packed, w_across, x_across, x_low, x_high, place = lax.optimization_barrier(
        (packed, w_across, x_across, x_low, x_high, me.reshape(1))
    )
    x_low_across, x_high_across = along(x_across, 1), along(x_across, -1)
    x_far, x_far_across = along(x_low, 1), along(x_high_across, -1)
    x_all = (x, x_across, x_low, x_low_across, x_high, x_high_across, x_far, x_far_across)
    got = lax.all_to_all(packed, "rows", 0, 0)
    w_near = jnp.concatenate([w_near, w_across], 0)
    w_line = [w_near]
    for back in (1, 2, 3):
        w_line.append(lax.ppermute(w_near, "dp", [(d, (d + 4 * back) % slots) for d in range(slots)]))
    w_mine = jnp.concatenate(w_line, 0)
    w_other = lax.ppermute(w_mine, "dp", [(d, d ^ 1) for d in range(slots)])

    wqkv_t, wkv, pick, wo_pick, wo_order = pl.pallas_call(
        prepare_kernel,
        out_shape=(
            jax.ShapeDtypeStruct((3 * chans, chans), BF16),
            jax.ShapeDtypeStruct((chans, 2 * chans), BF16),
            jax.ShapeDtypeStruct((part, chans), BF16),
            jax.ShapeDtypeStruct((part, chans), BF16),
            jax.ShapeDtypeStruct((chans, chans), BF16),
        ),
        in_specs=[pl.BlockSpec(memory_space=pltpu.SMEM)] + whole(5),
        out_specs=tuple(whole(5)),
        compiler_params=params(56),
        name="prepare",
    )(place, query_weight, key_weight, value_weight, out_weight, order_b)

    grad_sent = pl.pallas_call(
        lambda *refs: conv_input_kernel(width, *refs),
        out_shape=jax.ShapeDtypeStruct((groups, part, total), BF16),
        in_specs=[pl.BlockSpec(memory_space=pltpu.SMEM)] + whole(3) + anywhere(5),
        out_specs=in_hbm(1)[0],
        scratch_shapes=[
            pltpu.VMEM((9 * part, total + 2 * width), F32),
            pltpu.VMEM((chans // 128, slots * per * 16, 128), F32),
            pltpu.VMEM((9 * part, chans), BF16),
            pltpu.VMEM((part, total), BF16),
            pltpu.SemaphoreType.DMA((groups,)),
        ],
        compiler_params=params(56),
        name="conv_input",
    )(lax.axis_index("dp").reshape(1), got, w_mine, w_other, wo_order, *x_all[3:4], *x_all[5:])
    grad_all = lax.all_to_all(grad_sent, "rows", 0, 0).reshape(chans, total)

    qt, kt, key, value, att, top, inv, conv_give, conv_keep = pl.pallas_call(
        lambda *refs: forward_kernel(width, *refs),
        out_shape=(
            jax.ShapeDtypeStruct((chans, total), BF16),
            jax.ShapeDtypeStruct((chans, total), BF16),
            jax.ShapeDtypeStruct((total, chans), BF16),
            jax.ShapeDtypeStruct((total, chans), BF16),
            jax.ShapeDtypeStruct((chans, total), F32),
            jax.ShapeDtypeStruct((1, total), F32),
            jax.ShapeDtypeStruct((1, total), F32),
            jax.ShapeDtypeStruct((slots // 2, per * 32, chans), BF16),
            jax.ShapeDtypeStruct((slots // 2, per * 32, chans), BF16),
        ),
        in_specs=[pl.BlockSpec(memory_space=pltpu.SMEM)] + anywhere(9) + whole(4),
        out_specs=tuple(anywhere(5) + whole(4)),
        scratch_shapes=[
            pltpu.VMEM(got.shape, BF16),
            pltpu.VMEM((groups, cells, chans), BF16),
            pltpu.VMEM((chans, total), BF16),
            pltpu.VMEM((chans, total), BF16),
            pltpu.VMEM((total, chans), BF16),
            pltpu.VMEM((total, chans), BF16),
            pltpu.VMEM((chans, total), F32),
            pltpu.SemaphoreType.DMA((groups,)),
            pltpu.SemaphoreType.DMA((groups,)),
            pltpu.SemaphoreType.DMA((4,)),
            pltpu.SemaphoreType.DMA((groups,)),
            pltpu.VMEM((chans, total), BF16),
            pltpu.VMEM((9 * part, total + 2 * width), BF16),
            pltpu.VMEM((chans, total), BF16),
            pltpu.VMEM((chans // 128, 32 * part, 128), F32),
            pltpu.VMEM((total, cells), F32),
            pltpu.VMEM((total, cells), F32),
            pltpu.VMEM((total, cells), BF16),
        ],
        compiler_params=params(56),
        name="forward",
    )(jnp.stack([me, core]), got, *x_all, wqkv_t, wkv, pick, wo_pick)
    conv_taken = lax.ppermute(conv_give, "dp", [(d, d ^ 1) for d in range(slots)])

    feature_grad, give, keep = pl.pallas_call(
        backward_kernel,
        out_shape=(
            jax.ShapeDtypeStruct((cells, chans), BF16),
            jax.ShapeDtypeStruct((pairs * groups * 8, 2 * chans), BF16),
            jax.ShapeDtypeStruct((pairs * groups * 8, 2 * chans), BF16),
        ),
        in_specs=[pl.BlockSpec(memory_space=pltpu.SMEM)] + whole(1) + anywhere(7) + whole(7),
        out_specs=tuple(whole(3)),
        scratch_shapes=[
            pltpu.VMEM((chans, total), BF16),
            pltpu.VMEM((chans, total), BF16),
            pltpu.VMEM((chans, total), BF16),
            pltpu.VMEM((total, chans), BF16),
            pltpu.VMEM((total, chans), BF16),
            pltpu.VMEM((chans, total), F32),
            pltpu.VMEM(by_core.shape, BF16),
            pltpu.SemaphoreType.DMA((7,)),
            pltpu.VMEM((chans, total), BF16),
            pltpu.VMEM((1, total), F32),
            pltpu.VMEM((total, cells), BF16),
            pltpu.VMEM((cells, total), BF16),
            pltpu.VMEM((cells, total), BF16),
            pltpu.VMEM((total, cells), F32),
            pltpu.VMEM((cells, total), F32),
        ],
        compiler_params=params(56),
        name="backward",
    )(
        jnp.stack([me, core]),
        x,
        grad_all,
        qt,
        kt,
        key,
        value,
        att,
        by_core,
        top,
        inv,
        query_weight,
        key_weight,
        value_weight,
        wo_order,
        back_b,
    )

    taken = lax.ppermute(give, "dp", [(d, d ^ 1) for d in range(slots)])
    chip = (keep.astype(F32) + taken.astype(F32)).astype(BF16)
    chip = chip.reshape(pairs * groups, 8, 2 * chans)
    same_core = [[d * groups + r for d in range(c, slots, 2) for r in range(groups)] for c in range(2)]
    conv_taken, chip = lax.optimization_barrier((conv_taken, chip))
    got_chip = lax.all_to_all(chip, ("dp", "rows"), 0, 0, axis_index_groups=same_core)
    me_dp = lax.axis_index("dp")
    z, y = lax.div(me_dp, 4), lax.rem(lax.div(me_dp, 2), 2)
    conv_line = conv_keep.astype(F32) + conv_taken.astype(F32)
    sent = lax.dynamic_slice_in_dim(conv_line, (1 - y) * 4, 4, 0).astype(BF16)
    taken = lax.ppermute(sent, "dp", [(d, d ^ 2) for d in range(slots)])
    conv_line = lax.dynamic_slice_in_dim(conv_line, y * 4, 4, 0) + taken.astype(F32)
    conv_sum = lax.dynamic_index_in_dim(conv_line, z, 0, keepdims=False)
    for on in (1, 2, 3):
        sent = lax.dynamic_index_in_dim(conv_line, lax.rem(z + on, 4), 0, keepdims=False).astype(BF16)
        taken = lax.ppermute(sent, "dp", [(d, (d + 4 * on) % slots) for d in range(slots)])
        conv_sum = conv_sum + taken.astype(F32)
    conv_grad = conv_sum.reshape(per, 32, chans)[:, :27].reshape(per, 27 * chans)
    proj = jnp.sum(got_chip.astype(F32), 0).reshape(2, 4, 2, chans)[:, :per]
    proj_grads = proj.transpose(1, 0, 2, 3).reshape(per, 4 * chans)
    return feature_grad.reshape(features.shape), proj_grads, conv_grad


def solution(mesh):
    placed = (
        P("dp", None, "rows", None, None),
        P("dp", None, "rows", None, None),
        P("dp", None, "rows", None, None),
        P(),
        P(),
        P(),
        P(),
        P(("dp", "rows"), None, None),
    )
    return jax.shard_map(
        shards,
        mesh=mesh,
        in_specs=placed,
        out_specs=(
            P("dp", None, "rows", None, None),
            P(("dp", "rows"), None),
            P(("dp", "rows"), None),
        ),
        check_vma=False,
    )
```

time: 161 us -> 139 us (0.86)
  waiting for transfers between devices: 56.3 us -> 28.4 us
  starting transfers between devices: 38.9 us -> 51.2 us
  Pallas kernels: 53.2 us -> 48.9 us
  local copies, waits for them, and re-layouts: 6.71 us -> 4.86 us
    ppermute x2 -> x14, starting transfers between devices: 1.43 us -> 24.3 us  [the longest x6 10.1 us: along(): lax.ppermute(block, 'rows', [(r, (r + 2 * step) % groups) for r in range(...]
    all_to_all x1, waiting for transfers between devices: 14.2 us -> 0.01 us  [shards(): lax.all_to_all(chip, ('dp', 'rows'), 0, 0, axis_index_groups=same_core)]
    all_to_all x1, waiting for transfers between devices: 9.21 us -> 0.01 us  [shards(): got = lax.all_to_all(packed, 'rows', 0, 0)]
    all_to_all x1, starting transfers between devices: 9.92 us -> 3.59 us  [shards(): grad_all = lax.all_to_all(grad_sent, 'rows', 0, 0).reshape(chans, total)]
    ppermute x3, waiting for transfers between devices: 5.55 us -> 0.12 us  [shards(): lax.ppermute(w_near, 'dp', [(d, (d + 4 * back) % slots) for d in range(sl...]
    pallas_call x1, Pallas kernels: 30.2 us -> 25.2 us  [shards(): pl.pallas_call(lambda *refs: forward_kernel(width, *refs), out_shape=(jax...]
    all_to_all x1 -> x0, starting transfers between devices: 4.59 us -> none  [shards(): conv_sum = jnp.sum(lax.all_to_all(conv_terms, 'dp', 0, 0).astype(F32), 0)]
    all_to_all x1, starting transfers between devices: 7.48 us -> 3.6 us  [shards(): got = lax.all_to_all(packed, 'rows', 0, 0)]
  transfers between devices with their start and end apart: 10 -> 21, of which waited for: 8 -> 8; matrix products, arithmetic and copies ran while one was open for 5% -> 3% of each run, Pallas kernels for 28% -> 23%
where the time goes in v3:
time: 139 us; the launch traced here: 137 us
  starting transfers between devices  51.2 us (37%)
  Pallas kernels  48.9 us (35%)
  waiting for transfers between devices  28.4 us (20%)
  local copies, waits for them, and re-layouts  4.86 us (3%)
  other arithmetic  3.15 us (2%)
    pallas_call x1, Pallas kernels, shards(): pl.pallas_call(lambda *refs: forward_kernel(width, *refs), out_shape=(jax...  25.2 us
    ppermute x6, waiting for transfers between devices, along(): lax.ppermute(block, 'rows', [(r, (r + 2 * step) % groups) for r in range(...  14.2 us
    pallas_call x1, Pallas kernels, shards(): pl.pallas_call(backward_kernel, out_shape=(jax.ShapeDtypeStruct((cells, c...  12.9 us
    all_to_all x1, starting transfers between devices, shards(): lax.all_to_all(chip, ('dp', 'rows'), 0, 0, axis_index_groups=same_core)  12 us
    ppermute x6, starting transfers between devices, along(): lax.ppermute(block, 'rows', [(r, (r + 2 * step) % groups) for r in range(...  10.1 us
    ppermute x3, waiting for transfers between devices, shards(): lax.ppermute(sent, 'dp', [(d, (d + 4 * on) % slots) for d in range(slots)])  9.67 us
    ppermute x3, starting transfers between devices, shards(): lax.ppermute(w_near, 'dp', [(d, (d + 4 * back) % slots) for d in range(sl...  5.74 us
    ppermute x3, starting transfers between devices, shards(): lax.ppermute(sent, 'dp', [(d, (d + 4 * on) % slots) for d in range(slots)])  4.76 us
  transfers between devices with their start and end apart: 21, of which 8 were waited for; matrix products, arithmetic and copies ran while one was open for 3% of the time, Pallas kernels for 23%

profile of v3, /device:TPU:1, one launch (start us, length us, event | category | flops | bytes accessed | tf_op | source)
XLA Modules:
  0.0 137.5 jit_solution(368638786851693741)
XLA Ops:
  0.6 3.8 %collective-permute-start.1 = (bf16[256,384]{1,0:T(8,128)(2,1)}, bf16[256,384]{1,0:T(8,128)(2,1)S(1)}, u32[]{:S(2)}, u32[]{:S(2)}) collective-permute-start(bf16[256,384]{1,0:T(8,128)(2,1)} %bitcast.32), channel_id=1, source_target_pairs={{0,1},{1,0},{2,3},{3,2},{4,5},{5,4},{6,7},{7,6},{8,9},{9,8},{10,11... | collective-permute-start | bytes 589832 | tf_op jit(solution)/shard_map/ppermute | solution.py:446
  4.5 1.2 collective-permute-start.2
  5.7 1.5 %collective-permute-start.3 = (bf16[256,384]{1,0:T(8,128)(2,1)}, bf16[256,384]{1,0:T(8,128)(2,1)S(1)}, u32[]{:S(2)}, u32[]{:S(2)}) collective-permute-start(bf16[256,384]{1,0:T(8,128)(2,1)} %bitcast.34), channel_id=1, source_target_pairs={{0,6},{1,7},{2,0},{3,1},{4,2},{5,3},{6,4},{7,5},{8,14},{9,15},{10,... | collective-permute-start | bytes 589832 | tf_op jit(solution)/shard_map/ppermute | solution.py:449
  7.1 3.0 %pack.1 = (bf16[8,480,256]{2,1,0:T(8,128)(2,1)}, bf16[3,16,384]{2,1,0:T(8,128)(2,1)}) custom-call(bf16[256,384]{1,0:T(8,128)(2,1)} %bitcast.39, bf16[2,256,384]{2,1,0:T(8,128)(2,1)} %bitcast.38, bf16[384,384]{1,0:T(8,128)(2,1)} %constant.53.clone.order_ref, bf16[3,27,384]{2,1,0:T(8,128)(2,1)} %conv_ref.1), custom_call_target="tpu_custom_call" | custom-call | tf_op jit(solution)/shard_map/pack/pallas_call | solution.py:454
  10.1 0.4 collective-permute-start
  10.5 2.6 %collective-permute-done = bf16[1,48,384]{2,1,0:T(8,128)(2,1)S(1)} collective-permute-done((bf16[1,48,384]{2,1,0:T(8,128)(2,1)}, bf16[1,48,384]{2,1,0:T(8,128)(2,1)S(1)}, u32[]{:S(2)}, u32[]{:S(2)}) %collective-permute-start) | collective-permute-done | bytes 36896 | tf_op jit(solution)/shard_map/ppermute | solution.py:467
  13.2 0.0 collective-permute-done.3.refs_6_
  13.2 0.7 copy-done.10
  13.9 3.6 %all-to-all-start = ((bf16[8,480,256]{2,1,0:T(8,128)(2,1)}), bf16[8,480,256]{2,1,0:T(8,128)(2,1)S(1)}, u32[]{:S(2)}, u32[]{:S(2)}) async-start(bf16[8,480,256]{2,1,0:T(8,128)(2,1)} %get-tuple-element.32), calls=%async_computation | async-start | bytes 3932160 | tf_op jit(solution)/shard_map/all_to_all | solution.py:474
  17.5 1.7 %collective-permute-start.4 = (bf16[2,48,384]{2,1,0:T(8,128)(2,1)S(1)}, bf16[2,48,384]{2,1,0:T(8,128)(2,1)S(1)}, u32[]{:S(2)}, u32[]{:S(2)}) collective-permute-start(bf16[2,48,384]{2,1,0:T(8,128)(2,1)S(1)} %pad_maximum_fusion), channel_id=1, source_target_pairs={{0,32},{8,40},{16,48},{24,56},{32,64},{40,72},{48,80},{56,88},{64,... | collective-permute-start | bytes 221192 | tf_op jit(solution)/shard_map/ppermute | solution.py:478
  19.2 3.3 %collective-permute-start.5 = (bf16[2,48,384]{2,1,0:T(8,128)(2,1)S(1)}, bf16[2,48,384]{2,1,0:T(8,128)(2,1)S(1)}, u32[]{:S(2)}, u32[]{:S(2)}) collective-permute-start(bf16[2,48,384]{2,1,0:T(8,128)(2,1)S(1)} %pad_maximum_fusion), channel_id=1, source_target_pairs={{0,64},{8,72},{16,80},{24,88},{32,96},{40,104},{48,112},{56,120},{... | collective-permute-start | bytes 221192 | tf_op jit(solution)/shard_map/ppermute | solution.py:478
  22.5 0.7 collective-permute-start.6
  23.3 2.6 %collective-permute-start.9 = (bf16[256,384]{1,0:T(8,128)(2,1)S(1)}, bf16[256,384]{1,0:T(8,128)(2,1)S(1)}, u32[]{:S(2)}, u32[]{:S(2)}) collective-permute-start(bf16[256,384]{1,0:T(8,128)(2,1)S(1)} %collective-permute-done.1.refs_3_), channel_id=1, source_target_pairs={{0,6},{1,7},{2,0},{3,1},{4,2},{5,3},{6,4},{7,5},{8,14},{9,15},{10,... | collective-permute-start | bytes 589832 | tf_op jit(solution)/shard_map/ppermute | solution.py:449
  25.9 0.1 collective-permute-done.6
  26.1 4.2 %collective-permute-start.7 = (bf16[8,48,384]{2,1,0:T(8,128)(2,1)S(1)}, bf16[8,48,384]{2,1,0:T(8,128)(2,1)S(1)}, u32[]{:S(2)}, u32[]{:S(2)}) collective-permute-start(bf16[8,48,384]{2,1,0:T(8,128)(2,1)S(1)} %constant_dynamic-update-slice_fusion.refs_2_), channel_id=1, source_target_pairs={{0,8},{8,0},{16,24},{24,16},{32,40},{40,32},{48,56},{56,48},{64,72... | collective-permute-start | bytes 884744 | tf_op jit(solution)/shard_map/ppermute | solution.py:480
  30.2 1.6 %collective-permute-start.8 = (bf16[256,384]{1,0:T(8,128)(2,1)S(1)}, bf16[256,384]{1,0:T(8,128)(2,1)S(1)}, u32[]{:S(2)}, u32[]{:S(2)}) collective-permute-start(bf16[256,384]{1,0:T(8,128)(2,1)S(1)} %collective-permute-done.1.refs_3_), channel_id=1, source_target_pairs={{0,2},{1,3},{2,4},{3,5},{4,6},{5,7},{6,0},{7,1},{8,10},{9,11},{10,... | collective-permute-start | bytes 589832 | tf_op jit(solution)/shard_map/ppermute | solution.py:449
  31.9 1.2 collective-permute-start.10
  33.1 11.3 %collective-permute-done.9.refs_6_.refs_7_ = bf16[256,384]{1,0:T(8,128)(2,1)S(1)} collective-permute-done((bf16[256,384]{1,0:T(8,128)(2,1)S(1)}, bf16[256,384]{1,0:T(8,128)(2,1)S(1)}, u32[]{:S(2)}, u32[]{:S(2)}) %collective-permute-start.9) | collective-permute-done | bytes 196640 | tf_op jit(solution)/shard_map/ppermute | solution.py:449
  44.3 2.0 %collective-permute-start.11 = (bf16[256,384]{1,0:T(8,128)(2,1)S(1)}, bf16[256,384]{1,0:T(8,128)(2,1)S(1)}, u32[]{:S(2)}, u32[]{:S(2)}) collective-permute-start(bf16[256,384]{1,0:T(8,128)(2,1)S(1)} %collective-permute-done.9.refs_6_.refs_7_), channel_id=1, source_target_pairs={{0,6},{1,7},{2,0},{3,1},{4,2},{5,3},{6,4},{7,5},{8,14},{9,15},{10,... | collective-permute-start | bytes 589832 | tf_op jit(solution)/shard_map/ppermute | solution.py:449
  46.3 3.5 %prepare.1 = (bf16[1152,384]{1,0:T(8,128)(2,1)}, bf16[384,768]{1,0:T(8,128)(2,1)}, bf16[48,384]{1,0:T(8,128)(2,1)}, bf16[48,384]{1,0:T(8,128)(2,1)}, bf16[384,384]{1,0:T(8,128)(2,1)}) custom-call(s32[1]{0:T(128)} %bitcast.me_ref, bf16[384,384]{1,0:T(8,128)(2,1)} %wq_ref.3, bf16[384,384]{1,0:T(8,128)(2,1)} %wk_ref.3, bf16[384,384]{1,0:T(8,128)(2,1)} %wv_ref.3, ...), custom_call_target="tpu_custom_call" | custom-call | tf_op jit(solution)/shard_map/prepare/pallas_call | solution.py:482
  49.8 2.9 %collective-permute-done.10.refs_7_.refs_8_ = bf16[256,384]{1,0:T(8,128)(2,1)S(1)} collective-permute-done((bf16[256,384]{1,0:T(8,128)(2,1)}, bf16[256,384]{1,0:T(8,128)(2,1)S(1)}, u32[]{:S(2)}, u32[]{:S(2)}) %collective-permute-start.10) | collective-permute-done | bytes 196640 | tf_op jit(solution)/shard_map/ppermute | solution.py:449
  52.8 0.6 copy-done.4
  53.4 0.1 copy-done.8
  53.5 0.1 copy-done.5
  53.6 0.6 copy-done
  54.2 4.3 %conv_input.1 = bf16[8,48,2048]{2,1,0:T(8,128)(2,1)} custom-call(s32[1]{0:T(128)} %bitcast.3.refs_0_, bf16[8,480,256]{2,1,0:T(8,128)(2,1)} %copy-done, bf16[8,48,384]{2,1,0:T(8,128)(2,1)} %copy-done.7, bf16[8,48,384]{2,1,0:T(8,128)(2,1)} %copy-done.8, bf16[384,384]{1,0:T(8,128)(2,1)} %get-tuple-element.35.refs_4_.wo_order_ref, bf16[256,384]{1,0:T(8,128)(2,1)} %copy-done.3, ...), custom_call_target="tpu_custom_call" | custom-call | tf_op jit(solution)/shard_map/conv_input/pallas_call | solution.py:497
  58.5 3.6 %all-to-all-start.1 = ((bf16[8,48,2048]{2,1,0:T(8,128)(2,1)}), bf16[8,48,2048]{2,1,0:T(8,128)(2,1)S(1)}, u32[]{:S(2)}, u32[]{:S(2)}) async-start(bf16[8,48,2048]{2,1,0:T(8,128)(2,1)} %conv_input.1), calls=%async_computation.1 | async-start | bytes 3145728 | tf_op jit(solution)/shard_map/all_to_all | solution.py:512
  62.1 0.6 pad_add_fusion.refs_0_.place_ref
  62.7 25.2 %forward.1 = (bf16[384,2048]{1,0:T(8,128)(2,1)}, bf16[384,2048]{1,0:T(8,128)(2,1)}, bf16[2048,384]{1,0:T(8,128)(2,1)}, bf16[2048,384]{1,0:T(8,128)(2,1)}, f32[38...) custom-call(s32[2]{0:T(128)} %pad_add_fusion.refs_0_.place_ref, ...), custom_call_target="tpu_custom_call" | custom-call | tf_op jit(solution)/shard_map/forward/pallas_call | solution.py:514
  88.0 1.1 copy-done.1
  89.1 12.9 %backward.1 = (bf16[256,384]{1,0:T(8,128)(2,1)}, bf16[512,768]{1,0:T(8,128)(2,1)}, bf16[512,768]{1,0:T(8,128)(2,1)}) custom-call(s32[2]{0:T(128)} %pad_add_fusion.refs_0_.place_ref, bf16[256,384]{1,0:T(8,128)(2,1)} %bitcast.36, bf16[384,2048]{1,0:T(8,128)(2,1)} %bitcast.31, bf16[384,2048]{1,0:T(8,128)(2,1)} %get-tuple-element.43.qt_in, ...), custom_call_target="tpu_custom_call" | custom-call | tf_op jit(solution)/shard_map/backward/pallas_call | solution.py:554
  102.1 1.9 %collective-permute-start.13 = (bf16[512,768]{1,0:T(8,128)(2,1)}, bf16[512,768]{1,0:T(8,128)(2,1)S(1)}, u32[]{:S(2)}, u32[]{:S(2)}) collective-permute-start(bf16[512,768]{1,0:T(8,128)(2,1)} %get-tuple-element.53), channel_id=1, source_target_pairs={{0,8},{8,0},{16,24},{24,16},{32,40},{40,32},{48,56},{56,48},{64,72... | collective-permute-start | bytes 2359304 | tf_op jit(solution)/shard_map/ppermute | solution.py:601
  104.0 0.3 collective-permute-start.12
  104.3 1.8 %collective-permute-done.13 = bf16[512,768]{1,0:T(8,128)(2,1)S(1)} collective-permute-done((bf16[512,768]{1,0:T(8,128)(2,1)}, bf16[512,768]{1,0:T(8,128)(2,1)S(1)}, u32[]{:S(2)}, u32[]{:S(2)}) %collective-permute-start.13) | collective-permute-done | bytes 786464 | tf_op jit(solution)/shard_map/ppermute | solution.py:601
  106.1 2.2 %fusion = bf16[64,8,768]{2,1,0:T(8,128)(2,1)} fusion(bf16[512,768]{1,0:T(8,128)(2,1)S(1)} %collective-permute-done.13, bf16[512,768]{1,0:T(8,128)(2,1)} %get-tuple-element.52), kind=kLoop, calls=%fused_computation.3 | loop fusion | flops 1572864 | bytes 2359296 | tf_op jit(solution)/shard_map/reshape | solution.py:603
  108.3 0.1 convert_add_fusion
  108.5 0.8 collective-permute-start.14
  109.2 12.0 %all-to-all-start.2 = ((bf16[64,8,768]{2,1,0:T(8,128)(2,1)}), bf16[64,8,768]{2,1,0:T(8,128)(2,1)S(1)}, u32[]{:S(2)}, u32[]{:S(2)}) async-start(bf16[64,8,768]{2,1,0:T(8,128)(2,1)} %fusion), calls=%async_computation.2 | async-start | bytes 1572864 | tf_op jit(solution)/shard_map/all_to_all | solution.py:606
  121.3 0.1 convert_add_fusion.1
  121.4 1.1 collective-permute-start.15
  122.5 2.6 %collective-permute-start.16 = (bf16[96,384]{1,0:T(8,128)(2,1)S(1)}, bf16[96,384]{1,0:T(8,128)(2,1)S(1)}, u32[]{:S(2)}, u32[]{:S(2)}) collective-permute-start(bf16[96,384]{1,0:T(8,128)(2,1)S(1)} %get-tuple-element.59), channel_id=1, source_target_pairs={{0,64},{8,72},{16,80},{24,88},{32,96},{40,104},{48,112},{56,120},{... | collective-permute-start | bytes 221192 | tf_op jit(solution)/shard_map/ppermute | solution.py:616
  125.1 1.1 collective-permute-start.17
  126.2 0.2 collective-permute-done.15
  126.4 9.0 %collective-permute-done.16 = bf16[96,384]{1,0:T(8,128)(2,1)S(1)} collective-permute-done((bf16[96,384]{1,0:T(8,128)(2,1)S(1)}, bf16[96,384]{1,0:T(8,128)(2,1)S(1)}, u32[]{:S(2)}, u32[]{:S(2)}) %collective-permute-start.16) | collective-permute-done | bytes 73760 | tf_op jit(solution)/shard_map/ppermute | solution.py:616
  135.4 0.4 collective-permute-done.17
  135.9 0.8 copy.15
  136.7 0.1 convert_reduce_fusion
  136.8 0.6 reshape.55
  (45 shorter events, 0.3 us)
Async XLA Ops:
  0.6 12.5 %collective-permute-start.1 = (bf16[256,384]{1,0:T(8,128)(2,1)}, bf16[256,384]{1,0:T(8,128)(2,1)S(1)}, u32[]{:S(2)}, u32[]{:S(2)}) collective-permute-start(bf16[256,384]{1,0:T(8,128)(2,1)} %bitcast.32), channel_id=1, source_target_pairs={{0,1},{1,0},{2,3},{3,2},{4,5},{5,4},{6,7},{7,6},{8,9},{9,8},{10,11... | collective-permute-start | bytes 589832 | tf_op jit(solution)/shard_map/ppermute | solution.py:446
  4.5 8.7 %collective-permute-start.2 = (bf16[256,384]{1,0:T(8,128)(2,1)}, bf16[256,384]{1,0:T(8,128)(2,1)}, u32[]{:S(2)}, u32[]{:S(2)}) collective-permute-start(bf16[256,384]{1,0:T(8,128)(2,1)} %bitcast.33), channel_id=1, source_target_pairs={{0,2},{1,3},{2,4},{3,5},{4,6},{5,7},{6,0},{7,1},{8,10},{9,11},{10,... | collective-permute-start | bytes 589832 | tf_op jit(solution)/shard_map/ppermute | solution.py:449
  5.7 7.5 %collective-permute-start.3 = (bf16[256,384]{1,0:T(8,128)(2,1)}, bf16[256,384]{1,0:T(8,128)(2,1)S(1)}, u32[]{:S(2)}, u32[]{:S(2)}) collective-permute-start(bf16[256,384]{1,0:T(8,128)(2,1)} %bitcast.34), channel_id=1, source_target_pairs={{0,6},{1,7},{2,0},{3,1},{4,2},{5,3},{6,4},{7,5},{8,14},{9,15},{10,... | collective-permute-start | bytes 589832 | tf_op jit(solution)/shard_map/ppermute | solution.py:449
  10.1 3.0 %collective-permute-start = (bf16[1,48,384]{2,1,0:T(8,128)(2,1)}, bf16[1,48,384]{2,1,0:T(8,128)(2,1)S(1)}, u32[]{:S(2)}, u32[]{:S(2)}) collective-permute-start(bf16[1,48,384]{2,1,0:T(8,128)(2,1)} %bitcast.41), channel_id=1, source_target_pairs={{0,16},{8,24},{16,0},{24,8},{32,48},{40,56},{48,32},{56,40},{64,80... | collective-permute-start | bytes 110600 | tf_op jit(solution)/shard_map/ppermute | solution.py:467
  13.1 17.1 %copy-start.9 = (bf16[256,384]{1,0:T(8,128)(2,1)}, bf16[256,384]{1,0:T(8,128)(2,1)S(1)}, u32[]{:S(2)}) copy-start(bf16[256,384]{1,0:T(8,128)(2,1)S(1)} %collective-permute-done.1.refs_3_) | copy-start | bytes 589828
  13.2 0.7 copy-start.10
  13.2 4.3 %copy-start.11 = (bf16[3,16,384]{2,1,0:T(8,128)(2,1)S(1)}, bf16[3,16,384]{2,1,0:T(8,128)(2,1)}, u32[]{:S(2)}) copy-start(bf16[3,16,384]{2,1,0:T(8,128)(2,1)} %get-tuple-element.31) | copy-start | bytes 110596
  13.9 38.9 %all-to-all-start = ((bf16[8,480,256]{2,1,0:T(8,128)(2,1)}), bf16[8,480,256]{2,1,0:T(8,128)(2,1)S(1)}, u32[]{:S(2)}, u32[]{:S(2)}) async-start(bf16[8,480,256]{2,1,0:T(8,128)(2,1)} %get-tuple-element.32), calls=%async_computation | async-start | bytes 3932160 | tf_op jit(solution)/shard_map/all_to_all | solution.py:474
  17.5 8.3 %collective-permute-start.4 = (bf16[2,48,384]{2,1,0:T(8,128)(2,1)S(1)}, bf16[2,48,384]{2,1,0:T(8,128)(2,1)S(1)}, u32[]{:S(2)}, u32[]{:S(2)}) collective-permute-start(bf16[2,48,384]{2,1,0:T(8,128)(2,1)S(1)} %pad_maximum_fusion), channel_id=1, source_target_pairs={{0,32},{8,40},{16,48},{24,56},{32,64},{40,72},{48,80},{56,88},{64,... | collective-permute-start | bytes 221192 | tf_op jit(solution)/shard_map/ppermute | solution.py:478
  19.2 6.7 %collective-permute-start.5 = (bf16[2,48,384]{2,1,0:T(8,128)(2,1)S(1)}, bf16[2,48,384]{2,1,0:T(8,128)(2,1)S(1)}, u32[]{:S(2)}, u32[]{:S(2)}) collective-permute-start(bf16[2,48,384]{2,1,0:T(8,128)(2,1)S(1)} %pad_maximum_fusion), channel_id=1, source_target_pairs={{0,64},{8,72},{16,80},{24,88},{32,96},{40,104},{48,112},{56,120},{... | collective-permute-start | bytes 221192 | tf_op jit(solution)/shard_map/ppermute | solution.py:478
  22.5 3.5 %collective-permute-start.6 = (bf16[2,48,384]{2,1,0:T(8,128)(2,1)S(1)}, bf16[2,48,384]{2,1,0:T(8,128)(2,1)S(1)}, u32[]{:S(2)}, u32[]{:S(2)}) collective-permute-start(bf16[2,48,384]{2,1,0:T(8,128)(2,1)S(1)} %pad_maximum_fusion), channel_id=1, source_target_pairs={{0,96},{8,104},{16,112},{24,120},{32,0},{40,8},{48,16},{56,24},{64... | collective-permute-start | bytes 221192 | tf_op jit(solution)/shard_map/ppermute | solution.py:478
  23.3 21.1 %collective-permute-start.9 = (bf16[256,384]{1,0:T(8,128)(2,1)S(1)}, bf16[256,384]{1,0:T(8,128)(2,1)S(1)}, u32[]{:S(2)}, u32[]{:S(2)}) collective-permute-start(bf16[256,384]{1,0:T(8,128)(2,1)S(1)} %collective-permute-done.1.refs_3_), channel_id=1, source_target_pairs={{0,6},{1,7},{2,0},{3,1},{4,2},{5,3},{6,4},{7,5},{8,14},{9,15},{10,... | collective-permute-start | bytes 589832 | tf_op jit(solution)/shard_map/ppermute | solution.py:449
  26.1 26.7 %copy-start.7 = (bf16[8,48,384]{2,1,0:T(8,128)(2,1)}, bf16[8,48,384]{2,1,0:T(8,128)(2,1)S(1)}, u32[]{:S(2)}) copy-start(bf16[8,48,384]{2,1,0:T(8,128)(2,1)S(1)} %constant_dynamic-update-slice_fusion.refs_2_) | copy-start | bytes 884740
  26.1 26.7 %collective-permute-start.7 = (bf16[8,48,384]{2,1,0:T(8,128)(2,1)S(1)}, bf16[8,48,384]{2,1,0:T(8,128)(2,1)S(1)}, u32[]{:S(2)}, u32[]{:S(2)}) collective-permute-start(bf16[8,48,384]{2,1,0:T(8,128)(2,1)S(1)} %constant_dynamic-update-slice_fusion.refs_2_), channel_id=1, source_target_pairs={{0,8},{8,0},{16,24},{24,16},{32,40},{40,32},{48,56},{56,48},{64,72... | collective-permute-start | bytes 884744 | tf_op jit(solution)/shard_map/ppermute | solution.py:480
  30.2 19.6 %collective-permute-start.8 = (bf16[256,384]{1,0:T(8,128)(2,1)S(1)}, bf16[256,384]{1,0:T(8,128)(2,1)S(1)}, u32[]{:S(2)}, u32[]{:S(2)}) collective-permute-start(bf16[256,384]{1,0:T(8,128)(2,1)S(1)} %collective-permute-done.1.refs_3_), channel_id=1, source_target_pairs={{0,2},{1,3},{2,4},{3,5},{4,6},{5,7},{6,0},{7,1},{8,10},{9,11},{10,... | collective-permute-start | bytes 589832 | tf_op jit(solution)/shard_map/ppermute | solution.py:449
  31.9 20.9 %collective-permute-start.10 = (bf16[256,384]{1,0:T(8,128)(2,1)}, bf16[256,384]{1,0:T(8,128)(2,1)S(1)}, u32[]{:S(2)}, u32[]{:S(2)}) collective-permute-start(bf16[256,384]{1,0:T(8,128)(2,1)} %collective-permute-done.2.refs_4_), channel_id=1, source_target_pairs={{0,2},{1,3},{2,4},{3,5},{4,6},{5,7},{6,0},{7,1},{8,10},{9,11},{10,... | collective-permute-start | bytes 589832 | tf_op jit(solution)/shard_map/ppermute | solution.py:449
  44.3 8.5 %copy-start.2 = (bf16[256,384]{1,0:T(8,128)(2,1)}, bf16[256,384]{1,0:T(8,128)(2,1)S(1)}, u32[]{:S(2)}) copy-start(bf16[256,384]{1,0:T(8,128)(2,1)S(1)} %collective-permute-done.9.refs_6_.refs_7_) | copy-start | bytes 589828
  44.3 8.4 %collective-permute-start.11 = (bf16[256,384]{1,0:T(8,128)(2,1)S(1)}, bf16[256,384]{1,0:T(8,128)(2,1)S(1)}, u32[]{:S(2)}, u32[]{:S(2)}) collective-permute-start(bf16[256,384]{1,0:T(8,128)(2,1)S(1)} %collective-permute-done.9.refs_6_.refs_7_), channel_id=1, source_target_pairs={{0,6},{1,7},{2,0},{3,1},{4,2},{5,3},{6,4},{7,5},{8,14},{9,15},{10,... | collective-permute-start | bytes 589832 | tf_op jit(solution)/shard_map/ppermute | solution.py:449
  49.8 3.0 %copy-start.3 = (bf16[256,384]{1,0:T(8,128)(2,1)}, bf16[256,384]{1,0:T(8,128)(2,1)S(1)}, u32[]{:S(2)}) copy-start(bf16[256,384]{1,0:T(8,128)(2,1)S(1)} %collective-permute-done.8.refs_5_) | copy-start | bytes 589828
  52.7 0.7 copy-start.4
  52.7 0.8 copy-start.8
  52.8 0.8 copy-start.5
  52.8 1.5 %copy-start = (bf16[8,480,256]{2,1,0:T(8,128)(2,1)}, bf16[8,480,256]{2,1,0:T(8,128)(2,1)S(1)}, u32[]{:S(2)}) copy-start(bf16[8,480,256]{2,1,0:T(8,128)(2,1)S(1)} %all-to-all-done.refs_1_) | copy-start | bytes 5898244
  58.5 29.4 %all-to-all-start.1 = ((bf16[8,48,2048]{2,1,0:T(8,128)(2,1)}), bf16[8,48,2048]{2,1,0:T(8,128)(2,1)S(1)}, u32[]{:S(2)}, u32[]{:S(2)}) async-start(bf16[8,48,2048]{2,1,0:T(8,128)(2,1)} %conv_input.1), calls=%async_computation.1 | async-start | bytes 3145728 | tf_op jit(solution)/shard_map/all_to_all | solution.py:512
  88.0 1.1 copy-start.1
  89.1 14.9 %copy-start.12 = (bf16[8,96,384]{2,1,0:T(8,128)(2,1)S(1)}, bf16[8,96,384]{2,1,0:T(8,128)(2,1)}, u32[]{:S(2)}) copy-start(bf16[8,96,384]{2,1,0:T(8,128)(2,1)} %get-tuple-element.51) | copy-start | bytes 1769476
  102.1 6.2 %copy-start.6 = (bf16[8,96,384]{2,1,0:T(8,128)(2,1)S(1)}, bf16[8,96,384]{2,1,0:T(8,128)(2,1)}, u32[]{:S(2)}) copy-start(bf16[8,96,384]{2,1,0:T(8,128)(2,1)} %get-tuple-element.55) | copy-start | bytes 1769476
  102.1 4.0 %collective-permute-start.13 = (bf16[512,768]{1,0:T(8,128)(2,1)}, bf16[512,768]{1,0:T(8,128)(2,1)S(1)}, u32[]{:S(2)}, u32[]{:S(2)}) collective-permute-start(bf16[512,768]{1,0:T(8,128)(2,1)} %get-tuple-element.53), channel_id=1, source_target_pairs={{0,8},{8,0},{16,24},{24,16},{32,40},{40,32},{48,56},{56,48},{64,72... | collective-permute-start | bytes 2359304 | tf_op jit(solution)/shard_map/ppermute | solution.py:601
  104.0 4.3 %collective-permute-start.12 = (bf16[8,96,384]{2,1,0:T(8,128)(2,1)S(1)}, bf16[8,96,384]{2,1,0:T(8,128)(2,1)S(1)}, u32[]{:S(2)}, u32[]{:S(2)}) collective-permute-start(bf16[8,96,384]{2,1,0:T(8,128)(2,1)S(1)} %copy-done.12), channel_id=1, source_target_pairs={{0,8},{8,0},{16,24},{24,16},{32,40},{40,32},{48,56},{56,48},{64,72... | collective-permute-start | bytes 1769480 | tf_op jit(solution)/shard_map/ppermute | solution.py:552
  108.5 12.8 %collective-permute-start.14 = (bf16[4,96,384]{2,1,0:T(8,128)(2,1)S(1)}, bf16[4,96,384]{2,1,0:T(8,128)(2,1)S(1)}, u32[]{:S(2)}, u32[]{:S(2)}) collective-permute-start(bf16[4,96,384]{2,1,0:T(8,128)(2,1)S(1)} %dynamic-slice_convert_fusion), channel_id=1, source_target_pairs={{0,16},{8,24},{16,0},{24,8},{32,48},{40,56},{48,32},{56,40},{64,80... | collective-permute-start | bytes 884744 | tf_op jit(solution)/shard_map/ppermute | solution.py:611
  109.2 27.4 %all-to-all-start.2 = ((bf16[64,8,768]{2,1,0:T(8,128)(2,1)}), bf16[64,8,768]{2,1,0:T(8,128)(2,1)S(1)}, u32[]{:S(2)}, u32[]{:S(2)}) async-start(bf16[64,8,768]{2,1,0:T(8,128)(2,1)} %fusion), calls=%async_computation.2 | async-start | bytes 1572864 | tf_op jit(solution)/shard_map/all_to_all | solution.py:606
  121.4 5.0 %collective-permute-start.15 = (bf16[96,384]{1,0:T(8,128)(2,1)S(1)}, bf16[96,384]{1,0:T(8,128)(2,1)S(1)}, u32[]{:S(2)}, u32[]{:S(2)}) collective-permute-start(bf16[96,384]{1,0:T(8,128)(2,1)S(1)} %get-tuple-element.57), channel_id=1, source_target_pairs={{0,32},{8,40},{16,48},{24,56},{32,64},{40,72},{48,80},{56,88},{64,... | collective-permute-start | bytes 221192 | tf_op jit(solution)/shard_map/ppermute | solution.py:616
  122.5 12.9 %collective-permute-start.16 = (bf16[96,384]{1,0:T(8,128)(2,1)S(1)}, bf16[96,384]{1,0:T(8,128)(2,1)S(1)}, u32[]{:S(2)}, u32[]{:S(2)}) collective-permute-start(bf16[96,384]{1,0:T(8,128)(2,1)S(1)} %get-tuple-element.59), channel_id=1, source_target_pairs={{0,64},{8,72},{16,80},{24,88},{32,96},{40,104},{48,112},{56,120},{... | collective-permute-start | bytes 221192 | tf_op jit(solution)/shard_map/ppermute | solution.py:616
  125.1 10.7 %collective-permute-start.17 = (bf16[96,384]{1,0:T(8,128)(2,1)S(1)}, bf16[96,384]{1,0:T(8,128)(2,1)S(1)}, u32[]{:S(2)}, u32[]{:S(2)}) collective-permute-start(bf16[96,384]{1,0:T(8,128)(2,1)S(1)} %get-tuple-element.58), channel_id=1, source_target_pairs={{0,96},{8,104},{16,112},{24,120},{32,0},{40,8},{48,16},{56,24},{64... | collective-permute-start | bytes 221192 | tf_op jit(solution)/shard_map/ppermute | solution.py:616

commit v4 on v3

--- a/solution.py
+++ b/solution.py
@@ -295,6 +295,18 @@
         keep_att(r).wait()
 
 
+def features_kernel(x_ref, gq_ref, gk_ref, gv_ref, gb_ref, wq_ref, wk_ref, wv_ref, out_ref):
+    cells, chans = x_ref.shape
+    x = nt(eye_of(chans), x_ref[...])
+    recip = lax.rsqrt(jnp.mean(x * x, 0, keepdims=True) + 1e-06)
+    grad_normed = (
+        nn(wq_ref[...], gq_ref[...]) + nn(wk_ref[...], gk_ref[...]) + nn(wv_ref[...], gv_ref[...])
+    )
+    inner = jnp.mean(grad_normed * x, 0, keepdims=True)
+    out = gb_ref[...].astype(F32) + recip * grad_normed - x * (recip * recip * recip) * inner
+    out_ref[...] = nt(eye_of(cells), out.astype(BF16)).astype(BF16)
+
+
 def backward_kernel(
     place_ref,
     x_ref,
@@ -307,12 +319,12 @@
     rows_in,
     top_ref,
     inv_ref,
-    wq_ref,
-    wk_ref,
-    wv_ref,
     wo_order_ref,
     back_ref,
-    out_ref,
+    gq_ref,
+    gk_ref,
+    gv_ref,
+    gb_ref,
     give_ref,
     keep_ref,
     grad_ref,
@@ -385,14 +397,14 @@
     gq = nn(kt_ref[...], sq_ref[...]).astype(BF16)
     gk = nt(qt_ref[...], sk_ref[...]).astype(BF16)
     gv = nt(ga_ref[...], pb_ref[...]).astype(BF16)
+    gq_ref[...] = gq
+    gk_ref[...] = gk
+    gv_ref[...] = gv
     x = nt(eye_of(chans), x_ref[...])
     recip = lax.rsqrt(jnp.mean(x * x, 0, keepdims=True) + 1e-06)
     normed = (x * recip).astype(BF16)
     grad_b = nn(back_ref[...], grad_ref[:, mine])
-    grad_normed = nn(wq_ref[...], gq) + nn(wk_ref[...], gk) + nn(wv_ref[...], gv)
-    inner = jnp.mean(grad_normed * x, 0, keepdims=True)
-    out = grad_b + recip * grad_normed - x * (recip * recip * recip) * inner
-    out_ref[...] = nt(eye_of(cells), out.astype(BF16)).astype(BF16)
+    gb_ref[...] = grad_b.astype(BF16)
     moves[6].wait()
     att = att_ref[:, mine].astype(BF16)
     gq_gv = jnp.concatenate([nt(eye_of(cells), gq), nt(eye_of(cells), gv)], 0).astype(BF16)
@@ -472,13 +484,6 @@
     x_far, x_far_across = along(x_low, 1), along(x_high_across, -1)
     x_all = (x, x_across, x_low, x_low_across, x_high, x_high_across, x_far, x_far_across)
     got = lax.all_to_all(packed, "rows", 0, 0)
-    w_near = jnp.concatenate([w_near, w_across], 0)
-    w_line = [w_near]
-    for back in (1, 2, 3):
-        w_line.append(lax.ppermute(w_near, "dp", [(d, (d + 4 * back) % slots) for d in range(slots)]))
-    w_mine = jnp.concatenate(w_line, 0)
-    w_other = lax.ppermute(w_mine, "dp", [(d, d ^ 1) for d in range(slots)])
-
     wqkv_t, wkv, pick, wo_pick, wo_order = pl.pallas_call(
         prepare_kernel,
         out_shape=(
@@ -494,10 +499,18 @@
         name="prepare",
     )(place, query_weight, key_weight, value_weight, out_weight, order_b)
 
+    w_across, wo_order = lax.optimization_barrier((w_across, wo_order))
+    w_near = jnp.concatenate([w_near, w_across], 0)
+    w_line = [w_near]
+    for back in (1, 2, 3):
+        w_line.append(lax.ppermute(w_near, "dp", [(d, (d + 4 * back) % slots) for d in range(slots)]))
+    w_mine = jnp.concatenate(w_line, 0)
+    w_other = lax.ppermute(w_mine, "dp", [(d, d ^ 1) for d in range(slots)])
+
     grad_sent = pl.pallas_call(
         lambda *refs: conv_input_kernel(width, *refs),
         out_shape=jax.ShapeDtypeStruct((groups, part, total), BF16),
-        in_specs=[pl.BlockSpec(memory_space=pltpu.SMEM)] + whole(3) + anywhere(5),
+        in_specs=[pl.BlockSpec(memory_space=pltpu.SMEM)] + whole(3),
         out_specs=in_hbm(1)[0],
         scratch_shapes=[
             pltpu.VMEM((9 * part, total + 2 * width), F32),
@@ -508,7 +521,8 @@
         ],
         compiler_params=params(56),
         name="conv_input",
-    )(lax.axis_index("dp").reshape(1), got, w_mine, w_other, wo_order, *x_all[3:4], *x_all[5:])
+    )(lax.axis_index("dp").reshape(1), got, w_mine, w_other)
+    grad_sent, x_all = lax.optimization_barrier((grad_sent, x_all))
     grad_all = lax.all_to_all(grad_sent, "rows", 0, 0).reshape(chans, total)
 
     qt, kt, key, value, att, top, inv, conv_give, conv_keep = pl.pallas_call(
@@ -551,15 +565,18 @@
     )(jnp.stack([me, core]), got, *x_all, wqkv_t, wkv, pick, wo_pick)
     conv_taken = lax.ppermute(conv_give, "dp", [(d, d ^ 1) for d in range(slots)])
 
-    feature_grad, give, keep = pl.pallas_call(
+    gq, gk, gv, gb, give, keep = pl.pallas_call(
         backward_kernel,
         out_shape=(
-            jax.ShapeDtypeStruct((cells, chans), BF16),
+            jax.ShapeDtypeStruct((chans, cells), BF16),
+            jax.ShapeDtypeStruct((chans, cells), BF16),
+            jax.ShapeDtypeStruct((chans, cells), BF16),
+            jax.ShapeDtypeStruct((chans, cells), BF16),
             jax.ShapeDtypeStruct((pairs * groups * 8, 2 * chans), BF16),
             jax.ShapeDtypeStruct((pairs * groups * 8, 2 * chans), BF16),
         ),
-        in_specs=[pl.BlockSpec(memory_space=pltpu.SMEM)] + whole(1) + anywhere(7) + whole(7),
-        out_specs=tuple(whole(3)),
+        in_specs=[pl.BlockSpec(memory_space=pltpu.SMEM)] + whole(1) + anywhere(7) + whole(4),
+        out_specs=tuple(whole(6)),
         scratch_shapes=[
             pltpu.VMEM((chans, total), BF16),
             pltpu.VMEM((chans, total), BF16),
@@ -591,9 +608,6 @@
         by_core,
         top,
         inv,
-        query_weight,
-        key_weight,
-        value_weight,
         wo_order,
         back_b,
     )
@@ -602,8 +616,16 @@
     chip = (keep.astype(F32) + taken.astype(F32)).astype(BF16)
     chip = chip.reshape(pairs * groups, 8, 2 * chans)
     same_core = [[d * groups + r for d in range(c, slots, 2) for r in range(groups)] for c in range(2)]
-    conv_taken, chip = lax.optimization_barrier((conv_taken, chip))
+    conv_taken, chip, gb = lax.optimization_barrier((conv_taken, chip, gb))
     got_chip = lax.all_to_all(chip, ("dp", "rows"), 0, 0, axis_index_groups=same_core)
+    feature_grad = pl.pallas_call(
+        features_kernel,
+        out_shape=jax.ShapeDtypeStruct((cells, chans), BF16),
+        in_specs=whole(8),
+        out_specs=pl.BlockSpec(memory_space=pltpu.VMEM),
+        compiler_params=params(56),
+        name="features",
+    )(x, gq, gk, gv, gb, query_weight, key_weight, value_weight)
     me_dp = lax.axis_index("dp")
     z, y = lax.div(me_dp, 4), lax.rem(lax.div(me_dp, 2), 2)
     conv_line = conv_keep.astype(F32) + conv_taken.astype(F32)

time: 139 us -> 135 us (0.971); the launches traced: 137 us -> 135 us
  waiting for transfers between devices: 28.4 us -> 24.9 us
  Pallas kernels: 48.9 us -> 51.3 us
  starting transfers between devices: 51.2 us -> 49.2 us
    ppermute x6, waiting for transfers between devices: 14.2 us -> 10.3 us  [along(): lax.ppermute(block, 'rows', [(r, (r + 2 * step) % groups) for r in range(...]
    pallas_call x1 -> x2, Pallas kernels: 12.9 us -> 15.3 us  [the longest x1 12.1 us: shards(): pl.pallas_call(backward_kernel, out_shape=(jax.ShapeDtypeStruct((chans, c...]
  transfers between devices with their start and end apart: 21 -> 21, of which waited for: 8 -> 8; matrix products, arithmetic and copies ran while one was open for 3% -> 3% of each run, Pallas kernels for 23% -> 29%
where the time goes in v4:
time: 135 us
  Pallas kernels  51.3 us (38%)
  starting transfers between devices  49.2 us (36%)
  waiting for transfers between devices  24.9 us (18%)
  local copies, waits for them, and re-layouts  5.49 us (4%)
  other arithmetic  3.15 us (2%)
    pallas_call x1, Pallas kernels, shards(): pl.pallas_call(lambda *refs: forward_kernel(width, *refs), out_shape=(jax...  25.2 us
    all_to_all x1, starting transfers between devices, shards(): lax.all_to_all(chip, ('dp', 'rows'), 0, 0, axis_index_groups=same_core)  12.3 us
    pallas_call x1, Pallas kernels, shards(): pl.pallas_call(backward_kernel, out_shape=(jax.ShapeDtypeStruct((chans, c...  12.1 us
    ppermute x6, waiting for transfers between devices, along(): lax.ppermute(block, 'rows', [(r, (r + 2 * step) % groups) for r in range(...  10.3 us
    ppermute x6, starting transfers between devices, along(): lax.ppermute(block, 'rows', [(r, (r + 2 * step) % groups) for r in range(...  10.1 us
    ppermute x3, waiting for transfers between devices, shards(): lax.ppermute(sent, 'dp', [(d, (d + 4 * on) % slots) for d in range(slots)])  9.71 us
    ppermute x3, starting transfers between devices, shards(): lax.ppermute(w_near, 'dp', [(d, (d + 4 * back) % slots) for d in range(sl...  5.73 us
    unnamed x32, local copies, waits for them, and re-layouts  4.73 us
  transfers between devices with their start and end apart: 21, of which 8 were waited for; matrix products, arithmetic and copies ran while one was open for 3% of the time, Pallas kernels for 29%

profile of v4, /device:TPU:1, one launch (start us, length us, event | category | flops | bytes accessed | tf_op | source)
XLA Modules:
  0.0 134.9 jit_solution(5683723013009438378)
XLA Ops:
  0.6 3.8 %collective-permute-start.1 = (bf16[256,384]{1,0:T(8,128)(2,1)}, bf16[256,384]{1,0:T(8,128)(2,1)S(1)}, u32[]{:S(2)}, u32[]{:S(2)}) collective-permute-start(bf16[256,384]{1,0:T(8,128)(2,1)} %bitcast.32), channel_id=1, source_target_pairs={{0,1},{1,0},{2,3},{3,2},{4,5},{5,4},{6,7},{7,6},{8,9},{9,8},{10,11... | collective-permute-start | bytes 589832 | tf_op jit(solution)/shard_map/ppermute | solution.py:458
  4.5 1.2 collective-permute-start.2
  5.7 1.5 %collective-permute-start.3 = (bf16[256,384]{1,0:T(8,128)(2,1)}, bf16[256,384]{1,0:T(8,128)(2,1)S(1)}, u32[]{:S(2)}, u32[]{:S(2)}) collective-permute-start(bf16[256,384]{1,0:T(8,128)(2,1)} %bitcast.34), channel_id=1, source_target_pairs={{0,6},{1,7},{2,0},{3,1},{4,2},{5,3},{6,4},{7,5},{8,14},{9,15},{10,... | collective-permute-start | bytes 589832 | tf_op jit(solution)/shard_map/ppermute | solution.py:461
  7.1 3.0 %pack.1 = (bf16[8,480,256]{2,1,0:T(8,128)(2,1)}, bf16[3,16,384]{2,1,0:T(8,128)(2,1)}) custom-call(bf16[256,384]{1,0:T(8,128)(2,1)} %bitcast.40, bf16[2,256,384]{2,1,0:T(8,128)(2,1)} %bitcast.39, bf16[384,384]{1,0:T(8,128)(2,1)} %constant.53.clone.order_ref, bf16[3,27,384]{2,1,0:T(8,128)(2,1)} %conv_ref.1), custom_call_target="tpu_custom_call" | custom-call | tf_op jit(solution)/shard_map/pack/pallas_call | solution.py:466
  10.1 0.4 collective-permute-start
  10.5 2.6 %collective-permute-done = bf16[1,48,384]{2,1,0:T(8,128)(2,1)S(1)} collective-permute-done((bf16[1,48,384]{2,1,0:T(8,128)(2,1)}, bf16[1,48,384]{2,1,0:T(8,128)(2,1)S(1)}, u32[]{:S(2)}, u32[]{:S(2)}) %collective-permute-start) | collective-permute-done | bytes 36896 | tf_op jit(solution)/shard_map/ppermute | solution.py:479
  13.2 0.0 collective-permute-done.3.refs_6_
  13.2 0.7 copy-done.7
  13.9 3.6 %all-to-all-start = ((bf16[8,480,256]{2,1,0:T(8,128)(2,1)}), bf16[8,480,256]{2,1,0:T(8,128)(2,1)S(1)}, u32[]{:S(2)}, u32[]{:S(2)}) async-start(bf16[8,480,256]{2,1,0:T(8,128)(2,1)} %get-tuple-element.47), calls=%async_computation | async-start | bytes 3932160 | tf_op jit(solution)/shard_map/all_to_all | solution.py:486
  17.5 3.5 %prepare.1 = (bf16[1152,384]{1,0:T(8,128)(2,1)}, bf16[384,768]{1,0:T(8,128)(2,1)}, bf16[48,384]{1,0:T(8,128)(2,1)}, bf16[48,384]{1,0:T(8,128)(2,1)}, bf16[384,384]{1,0:T(8,128)(2,1)}) custom-call(s32[1]{0:T(128)} %bitcast.1.me_ref, bf16[384,384]{1,0:T(8,128)(2,1)} %wq_ref.3, bf16[384,384]{1,0:T(8,128)(2,1)} %wk_ref.3, bf16[384,384]{1,0:T(8,128)(2,1)} %wv_ref.3, ...), custom_call_target="tpu_custom_call" | custom-call | tf_op jit(solution)/shard_map/prepare/pallas_call | solution.py:487
  21.0 1.7 %collective-permute-start.4 = (bf16[2,48,384]{2,1,0:T(8,128)(2,1)S(1)}, bf16[2,48,384]{2,1,0:T(8,128)(2,1)S(1)}, u32[]{:S(2)}, u32[]{:S(2)}) collective-permute-start(bf16[2,48,384]{2,1,0:T(8,128)(2,1)S(1)} %pad_maximum_fusion), channel_id=1, source_target_pairs={{0,32},{8,40},{16,48},{24,56},{32,64},{40,72},{48,80},{56,88},{64,... | collective-permute-start | bytes 221192 | tf_op jit(solution)/shard_map/ppermute | solution.py:506
  22.7 3.3 %collective-permute-start.5 = (bf16[2,48,384]{2,1,0:T(8,128)(2,1)S(1)}, bf16[2,48,384]{2,1,0:T(8,128)(2,1)S(1)}, u32[]{:S(2)}, u32[]{:S(2)}) collective-permute-start(bf16[2,48,384]{2,1,0:T(8,128)(2,1)S(1)} %pad_maximum_fusion), channel_id=1, source_target_pairs={{0,64},{8,72},{16,80},{24,88},{32,96},{40,104},{48,112},{56,120},{... | collective-permute-start | bytes 221192 | tf_op jit(solution)/shard_map/ppermute | solution.py:506
  26.0 0.7 collective-permute-start.6
  26.7 2.6 %collective-permute-start.9 = (bf16[256,384]{1,0:T(8,128)(2,1)S(1)}, bf16[256,384]{1,0:T(8,128)(2,1)S(1)}, u32[]{:S(2)}, u32[]{:S(2)}) collective-permute-start(bf16[256,384]{1,0:T(8,128)(2,1)S(1)} %collective-permute-done.1.refs_3_), channel_id=1, source_target_pairs={{0,6},{1,7},{2,0},{3,1},{4,2},{5,3},{6,4},{7,5},{8,14},{9,15},{10,... | collective-permute-start | bytes 589832 | tf_op jit(solution)/shard_map/ppermute | solution.py:461
  29.4 0.1 collective-permute-done.6
  29.5 4.2 %collective-permute-start.7 = (bf16[8,48,384]{2,1,0:T(8,128)(2,1)S(1)}, bf16[8,48,384]{2,1,0:T(8,128)(2,1)S(1)}, u32[]{:S(2)}, u32[]{:S(2)}) collective-permute-start(bf16[8,48,384]{2,1,0:T(8,128)(2,1)S(1)} %constant_dynamic-update-slice_fusion.refs_2_), channel_id=1, source_target_pairs={{0,8},{8,0},{16,24},{24,16},{32,40},{40,32},{48,56},{56,48},{64,72... | collective-permute-start | bytes 884744 | tf_op jit(solution)/shard_map/ppermute | solution.py:508
  33.7 1.6 %collective-permute-start.8 = (bf16[256,384]{1,0:T(8,128)(2,1)S(1)}, bf16[256,384]{1,0:T(8,128)(2,1)S(1)}, u32[]{:S(2)}, u32[]{:S(2)}) collective-permute-start(bf16[256,384]{1,0:T(8,128)(2,1)S(1)} %collective-permute-done.1.refs_3_), channel_id=1, source_target_pairs={{0,2},{1,3},{2,4},{3,5},{4,6},{5,7},{6,0},{7,1},{8,10},{9,11},{10,... | collective-permute-start | bytes 589832 | tf_op jit(solution)/shard_map/ppermute | solution.py:461
  35.4 1.2 collective-permute-start.10
  36.6 7.8 %collective-permute-done.9.refs_7_ = bf16[256,384]{1,0:T(8,128)(2,1)S(1)} collective-permute-done((bf16[256,384]{1,0:T(8,128)(2,1)S(1)}, bf16[256,384]{1,0:T(8,128)(2,1)S(1)}, u32[]{:S(2)}, u32[]{:S(2)}) %collective-permute-start.9) | collective-permute-done | bytes 196640 | tf_op jit(solution)/shard_map/ppermute | solution.py:461
  44.3 2.0 %collective-permute-start.11 = (bf16[256,384]{1,0:T(8,128)(2,1)S(1)}, bf16[256,384]{1,0:T(8,128)(2,1)}, u32[]{:S(2)}, u32[]{:S(2)}) collective-permute-start(bf16[256,384]{1,0:T(8,128)(2,1)S(1)} %collective-permute-done.9.refs_7_), channel_id=1, source_target_pairs={{0,6},{1,7},{2,0},{3,1},{4,2},{5,3},{6,4},{7,5},{8,14},{9,15},{10,... | collective-permute-start | bytes 589832 | tf_op jit(solution)/shard_map/ppermute | solution.py:461
  46.4 0.7 copy-done.4
  47.1 0.7 copy-done
  47.8 4.3 %conv_input.1 = bf16[8,48,2048]{2,1,0:T(8,128)(2,1)} custom-call(s32[1]{0:T(128)} %bitcast.3.refs_0_, bf16[8,480,256]{2,1,0:T(8,128)(2,1)} %copy-done, bf16[8,48,384]{2,1,0:T(8,128)(2,1)} %copy-done.3, bf16[8,48,384]{2,1,0:T(8,128)(2,1)} %copy-done.4), custom_call_target="tpu_custom_call" | custom-call | tf_op jit(solution)/shard_map/conv_input/pallas_call | solution.py:510
  52.1 2.5 %collective-permute-done.10.refs_8_ = bf16[256,384]{1,0:T(8,128)(2,1)S(1)} collective-permute-done((bf16[256,384]{1,0:T(8,128)(2,1)S(1)}, bf16[256,384]{1,0:T(8,128)(2,1)S(1)}, u32[]{:S(2)}, u32[]{:S(2)}) %collective-permute-start.10) | collective-permute-done | bytes 196640 | tf_op jit(solution)/shard_map/ppermute | solution.py:461
  54.6 0.7 copy-done.10
  55.2 3.6 %all-to-all-start.1 = ((bf16[8,48,2048]{2,1,0:T(8,128)(2,1)}), bf16[8,48,2048]{2,1,0:T(8,128)(2,1)S(1)}, u32[]{:S(2)}, u32[]{:S(2)}) async-start(bf16[8,48,2048]{2,1,0:T(8,128)(2,1)} %conv_input.1), calls=%async_computation.1 | async-start | bytes 3145728 | tf_op jit(solution)/shard_map/all_to_all | solution.py:526
  58.8 0.6 pad_add_fusion.refs_0_.place_ref
  59.4 25.2 %forward.1 = (bf16[384,2048]{1,0:T(8,128)(2,1)}, bf16[384,2048]{1,0:T(8,128)(2,1)}, bf16[2048,384]{1,0:T(8,128)(2,1)}, bf16[2048,384]{1,0:T(8,128)(2,1)}, f32[38...) custom-call(s32[2]{0:T(128)} %pad_add_fusion.refs_0_.place_ref, ...), custom_call_target="tpu_custom_call" | custom-call | tf_op jit(solution)/shard_map/forward/pallas_call | solution.py:528
  84.7 1.1 copy-done.1
  85.8 12.1 %backward.1 = (bf16[384,256]{1,0:T(8,128)(2,1)}, bf16[384,256]{1,0:T(8,128)(2,1)}, bf16[384,256]{1,0:T(8,128)(2,1)}, bf16[384,256]{1,0:T(8,128)(2,1)}, bf16[512,...) custom-call(s32[2]{0:T(128)} %pad_add_fusion.refs_0_.place_ref, bf16[256,384]{1,0:T(8,128)(2,1)} %bitcast.36, ...), custom_call_target="tpu_custom_call" | custom-call | tf_op jit(solution)/shard_map/backward/pallas_call | solution.py:568
  98.0 1.1 collective-permute-start.13
  99.1 0.1 collective-permute-start.12
  99.2 2.1 %collective-permute-done.13 = bf16[512,768]{1,0:T(8,128)(2,1)S(1)} collective-permute-done((bf16[512,768]{1,0:T(8,128)(2,1)}, bf16[512,768]{1,0:T(8,128)(2,1)S(1)}, u32[]{:S(2)}, u32[]{:S(2)}) %collective-permute-start.13) | collective-permute-done | bytes 786464 | tf_op jit(solution)/shard_map/ppermute | solution.py:615
  101.3 2.2 %fusion = bf16[64,8,768]{2,1,0:T(8,128)(2,1)} fusion(bf16[512,768]{1,0:T(8,128)(2,1)S(1)} %collective-permute-done.13, bf16[512,768]{1,0:T(8,128)(2,1)} %get-tuple-element.80), kind=kLoop, calls=%fused_computation.3 | loop fusion | flops 1572864 | bytes 2359296 | tf_op jit(solution)/shard_map/reshape | solution.py:617
  103.5 0.1 convert_add_fusion
  103.7 0.7 collective-permute-start.14
  104.5 12.3 %all-to-all-start.2 = ((bf16[64,8,768]{2,1,0:T(8,128)(2,1)}), bf16[64,8,768]{2,1,0:T(8,128)(2,1)S(1)}, u32[]{:S(2)}, u32[]{:S(2)}) async-start(bf16[64,8,768]{2,1,0:T(8,128)(2,1)} %fusion), calls=%async_computation.2 | async-start | bytes 1572864 | tf_op jit(solution)/shard_map/all_to_all | solution.py:620
  116.7 0.1 convert_add_fusion.1
  116.8 2.5 %collective-permute-start.17 = (bf16[96,384]{1,0:T(8,128)(2,1)S(1)}, bf16[96,384]{1,0:T(8,128)(2,1)S(1)}, u32[]{:S(2)}, u32[]{:S(2)}) collective-permute-start(bf16[96,384]{1,0:T(8,128)(2,1)S(1)} %get-tuple-element.88), channel_id=1, source_target_pairs={{0,96},{8,104},{16,112},{24,120},{32,0},{40,8},{48,16},{56,24},{64... | collective-permute-start | bytes 221192 | tf_op jit(solution)/shard_map/ppermute | solution.py:638
  119.3 0.4 collective-permute-start.16
  119.7 0.7 collective-permute-start.15
  120.4 3.2 %features.1 = bf16[256,384]{1,0:T(8,128)(2,1)} custom-call(bf16[256,384]{1,0:T(8,128)(2,1)} %bitcast.37, bf16[384,256]{1,0:T(8,128)(2,1)} %get-tuple-element.76.gq_ref, bf16[384,256]{1,0:T(8,128)(2,1)} %get-tuple-element.77.gk_ref, bf16[384,256]{1,0:T(8,128)(2,1)} %get-tuple-element.78.gv_ref, bf16[384,256]{1,0:T(8,128)(2,1)} %get-tuple-element.83.gb_ref, ...), custom_call_target="tpu_custom_call" | custom-call | tf_op jit(solution)/shard_map/features/pallas_call | solution.py:621
  123.6 3.8 %collective-permute-done.17 = bf16[96,384]{1,0:T(8,128)(2,1)S(1)} collective-permute-done((bf16[96,384]{1,0:T(8,128)(2,1)S(1)}, bf16[96,384]{1,0:T(8,128)(2,1)S(1)}, u32[]{:S(2)}, u32[]{:S(2)}) %collective-permute-start.17) | collective-permute-done | bytes 73760 | tf_op jit(solution)/shard_map/ppermute | solution.py:638
  127.4 0.3 collective-permute-done.16
  127.7 5.6 %collective-permute-done.15 = bf16[96,384]{1,0:T(8,128)(2,1)S(1)} collective-permute-done((bf16[96,384]{1,0:T(8,128)(2,1)S(1)}, bf16[96,384]{1,0:T(8,128)(2,1)S(1)}, u32[]{:S(2)}, u32[]{:S(2)}) %collective-permute-start.15) | collective-permute-done | bytes 73760 | tf_op jit(solution)/shard_map/ppermute | solution.py:638
  133.4 0.8 copy.15
  134.1 0.1 convert_reduce_fusion
  134.3 0.6 reshape.55
  (46 shorter events, 0.3 us)
Async XLA Ops:
  0.6 12.5 %collective-permute-start.1 = (bf16[256,384]{1,0:T(8,128)(2,1)}, bf16[256,384]{1,0:T(8,128)(2,1)S(1)}, u32[]{:S(2)}, u32[]{:S(2)}) collective-permute-start(bf16[256,384]{1,0:T(8,128)(2,1)} %bitcast.32), channel_id=1, source_target_pairs={{0,1},{1,0},{2,3},{3,2},{4,5},{5,4},{6,7},{7,6},{8,9},{9,8},{10,11... | collective-permute-start | bytes 589832 | tf_op jit(solution)/shard_map/ppermute | solution.py:458
  4.5 8.7 %collective-permute-start.2 = (bf16[256,384]{1,0:T(8,128)(2,1)}, bf16[256,384]{1,0:T(8,128)(2,1)S(1)}, u32[]{:S(2)}, u32[]{:S(2)}) collective-permute-start(bf16[256,384]{1,0:T(8,128)(2,1)} %bitcast.33), channel_id=1, source_target_pairs={{0,2},{1,3},{2,4},{3,5},{4,6},{5,7},{6,0},{7,1},{8,10},{9,11},{10,... | collective-permute-start | bytes 589832 | tf_op jit(solution)/shard_map/ppermute | solution.py:461
  5.7 7.5 %collective-permute-start.3 = (bf16[256,384]{1,0:T(8,128)(2,1)}, bf16[256,384]{1,0:T(8,128)(2,1)S(1)}, u32[]{:S(2)}, u32[]{:S(2)}) collective-permute-start(bf16[256,384]{1,0:T(8,128)(2,1)} %bitcast.34), channel_id=1, source_target_pairs={{0,6},{1,7},{2,0},{3,1},{4,2},{5,3},{6,4},{7,5},{8,14},{9,15},{10,... | collective-permute-start | bytes 589832 | tf_op jit(solution)/shard_map/ppermute | solution.py:461
  10.1 3.0 %collective-permute-start = (bf16[1,48,384]{2,1,0:T(8,128)(2,1)}, bf16[1,48,384]{2,1,0:T(8,128)(2,1)S(1)}, u32[]{:S(2)}, u32[]{:S(2)}) collective-permute-start(bf16[1,48,384]{2,1,0:T(8,128)(2,1)} %bitcast.43), channel_id=1, source_target_pairs={{0,16},{8,24},{16,0},{24,8},{32,48},{40,56},{48,32},{56,40},{64,80... | collective-permute-start | bytes 110600 | tf_op jit(solution)/shard_map/ppermute | solution.py:479
  13.1 20.6 %copy-start.5 = (bf16[256,384]{1,0:T(8,128)(2,1)}, bf16[256,384]{1,0:T(8,128)(2,1)S(1)}, u32[]{:S(2)}) copy-start(bf16[256,384]{1,0:T(8,128)(2,1)S(1)} %collective-permute-done.1.refs_3_) | copy-start | bytes 589828
  13.2 22.2 %copy-start.6 = (bf16[256,384]{1,0:T(8,128)(2,1)}, bf16[256,384]{1,0:T(8,128)(2,1)S(1)}, u32[]{:S(2)}) copy-start(bf16[256,384]{1,0:T(8,128)(2,1)S(1)} %collective-permute-done.2.refs_4_) | copy-start | bytes 589828
  13.2 0.7 copy-start.7
  13.2 4.3 %copy-start.11 = (bf16[3,16,384]{2,1,0:T(8,128)(2,1)S(1)}, bf16[3,16,384]{2,1,0:T(8,128)(2,1)}, u32[]{:S(2)}) copy-start(bf16[3,16,384]{2,1,0:T(8,128)(2,1)} %get-tuple-element.46) | copy-start | bytes 110596
  13.9 32.5 %all-to-all-start = ((bf16[8,480,256]{2,1,0:T(8,128)(2,1)}), bf16[8,480,256]{2,1,0:T(8,128)(2,1)S(1)}, u32[]{:S(2)}, u32[]{:S(2)}) async-start(bf16[8,480,256]{2,1,0:T(8,128)(2,1)} %get-tuple-element.47), calls=%async_computation | async-start | bytes 3932160 | tf_op jit(solution)/shard_map/all_to_all | solution.py:486
  21.0 8.3 %collective-permute-start.4 = (bf16[2,48,384]{2,1,0:T(8,128)(2,1)S(1)}, bf16[2,48,384]{2,1,0:T(8,128)(2,1)S(1)}, u32[]{:S(2)}, u32[]{:S(2)}) collective-permute-start(bf16[2,48,384]{2,1,0:T(8,128)(2,1)S(1)} %pad_maximum_fusion), channel_id=1, source_target_pairs={{0,32},{8,40},{16,48},{24,56},{32,64},{40,72},{48,80},{56,88},{64,... | collective-permute-start | bytes 221192 | tf_op jit(solution)/shard_map/ppermute | solution.py:506
  22.7 6.7 %collective-permute-start.5 = (bf16[2,48,384]{2,1,0:T(8,128)(2,1)S(1)}, bf16[2,48,384]{2,1,0:T(8,128)(2,1)S(1)}, u32[]{:S(2)}, u32[]{:S(2)}) collective-permute-start(bf16[2,48,384]{2,1,0:T(8,128)(2,1)S(1)} %pad_maximum_fusion), channel_id=1, source_target_pairs={{0,64},{8,72},{16,80},{24,88},{32,96},{40,104},{48,112},{56,120},{... | collective-permute-start | bytes 221192 | tf_op jit(solution)/shard_map/ppermute | solution.py:506
  26.0 3.5 %collective-permute-start.6 = (bf16[2,48,384]{2,1,0:T(8,128)(2,1)S(1)}, bf16[2,48,384]{2,1,0:T(8,128)(2,1)S(1)}, u32[]{:S(2)}, u32[]{:S(2)}) collective-permute-start(bf16[2,48,384]{2,1,0:T(8,128)(2,1)S(1)} %pad_maximum_fusion), channel_id=1, source_target_pairs={{0,96},{8,104},{16,112},{24,120},{32,0},{40,8},{48,16},{56,24},{64... | collective-permute-start | bytes 221192 | tf_op jit(solution)/shard_map/ppermute | solution.py:506
  26.7 17.6 %collective-permute-start.9 = (bf16[256,384]{1,0:T(8,128)(2,1)S(1)}, bf16[256,384]{1,0:T(8,128)(2,1)S(1)}, u32[]{:S(2)}, u32[]{:S(2)}) collective-permute-start(bf16[256,384]{1,0:T(8,128)(2,1)S(1)} %collective-permute-done.1.refs_3_), channel_id=1, source_target_pairs={{0,6},{1,7},{2,0},{3,1},{4,2},{5,3},{6,4},{7,5},{8,14},{9,15},{10,... | collective-permute-start | bytes 589832 | tf_op jit(solution)/shard_map/ppermute | solution.py:461
  29.5 16.8 %copy-start.3 = (bf16[8,48,384]{2,1,0:T(8,128)(2,1)}, bf16[8,48,384]{2,1,0:T(8,128)(2,1)S(1)}, u32[]{:S(2)}) copy-start(bf16[8,48,384]{2,1,0:T(8,128)(2,1)S(1)} %constant_dynamic-update-slice_fusion.refs_2_) | copy-start | bytes 884740
  29.5 16.8 %collective-permute-start.7 = (bf16[8,48,384]{2,1,0:T(8,128)(2,1)S(1)}, bf16[8,48,384]{2,1,0:T(8,128)(2,1)S(1)}, u32[]{:S(2)}, u32[]{:S(2)}) collective-permute-start(bf16[8,48,384]{2,1,0:T(8,128)(2,1)S(1)} %constant_dynamic-update-slice_fusion.refs_2_), channel_id=1, source_target_pairs={{0,8},{8,0},{16,24},{24,16},{32,40},{40,32},{48,56},{56,48},{64,72... | collective-permute-start | bytes 884744 | tf_op jit(solution)/shard_map/ppermute | solution.py:508
  33.7 18.3 %collective-permute-start.8 = (bf16[256,384]{1,0:T(8,128)(2,1)S(1)}, bf16[256,384]{1,0:T(8,128)(2,1)S(1)}, u32[]{:S(2)}, u32[]{:S(2)}) collective-permute-start(bf16[256,384]{1,0:T(8,128)(2,1)S(1)} %collective-permute-done.1.refs_3_), channel_id=1, source_target_pairs={{0,2},{1,3},{2,4},{3,5},{4,6},{5,7},{6,0},{7,1},{8,10},{9,11},{10,... | collective-permute-start | bytes 589832 | tf_op jit(solution)/shard_map/ppermute | solution.py:461
  35.4 19.2 %collective-permute-start.10 = (bf16[256,384]{1,0:T(8,128)(2,1)S(1)}, bf16[256,384]{1,0:T(8,128)(2,1)S(1)}, u32[]{:S(2)}, u32[]{:S(2)}) collective-permute-start(bf16[256,384]{1,0:T(8,128)(2,1)S(1)} %collective-permute-done.2.refs_4_), channel_id=1, source_target_pairs={{0,2},{1,3},{2,4},{3,5},{4,6},{5,7},{6,0},{7,1},{8,10},{9,11},{10,... | collective-permute-start | bytes 589832 | tf_op jit(solution)/shard_map/ppermute | solution.py:461
  44.3 15.1 %copy-start.8 = (bf16[256,384]{1,0:T(8,128)(2,1)}, bf16[256,384]{1,0:T(8,128)(2,1)S(1)}, u32[]{:S(2)}) copy-start(bf16[256,384]{1,0:T(8,128)(2,1)S(1)} %collective-permute-done.9.refs_7_) | copy-start | bytes 589828
  44.3 10.2 %collective-permute-start.11 = (bf16[256,384]{1,0:T(8,128)(2,1)S(1)}, bf16[256,384]{1,0:T(8,128)(2,1)}, u32[]{:S(2)}, u32[]{:S(2)}) collective-permute-start(bf16[256,384]{1,0:T(8,128)(2,1)S(1)} %collective-permute-done.9.refs_7_), channel_id=1, source_target_pairs={{0,6},{1,7},{2,0},{3,1},{4,2},{5,3},{6,4},{7,5},{8,14},{9,15},{10,... | collective-permute-start | bytes 589832 | tf_op jit(solution)/shard_map/ppermute | solution.py:461
  46.3 0.7 copy-start.4
  46.3 1.4 %copy-start = (bf16[8,480,256]{2,1,0:T(8,128)(2,1)}, bf16[8,480,256]{2,1,0:T(8,128)(2,1)S(1)}, u32[]{:S(2)}) copy-start(bf16[8,480,256]{2,1,0:T(8,128)(2,1)S(1)} %all-to-all-done.refs_1_) | copy-start | bytes 5898244
  52.1 2.5 %copy-start.9 = (bf16[256,384]{1,0:T(8,128)(2,1)}, bf16[256,384]{1,0:T(8,128)(2,1)S(1)}, u32[]{:S(2)}) copy-start(bf16[256,384]{1,0:T(8,128)(2,1)S(1)} %collective-permute-done.8.refs_5_) | copy-start | bytes 589828
  54.6 0.7 copy-start.10
  55.2 29.4 %all-to-all-start.1 = ((bf16[8,48,2048]{2,1,0:T(8,128)(2,1)}), bf16[8,48,2048]{2,1,0:T(8,128)(2,1)S(1)}, u32[]{:S(2)}, u32[]{:S(2)}) async-start(bf16[8,48,2048]{2,1,0:T(8,128)(2,1)} %conv_input.1), calls=%async_computation.1 | async-start | bytes 3145728 | tf_op jit(solution)/shard_map/all_to_all | solution.py:526
  84.7 1.1 copy-start.1
  85.8 13.3 %copy-start.12 = (bf16[8,96,384]{2,1,0:T(8,128)(2,1)S(1)}, bf16[8,96,384]{2,1,0:T(8,128)(2,1)}, u32[]{:S(2)}) copy-start(bf16[8,96,384]{2,1,0:T(8,128)(2,1)} %get-tuple-element.79) | copy-start | bytes 1769476
  98.0 5.6 %copy-start.2 = (bf16[8,96,384]{2,1,0:T(8,128)(2,1)S(1)}, bf16[8,96,384]{2,1,0:T(8,128)(2,1)}, u32[]{:S(2)}) copy-start(bf16[8,96,384]{2,1,0:T(8,128)(2,1)} %get-tuple-element.85) | copy-start | bytes 1769476
  98.0 3.4 %collective-permute-start.13 = (bf16[512,768]{1,0:T(8,128)(2,1)}, bf16[512,768]{1,0:T(8,128)(2,1)S(1)}, u32[]{:S(2)}, u32[]{:S(2)}) collective-permute-start(bf16[512,768]{1,0:T(8,128)(2,1)} %get-tuple-element.81), channel_id=1, source_target_pairs={{0,8},{8,0},{16,24},{24,16},{32,40},{40,32},{48,56},{56,48},{64,72... | collective-permute-start | bytes 2359304 | tf_op jit(solution)/shard_map/ppermute | solution.py:615
  99.1 4.4 %collective-permute-start.12 = (bf16[8,96,384]{2,1,0:T(8,128)(2,1)S(1)}, bf16[8,96,384]{2,1,0:T(8,128)(2,1)S(1)}, u32[]{:S(2)}, u32[]{:S(2)}) collective-permute-start(bf16[8,96,384]{2,1,0:T(8,128)(2,1)S(1)} %copy-done.12), channel_id=1, source_target_pairs={{0,8},{8,0},{16,24},{24,16},{32,40},{40,32},{48,56},{56,48},{64,72... | collective-permute-start | bytes 1769480 | tf_op jit(solution)/shard_map/ppermute | solution.py:566
  103.7 13.0 %collective-permute-start.14 = (bf16[4,96,384]{2,1,0:T(8,128)(2,1)S(1)}, bf16[4,96,384]{2,1,0:T(8,128)(2,1)S(1)}, u32[]{:S(2)}, u32[]{:S(2)}) collective-permute-start(bf16[4,96,384]{2,1,0:T(8,128)(2,1)S(1)} %dynamic-slice_convert_fusion), channel_id=1, source_target_pairs={{0,16},{8,24},{16,0},{24,8},{32,48},{40,56},{48,32},{56,40},{64,80... | collective-permute-start | bytes 884744 | tf_op jit(solution)/shard_map/ppermute | solution.py:633
  104.5 29.7 %all-to-all-start.2 = ((bf16[64,8,768]{2,1,0:T(8,128)(2,1)}), bf16[64,8,768]{2,1,0:T(8,128)(2,1)S(1)}, u32[]{:S(2)}, u32[]{:S(2)}) async-start(bf16[64,8,768]{2,1,0:T(8,128)(2,1)} %fusion), calls=%async_computation.2 | async-start | bytes 1572864 | tf_op jit(solution)/shard_map/all_to_all | solution.py:620
  116.8 10.5 %collective-permute-start.17 = (bf16[96,384]{1,0:T(8,128)(2,1)S(1)}, bf16[96,384]{1,0:T(8,128)(2,1)S(1)}, u32[]{:S(2)}, u32[]{:S(2)}) collective-permute-start(bf16[96,384]{1,0:T(8,128)(2,1)S(1)} %get-tuple-element.88), channel_id=1, source_target_pairs={{0,96},{8,104},{16,112},{24,120},{32,0},{40,8},{48,16},{56,24},{64... | collective-permute-start | bytes 221192 | tf_op jit(solution)/shard_map/ppermute | solution.py:638
  119.3 8.3 %collective-permute-start.16 = (bf16[96,384]{1,0:T(8,128)(2,1)S(1)}, bf16[96,384]{1,0:T(8,128)(2,1)S(1)}, u32[]{:S(2)}, u32[]{:S(2)}) collective-permute-start(bf16[96,384]{1,0:T(8,128)(2,1)S(1)} %get-tuple-element.89), channel_id=1, source_target_pairs={{0,64},{8,72},{16,80},{24,88},{32,96},{40,104},{48,112},{56,120},{... | collective-permute-start | bytes 221192 | tf_op jit(solution)/shard_map/ppermute | solution.py:638
  119.7 13.6 %collective-permute-start.15 = (bf16[96,384]{1,0:T(8,128)(2,1)S(1)}, bf16[96,384]{1,0:T(8,128)(2,1)S(1)}, u32[]{:S(2)}, u32[]{:S(2)}) collective-permute-start(bf16[96,384]{1,0:T(8,128)(2,1)S(1)} %get-tuple-element.87), channel_id=1, source_target_pairs={{0,32},{8,40},{16,48},{24,56},{32,64},{40,72},{48,80},{56,88},{64,... | collective-permute-start | bytes 221192 | tf_op jit(solution)/shard_map/ppermute | solution.py:638

commit v5 on v4

--- a/solution.py
+++ b/solution.py
@@ -316,7 +316,6 @@
     key_in,
     value_in,
     att_in,
-    rows_in,
     top_ref,
     inv_ref,
     wo_order_ref,
@@ -333,7 +332,8 @@
     key_ref,
     value_ref,
     att_ref,
-    rows_ref,
+    term_ref,
+    line_ref,
     sems,
     ga_ref,
     tot_ref,
@@ -352,7 +352,6 @@
         (att_in, att_ref),
         (value_in, value_ref),
         (kt_in, kt_ref),
-        (rows_in, rows_ref),
     ]
     moves = [pltpu.make_async_copy(a, b, sems.at[n]) for n, (a, b) in enumerate(moves)]
     for copy in moves:
@@ -405,18 +404,28 @@
     normed = (x * recip).astype(BF16)
     grad_b = nn(back_ref[...], grad_ref[:, mine])
     gb_ref[...] = grad_b.astype(BF16)
-    moves[6].wait()
     att = att_ref[:, mine].astype(BF16)
-    gq_gv = jnp.concatenate([nt(eye_of(cells), gq), nt(eye_of(cells), gv)], 0).astype(BF16)
-    gk_gb = jnp.concatenate(
-        [nt(eye_of(cells), gk), nt(eye_of(cells), grad_b.astype(BF16))], 0
-    ).astype(BF16)
+    lane_tiles = chans // 128
+    pairs = ((normed, gq), (normed, gk), (normed, gv), (att, grad_b.astype(BF16)))
+    for n, (left, right) in enumerate(pairs):
+        term = nt(left, right)
+        for c in range(lane_tiles):
+            term_ref[n * lane_tiles + c] = term[:, c * 128 : (c + 1) * 128]
+    line_ref[...] = jnp.zeros(line_ref.shape, F32)
+    groups = total // cells
+    places = give_ref.shape[0] // (8 * groups)
+    per = chans // (2 * places * groups)
     for half, to_ref in ((1 - core, give_ref), (core, keep_ref)):
-        upper = nn(rows_ref[half, 0], normed).astype(BF16)
-        lower = nn(rows_ref[half, 1], normed).astype(BF16)
-        lower_att = nn(rows_ref[half, 1], att).astype(BF16)
-        to_ref[:, 0:chans] = nn(jnp.concatenate([upper, lower], 1), gq_gv).astype(BF16)
-        to_ref[:, chans:] = nn(jnp.concatenate([upper, lower_att], 1), gk_gb).astype(BF16)
+        for place in range(places):
+            for k in range(per):
+                first = (2 * place + half) * per * groups + k
+                for n in range(4):
+                    to = pl.ds(place * groups * 8 + (n // 2) * 4 + k, groups, stride=8)
+                    for c in range(lane_tiles):
+                        rows = term_ref[n * lane_tiles + c, pl.ds(first, groups, stride=per), :]
+                        line_ref[(n % 2) * lane_tiles + c, to, :] = rows
+        for c in range(2 * lane_tiles):
+            to_ref[:, c * 128 : (c + 1) * 128] = line_ref[c].astype(BF16)
 
 
 def shards(
@@ -439,16 +448,6 @@
     back_b = jnp.asarray(order.T, BF16)
 
     pairs = slots // 2
-    by_core = np.zeros((2, 2, pairs * groups * 8, chans), np.float32)
-    for core in range(2):
-        for pair in range(pairs):
-            for r in range(groups):
-                for k in range(per):
-                    row = (pair * groups + r) * 8 + k
-                    chan = (2 * pair + core) * per * groups + per * r + k
-                    by_core[core, 0, row, chan] = 1.0
-                    by_core[core, 1, row + 4, chan] = 1.0
-    by_core = jnp.asarray(by_core, BF16)
     core = lax.rem(lax.axis_index("dp"), 2)
 
     x = features.reshape(cells, chans)
@@ -575,7 +574,7 @@
             jax.ShapeDtypeStruct((pairs * groups * 8, 2 * chans), BF16),
             jax.ShapeDtypeStruct((pairs * groups * 8, 2 * chans), BF16),
         ),
-        in_specs=[pl.BlockSpec(memory_space=pltpu.SMEM)] + whole(1) + anywhere(7) + whole(4),
+        in_specs=[pl.BlockSpec(memory_space=pltpu.SMEM)] + whole(1) + anywhere(6) + whole(4),
         out_specs=tuple(whole(6)),
         scratch_shapes=[
             pltpu.VMEM((chans, total), BF16),
@@ -584,8 +583,9 @@
             pltpu.VMEM((total, chans), BF16),
             pltpu.VMEM((total, chans), BF16),
             pltpu.VMEM((chans, total), F32),
-            pltpu.VMEM(by_core.shape, BF16),
-            pltpu.SemaphoreType.DMA((7,)),
+            pltpu.VMEM((4 * chans // 128, chans, 128), F32),
+            pltpu.VMEM((2 * chans // 128, pairs * groups * 8, 128), F32),
+            pltpu.SemaphoreType.DMA((6,)),
             pltpu.VMEM((chans, total), BF16),
             pltpu.VMEM((1, total), F32),
             pltpu.VMEM((total, cells), BF16),
@@ -605,7 +605,6 @@
         key,
         value,
         att,
-        by_core,
         top,
         inv,
         wo_order,

time: 135 us -> 133 us (0.985)
  Pallas kernels: 51.3 us -> 49.9 us
    pallas_call x1, Pallas kernels: 12.1 us -> 10.7 us  [shards(): pl.pallas_call(backward_kernel, out_shape=(jax.ShapeDtypeStruct((chans, c...]
  transfers between devices with their start and end apart: 21 -> 21, of which waited for: 8 -> 8; matrix products, arithmetic and copies ran while one was open for 3% -> 3% of each run, Pallas kernels for 29% -> 30%
where the time goes in v5:
time: 133 us
  Pallas kernels  49.9 us (38%)
  starting transfers between devices  48.9 us (37%)
  waiting for transfers between devices  24.9 us (19%)
  local copies, waits for them, and re-layouts  4.85 us (4%)
  other arithmetic  3.15 us (2%)
    pallas_call x1, Pallas kernels, shards(): pl.pallas_call(lambda *refs: forward_kernel(width, *refs), out_shape=(jax...  25.2 us
    all_to_all x1, starting transfers between devices, shards(): lax.all_to_all(chip, ('dp', 'rows'), 0, 0, axis_index_groups=same_core)  12 us
    pallas_call x1, Pallas kernels, shards(): pl.pallas_call(backward_kernel, out_shape=(jax.ShapeDtypeStruct((chans, c...  10.7 us
    ppermute x6, waiting for transfers between devices, along(): lax.ppermute(block, 'rows', [(r, (r + 2 * step) % groups) for r in range(...  10.3 us
    ppermute x6, starting transfers between devices, along(): lax.ppermute(block, 'rows', [(r, (r + 2 * step) % groups) for r in range(...  10.1 us
    ppermute x3, waiting for transfers between devices, shards(): lax.ppermute(sent, 'dp', [(d, (d + 4 * on) % slots) for d in range(slots)])  9.71 us
    ppermute x3, starting transfers between devices, shards(): lax.ppermute(w_near, 'dp', [(d, (d + 4 * back) % slots) for d in range(sl...  5.73 us
    pallas_call x1, Pallas kernels, shards(): pl.pallas_call(lambda *refs: conv_input_kernel(width, *refs), out_shape=j...  4.29 us
  transfers between devices with their start and end apart: 21, of which 8 were waited for; matrix products, arithmetic and copies ran while one was open for 3% of the time, Pallas kernels for 30%

profile of v5, /device:TPU:1, one launch (start us, length us, event | category | flops | bytes accessed | tf_op | source)
XLA Modules:
  0.0 132.6 jit_solution(12135598092343307084)
XLA Ops:
  0.6 3.8 %collective-permute-start.1 = (bf16[256,384]{1,0:T(8,128)(2,1)}, bf16[256,384]{1,0:T(8,128)(2,1)S(1)}, u32[]{:S(2)}, u32[]{:S(2)}) collective-permute-start(bf16[256,384]{1,0:T(8,128)(2,1)} %bitcast.32), channel_id=1, source_target_pairs={{0,1},{1,0},{2,3},{3,2},{4,5},{5,4},{6,7},{7,6},{8,9},{9,8},{10,11... | collective-permute-start | bytes 589832 | tf_op jit(solution)/shard_map/ppermute | solution.py:457
  4.5 1.2 collective-permute-start.2
  5.7 1.5 %collective-permute-start.3 = (bf16[256,384]{1,0:T(8,128)(2,1)}, bf16[256,384]{1,0:T(8,128)(2,1)S(1)}, u32[]{:S(2)}, u32[]{:S(2)}) collective-permute-start(bf16[256,384]{1,0:T(8,128)(2,1)} %bitcast.34), channel_id=1, source_target_pairs={{0,6},{1,7},{2,0},{3,1},{4,2},{5,3},{6,4},{7,5},{8,14},{9,15},{10,... | collective-permute-start | bytes 589832 | tf_op jit(solution)/shard_map/ppermute | solution.py:460
  7.1 3.0 %pack.1 = (bf16[8,480,256]{2,1,0:T(8,128)(2,1)}, bf16[3,16,384]{2,1,0:T(8,128)(2,1)}) custom-call(bf16[256,384]{1,0:T(8,128)(2,1)} %bitcast.40, bf16[2,256,384]{2,1,0:T(8,128)(2,1)} %bitcast.39, bf16[384,384]{1,0:T(8,128)(2,1)} %constant.51.clone.order_ref, bf16[3,27,384]{2,1,0:T(8,128)(2,1)} %conv_ref.1), custom_call_target="tpu_custom_call" | custom-call | tf_op jit(solution)/shard_map/pack/pallas_call | solution.py:465
  10.1 0.4 collective-permute-start
  10.5 2.6 %collective-permute-done = bf16[1,48,384]{2,1,0:T(8,128)(2,1)S(1)} collective-permute-done((bf16[1,48,384]{2,1,0:T(8,128)(2,1)}, bf16[1,48,384]{2,1,0:T(8,128)(2,1)S(1)}, u32[]{:S(2)}, u32[]{:S(2)}) %collective-permute-start) | collective-permute-done | bytes 36896 | tf_op jit(solution)/shard_map/ppermute | solution.py:478
  13.2 0.0 collective-permute-done.3.refs_6_
  13.2 0.7 copy-done.7
  13.9 3.6 %all-to-all-start = ((bf16[8,480,256]{2,1,0:T(8,128)(2,1)}), bf16[8,480,256]{2,1,0:T(8,128)(2,1)S(1)}, u32[]{:S(2)}, u32[]{:S(2)}) async-start(bf16[8,480,256]{2,1,0:T(8,128)(2,1)} %get-tuple-element.47), calls=%async_computation | async-start | bytes 3932160 | tf_op jit(solution)/shard_map/all_to_all | solution.py:485
  17.5 3.5 %prepare.1 = (bf16[1152,384]{1,0:T(8,128)(2,1)}, bf16[384,768]{1,0:T(8,128)(2,1)}, bf16[48,384]{1,0:T(8,128)(2,1)}, bf16[48,384]{1,0:T(8,128)(2,1)}, bf16[384,384]{1,0:T(8,128)(2,1)}) custom-call(s32[1]{0:T(128)} %bitcast.1.me_ref, bf16[384,384]{1,0:T(8,128)(2,1)} %wq_ref.3, bf16[384,384]{1,0:T(8,128)(2,1)} %wk_ref.3, bf16[384,384]{1,0:T(8,128)(2,1)} %wv_ref.3, ...), custom_call_target="tpu_custom_call" | custom-call | tf_op jit(solution)/shard_map/prepare/pallas_call | solution.py:486
  21.0 1.7 %collective-permute-start.4 = (bf16[2,48,384]{2,1,0:T(8,128)(2,1)S(1)}, bf16[2,48,384]{2,1,0:T(8,128)(2,1)S(1)}, u32[]{:S(2)}, u32[]{:S(2)}) collective-permute-start(bf16[2,48,384]{2,1,0:T(8,128)(2,1)S(1)} %pad_maximum_fusion), channel_id=1, source_target_pairs={{0,32},{8,40},{16,48},{24,56},{32,64},{40,72},{48,80},{56,88},{64,... | collective-permute-start | bytes 221192 | tf_op jit(solution)/shard_map/ppermute | solution.py:505
  22.7 3.3 %collective-permute-start.5 = (bf16[2,48,384]{2,1,0:T(8,128)(2,1)S(1)}, bf16[2,48,384]{2,1,0:T(8,128)(2,1)S(1)}, u32[]{:S(2)}, u32[]{:S(2)}) collective-permute-start(bf16[2,48,384]{2,1,0:T(8,128)(2,1)S(1)} %pad_maximum_fusion), channel_id=1, source_target_pairs={{0,64},{8,72},{16,80},{24,88},{32,96},{40,104},{48,112},{56,120},{... | collective-permute-start | bytes 221192 | tf_op jit(solution)/shard_map/ppermute | solution.py:505
  26.0 0.7 collective-permute-start.6
  26.8 2.6 %collective-permute-start.9 = (bf16[256,384]{1,0:T(8,128)(2,1)S(1)}, bf16[256,384]{1,0:T(8,128)(2,1)S(1)}, u32[]{:S(2)}, u32[]{:S(2)}) collective-permute-start(bf16[256,384]{1,0:T(8,128)(2,1)S(1)} %collective-permute-done.1.refs_3_), channel_id=1, source_target_pairs={{0,6},{1,7},{2,0},{3,1},{4,2},{5,3},{6,4},{7,5},{8,14},{9,15},{10,... | collective-permute-start | bytes 589832 | tf_op jit(solution)/shard_map/ppermute | solution.py:460
  29.4 0.0 collective-permute-done.4
  29.4 0.1 collective-permute-done.6
  29.6 4.2 %collective-permute-start.7 = (bf16[8,48,384]{2,1,0:T(8,128)(2,1)S(1)}, bf16[8,48,384]{2,1,0:T(8,128)(2,1)S(1)}, u32[]{:S(2)}, u32[]{:S(2)}) collective-permute-start(bf16[8,48,384]{2,1,0:T(8,128)(2,1)S(1)} %constant_dynamic-update-slice_fusion.refs_2_), channel_id=1, source_target_pairs={{0,8},{8,0},{16,24},{24,16},{32,40},{40,32},{48,56},{56,48},{64,72... | collective-permute-start | bytes 884744 | tf_op jit(solution)/shard_map/ppermute | solution.py:507
  33.7 1.6 %collective-permute-start.8 = (bf16[256,384]{1,0:T(8,128)(2,1)S(1)}, bf16[256,384]{1,0:T(8,128)(2,1)S(1)}, u32[]{:S(2)}, u32[]{:S(2)}) collective-permute-start(bf16[256,384]{1,0:T(8,128)(2,1)S(1)} %collective-permute-done.1.refs_3_), channel_id=1, source_target_pairs={{0,2},{1,3},{2,4},{3,5},{4,6},{5,7},{6,0},{7,1},{8,10},{9,11},{10,... | collective-permute-start | bytes 589832 | tf_op jit(solution)/shard_map/ppermute | solution.py:460
  35.4 1.2 collective-permute-start.10
  36.6 7.8 %collective-permute-done.9.refs_7_ = bf16[256,384]{1,0:T(8,128)(2,1)S(1)} collective-permute-done((bf16[256,384]{1,0:T(8,128)(2,1)S(1)}, bf16[256,384]{1,0:T(8,128)(2,1)S(1)}, u32[]{:S(2)}, u32[]{:S(2)}) %collective-permute-start.9) | collective-permute-done | bytes 196640 | tf_op jit(solution)/shard_map/ppermute | solution.py:460
  44.4 2.0 %collective-permute-start.11 = (bf16[256,384]{1,0:T(8,128)(2,1)S(1)}, bf16[256,384]{1,0:T(8,128)(2,1)}, u32[]{:S(2)}, u32[]{:S(2)}) collective-permute-start(bf16[256,384]{1,0:T(8,128)(2,1)S(1)} %collective-permute-done.9.refs_7_), channel_id=1, source_target_pairs={{0,6},{1,7},{2,0},{3,1},{4,2},{5,3},{6,4},{7,5},{8,14},{9,15},{10,... | collective-permute-start | bytes 589832 | tf_op jit(solution)/shard_map/ppermute | solution.py:460
  46.4 0.7 copy-done.4
  47.1 0.7 copy-done
  47.8 4.3 %conv_input.1 = bf16[8,48,2048]{2,1,0:T(8,128)(2,1)} custom-call(s32[1]{0:T(128)} %bitcast.3.refs_0_, bf16[8,480,256]{2,1,0:T(8,128)(2,1)} %copy-done, bf16[8,48,384]{2,1,0:T(8,128)(2,1)} %copy-done.3, bf16[8,48,384]{2,1,0:T(8,128)(2,1)} %copy-done.4), custom_call_target="tpu_custom_call" | custom-call | tf_op jit(solution)/shard_map/conv_input/pallas_call | solution.py:509
  52.1 2.5 %collective-permute-done.10.refs_8_ = bf16[256,384]{1,0:T(8,128)(2,1)S(1)} collective-permute-done((bf16[256,384]{1,0:T(8,128)(2,1)S(1)}, bf16[256,384]{1,0:T(8,128)(2,1)S(1)}, u32[]{:S(2)}, u32[]{:S(2)}) %collective-permute-start.10) | collective-permute-done | bytes 196640 | tf_op jit(solution)/shard_map/ppermute | solution.py:460
  54.6 3.6 %all-to-all-start.1 = ((bf16[8,48,2048]{2,1,0:T(8,128)(2,1)}), bf16[8,48,2048]{2,1,0:T(8,128)(2,1)S(1)}, u32[]{:S(2)}, u32[]{:S(2)}) async-start(bf16[8,48,2048]{2,1,0:T(8,128)(2,1)} %conv_input.1), calls=%async_computation.1 | async-start | bytes 3145728 | tf_op jit(solution)/shard_map/all_to_all | solution.py:525
  58.2 0.6 pad_add_fusion.refs_0_.place_ref
  58.8 25.2 %forward.1 = (bf16[384,2048]{1,0:T(8,128)(2,1)}, bf16[384,2048]{1,0:T(8,128)(2,1)}, bf16[2048,384]{1,0:T(8,128)(2,1)}, bf16[2048,384]{1,0:T(8,128)(2,1)}, f32[38...) custom-call(s32[2]{0:T(128)} %pad_add_fusion.refs_0_.place_ref, ...), custom_call_target="tpu_custom_call" | custom-call | tf_op jit(solution)/shard_map/forward/pallas_call | solution.py:527
  84.1 1.1 copy-done.1
  85.2 10.7 %backward.1 = (bf16[384,256]{1,0:T(8,128)(2,1)}, bf16[384,256]{1,0:T(8,128)(2,1)}, bf16[384,256]{1,0:T(8,128)(2,1)}, bf16[384,256]{1,0:T(8,128)(2,1)}, bf16[512,...) custom-call(s32[2]{0:T(128)} %pad_add_fusion.refs_0_.place_ref, bf16[256,384]{1,0:T(8,128)(2,1)} %bitcast.36, ...), custom_call_target="tpu_custom_call" | custom-call | tf_op jit(solution)/shard_map/backward/pallas_call | solution.py:567
  95.9 1.1 collective-permute-start.13
  97.0 0.1 collective-permute-start.12
  97.1 2.1 %collective-permute-done.13 = bf16[512,768]{1,0:T(8,128)(2,1)S(1)} collective-permute-done((bf16[512,768]{1,0:T(8,128)(2,1)}, bf16[512,768]{1,0:T(8,128)(2,1)S(1)}, u32[]{:S(2)}, u32[]{:S(2)}) %collective-permute-start.13) | collective-permute-done | bytes 786464 | tf_op jit(solution)/shard_map/ppermute | solution.py:614
  99.2 2.2 %fusion = bf16[64,8,768]{2,1,0:T(8,128)(2,1)} fusion(bf16[512,768]{1,0:T(8,128)(2,1)S(1)} %collective-permute-done.13, bf16[512,768]{1,0:T(8,128)(2,1)} %get-tuple-element.80), kind=kLoop, calls=%fused_computation.3 | loop fusion | flops 1572864 | bytes 2359296 | tf_op jit(solution)/shard_map/reshape | solution.py:616
  101.4 0.1 convert_add_fusion
  101.6 0.7 collective-permute-start.14
  102.3 12.0 %all-to-all-start.2 = ((bf16[64,8,768]{2,1,0:T(8,128)(2,1)}), bf16[64,8,768]{2,1,0:T(8,128)(2,1)S(1)}, u32[]{:S(2)}, u32[]{:S(2)}) async-start(bf16[64,8,768]{2,1,0:T(8,128)(2,1)} %fusion), calls=%async_computation.2 | async-start | bytes 1572864 | tf_op jit(solution)/shard_map/all_to_all | solution.py:619
  114.4 0.1 convert_add_fusion.1
  114.5 2.5 %collective-permute-start.17 = (bf16[96,384]{1,0:T(8,128)(2,1)S(1)}, bf16[96,384]{1,0:T(8,128)(2,1)S(1)}, u32[]{:S(2)}, u32[]{:S(2)}) collective-permute-start(bf16[96,384]{1,0:T(8,128)(2,1)S(1)} %get-tuple-element.88), channel_id=1, source_target_pairs={{0,96},{8,104},{16,112},{24,120},{32,0},{40,8},{48,16},{56,24},{64... | collective-permute-start | bytes 221192 | tf_op jit(solution)/shard_map/ppermute | solution.py:637
  117.0 0.4 collective-permute-start.16
  117.3 0.7 collective-permute-start.15
  118.0 3.2 %features.1 = bf16[256,384]{1,0:T(8,128)(2,1)} custom-call(bf16[256,384]{1,0:T(8,128)(2,1)} %bitcast.37, bf16[384,256]{1,0:T(8,128)(2,1)} %get-tuple-element.76.gq_ref, bf16[384,256]{1,0:T(8,128)(2,1)} %get-tuple-element.77.gk_ref, bf16[384,256]{1,0:T(8,128)(2,1)} %get-tuple-element.78.gv_ref, bf16[384,256]{1,0:T(8,128)(2,1)} %get-tuple-element.83.gb_ref, ...), custom_call_target="tpu_custom_call" | custom-call | tf_op jit(solution)/shard_map/features/pallas_call | solution.py:620
  121.2 3.8 %collective-permute-done.17 = bf16[96,384]{1,0:T(8,128)(2,1)S(1)} collective-permute-done((bf16[96,384]{1,0:T(8,128)(2,1)S(1)}, bf16[96,384]{1,0:T(8,128)(2,1)S(1)}, u32[]{:S(2)}, u32[]{:S(2)}) %collective-permute-start.17) | collective-permute-done | bytes 73760 | tf_op jit(solution)/shard_map/ppermute | solution.py:637
  125.0 0.3 collective-permute-done.16
  125.3 5.6 %collective-permute-done.15 = bf16[96,384]{1,0:T(8,128)(2,1)S(1)} collective-permute-done((bf16[96,384]{1,0:T(8,128)(2,1)S(1)}, bf16[96,384]{1,0:T(8,128)(2,1)S(1)}, u32[]{:S(2)}, u32[]{:S(2)}) %collective-permute-start.15) | collective-permute-done | bytes 73760 | tf_op jit(solution)/shard_map/ppermute | solution.py:637
  131.0 0.8 copy.14
  131.7 0.1 convert_reduce_fusion
  131.9 0.6 reshape.55
  (46 shorter events, 0.3 us)
Async XLA Ops:
  0.6 12.5 %collective-permute-start.1 = (bf16[256,384]{1,0:T(8,128)(2,1)}, bf16[256,384]{1,0:T(8,128)(2,1)S(1)}, u32[]{:S(2)}, u32[]{:S(2)}) collective-permute-start(bf16[256,384]{1,0:T(8,128)(2,1)} %bitcast.32), channel_id=1, source_target_pairs={{0,1},{1,0},{2,3},{3,2},{4,5},{5,4},{6,7},{7,6},{8,9},{9,8},{10,11... | collective-permute-start | bytes 589832 | tf_op jit(solution)/shard_map/ppermute | solution.py:457
  4.5 8.7 %collective-permute-start.2 = (bf16[256,384]{1,0:T(8,128)(2,1)}, bf16[256,384]{1,0:T(8,128)(2,1)S(1)}, u32[]{:S(2)}, u32[]{:S(2)}) collective-permute-start(bf16[256,384]{1,0:T(8,128)(2,1)} %bitcast.33), channel_id=1, source_target_pairs={{0,2},{1,3},{2,4},{3,5},{4,6},{5,7},{6,0},{7,1},{8,10},{9,11},{10,... | collective-permute-start | bytes 589832 | tf_op jit(solution)/shard_map/ppermute | solution.py:460
  5.7 7.5 %collective-permute-start.3 = (bf16[256,384]{1,0:T(8,128)(2,1)}, bf16[256,384]{1,0:T(8,128)(2,1)S(1)}, u32[]{:S(2)}, u32[]{:S(2)}) collective-permute-start(bf16[256,384]{1,0:T(8,128)(2,1)} %bitcast.34), channel_id=1, source_target_pairs={{0,6},{1,7},{2,0},{3,1},{4,2},{5,3},{6,4},{7,5},{8,14},{9,15},{10,... | collective-permute-start | bytes 589832 | tf_op jit(solution)/shard_map/ppermute | solution.py:460
  10.1 3.0 %collective-permute-start = (bf16[1,48,384]{2,1,0:T(8,128)(2,1)}, bf16[1,48,384]{2,1,0:T(8,128)(2,1)S(1)}, u32[]{:S(2)}, u32[]{:S(2)}) collective-permute-start(bf16[1,48,384]{2,1,0:T(8,128)(2,1)} %bitcast.43), channel_id=1, source_target_pairs={{0,16},{8,24},{16,0},{24,8},{32,48},{40,56},{48,32},{56,40},{64,80... | collective-permute-start | bytes 110600 | tf_op jit(solution)/shard_map/ppermute | solution.py:478
  13.1 20.6 %copy-start.5 = (bf16[256,384]{1,0:T(8,128)(2,1)}, bf16[256,384]{1,0:T(8,128)(2,1)S(1)}, u32[]{:S(2)}) copy-start(bf16[256,384]{1,0:T(8,128)(2,1)S(1)} %collective-permute-done.1.refs_3_) | copy-start | bytes 589828
  13.2 22.2 %copy-start.6 = (bf16[256,384]{1,0:T(8,128)(2,1)}, bf16[256,384]{1,0:T(8,128)(2,1)S(1)}, u32[]{:S(2)}) copy-start(bf16[256,384]{1,0:T(8,128)(2,1)S(1)} %collective-permute-done.2.refs_4_) | copy-start | bytes 589828
  13.2 0.7 copy-start.7
  13.2 4.3 %copy-start.11 = (bf16[3,16,384]{2,1,0:T(8,128)(2,1)S(1)}, bf16[3,16,384]{2,1,0:T(8,128)(2,1)}, u32[]{:S(2)}) copy-start(bf16[3,16,384]{2,1,0:T(8,128)(2,1)} %get-tuple-element.46) | copy-start | bytes 110596
  13.9 32.5 %all-to-all-start = ((bf16[8,480,256]{2,1,0:T(8,128)(2,1)}), bf16[8,480,256]{2,1,0:T(8,128)(2,1)S(1)}, u32[]{:S(2)}, u32[]{:S(2)}) async-start(bf16[8,480,256]{2,1,0:T(8,128)(2,1)} %get-tuple-element.47), calls=%async_computation | async-start | bytes 3932160 | tf_op jit(solution)/shard_map/all_to_all | solution.py:485
  21.0 8.3 %collective-permute-start.4 = (bf16[2,48,384]{2,1,0:T(8,128)(2,1)S(1)}, bf16[2,48,384]{2,1,0:T(8,128)(2,1)S(1)}, u32[]{:S(2)}, u32[]{:S(2)}) collective-permute-start(bf16[2,48,384]{2,1,0:T(8,128)(2,1)S(1)} %pad_maximum_fusion), channel_id=1, source_target_pairs={{0,32},{8,40},{16,48},{24,56},{32,64},{40,72},{48,80},{56,88},{64,... | collective-permute-start | bytes 221192 | tf_op jit(solution)/shard_map/ppermute | solution.py:505
  22.7 6.7 %collective-permute-start.5 = (bf16[2,48,384]{2,1,0:T(8,128)(2,1)S(1)}, bf16[2,48,384]{2,1,0:T(8,128)(2,1)S(1)}, u32[]{:S(2)}, u32[]{:S(2)}) collective-permute-start(bf16[2,48,384]{2,1,0:T(8,128)(2,1)S(1)} %pad_maximum_fusion), channel_id=1, source_target_pairs={{0,64},{8,72},{16,80},{24,88},{32,96},{40,104},{48,112},{56,120},{... | collective-permute-start | bytes 221192 | tf_op jit(solution)/shard_map/ppermute | solution.py:505
  26.0 3.5 %collective-permute-start.6 = (bf16[2,48,384]{2,1,0:T(8,128)(2,1)S(1)}, bf16[2,48,384]{2,1,0:T(8,128)(2,1)S(1)}, u32[]{:S(2)}, u32[]{:S(2)}) collective-permute-start(bf16[2,48,384]{2,1,0:T(8,128)(2,1)S(1)} %pad_maximum_fusion), channel_id=1, source_target_pairs={{0,96},{8,104},{16,112},{24,120},{32,0},{40,8},{48,16},{56,24},{64... | collective-permute-start | bytes 221192 | tf_op jit(solution)/shard_map/ppermute | solution.py:505
  26.8 17.6 %collective-permute-start.9 = (bf16[256,384]{1,0:T(8,128)(2,1)S(1)}, bf16[256,384]{1,0:T(8,128)(2,1)S(1)}, u32[]{:S(2)}, u32[]{:S(2)}) collective-permute-start(bf16[256,384]{1,0:T(8,128)(2,1)S(1)} %collective-permute-done.1.refs_3_), channel_id=1, source_target_pairs={{0,6},{1,7},{2,0},{3,1},{4,2},{5,3},{6,4},{7,5},{8,14},{9,15},{10,... | collective-permute-start | bytes 589832 | tf_op jit(solution)/shard_map/ppermute | solution.py:460
  29.6 16.8 %copy-start.3 = (bf16[8,48,384]{2,1,0:T(8,128)(2,1)}, bf16[8,48,384]{2,1,0:T(8,128)(2,1)S(1)}, u32[]{:S(2)}) copy-start(bf16[8,48,384]{2,1,0:T(8,128)(2,1)S(1)} %constant_dynamic-update-slice_fusion.refs_2_) | copy-start | bytes 884740
  29.6 16.8 %collective-permute-start.7 = (bf16[8,48,384]{2,1,0:T(8,128)(2,1)S(1)}, bf16[8,48,384]{2,1,0:T(8,128)(2,1)S(1)}, u32[]{:S(2)}, u32[]{:S(2)}) collective-permute-start(bf16[8,48,384]{2,1,0:T(8,128)(2,1)S(1)} %constant_dynamic-update-slice_fusion.refs_2_), channel_id=1, source_target_pairs={{0,8},{8,0},{16,24},{24,16},{32,40},{40,32},{48,56},{56,48},{64,72... | collective-permute-start | bytes 884744 | tf_op jit(solution)/shard_map/ppermute | solution.py:507
  33.7 18.3 %collective-permute-start.8 = (bf16[256,384]{1,0:T(8,128)(2,1)S(1)}, bf16[256,384]{1,0:T(8,128)(2,1)S(1)}, u32[]{:S(2)}, u32[]{:S(2)}) collective-permute-start(bf16[256,384]{1,0:T(8,128)(2,1)S(1)} %collective-permute-done.1.refs_3_), channel_id=1, source_target_pairs={{0,2},{1,3},{2,4},{3,5},{4,6},{5,7},{6,0},{7,1},{8,10},{9,11},{10,... | collective-permute-start | bytes 589832 | tf_op jit(solution)/shard_map/ppermute | solution.py:460
  35.4 19.2 %collective-permute-start.10 = (bf16[256,384]{1,0:T(8,128)(2,1)S(1)}, bf16[256,384]{1,0:T(8,128)(2,1)S(1)}, u32[]{:S(2)}, u32[]{:S(2)}) collective-permute-start(bf16[256,384]{1,0:T(8,128)(2,1)S(1)} %collective-permute-done.2.refs_4_), channel_id=1, source_target_pairs={{0,2},{1,3},{2,4},{3,5},{4,6},{5,7},{6,0},{7,1},{8,10},{9,11},{10,... | collective-permute-start | bytes 589832 | tf_op jit(solution)/shard_map/ppermute | solution.py:460
  44.4 14.4 %copy-start.8 = (bf16[256,384]{1,0:T(8,128)(2,1)}, bf16[256,384]{1,0:T(8,128)(2,1)S(1)}, u32[]{:S(2)}) copy-start(bf16[256,384]{1,0:T(8,128)(2,1)S(1)} %collective-permute-done.9.refs_7_) | copy-start | bytes 589828
  44.4 10.2 %collective-permute-start.11 = (bf16[256,384]{1,0:T(8,128)(2,1)S(1)}, bf16[256,384]{1,0:T(8,128)(2,1)}, u32[]{:S(2)}, u32[]{:S(2)}) collective-permute-start(bf16[256,384]{1,0:T(8,128)(2,1)S(1)} %collective-permute-done.9.refs_7_), channel_id=1, source_target_pairs={{0,6},{1,7},{2,0},{3,1},{4,2},{5,3},{6,4},{7,5},{8,14},{9,15},{10,... | collective-permute-start | bytes 589832 | tf_op jit(solution)/shard_map/ppermute | solution.py:460
  46.4 0.7 copy-start.4
  46.4 1.4 %copy-start = (bf16[8,480,256]{2,1,0:T(8,128)(2,1)}, bf16[8,480,256]{2,1,0:T(8,128)(2,1)S(1)}, u32[]{:S(2)}) copy-start(bf16[8,480,256]{2,1,0:T(8,128)(2,1)S(1)} %all-to-all-done.refs_1_) | copy-start | bytes 5898244
  52.1 6.1 %copy-start.9 = (bf16[256,384]{1,0:T(8,128)(2,1)}, bf16[256,384]{1,0:T(8,128)(2,1)S(1)}, u32[]{:S(2)}) copy-start(bf16[256,384]{1,0:T(8,128)(2,1)S(1)} %collective-permute-done.8.refs_5_) | copy-start | bytes 589828
  54.6 3.6 %copy-start.10 = (bf16[256,384]{1,0:T(8,128)(2,1)}, bf16[256,384]{1,0:T(8,128)(2,1)S(1)}, u32[]{:S(2)}) copy-start(bf16[256,384]{1,0:T(8,128)(2,1)S(1)} %collective-permute-done.10.refs_8_) | copy-start | bytes 589828
  54.6 29.5 %all-to-all-start.1 = ((bf16[8,48,2048]{2,1,0:T(8,128)(2,1)}), bf16[8,48,2048]{2,1,0:T(8,128)(2,1)S(1)}, u32[]{:S(2)}, u32[]{:S(2)}) async-start(bf16[8,48,2048]{2,1,0:T(8,128)(2,1)} %conv_input.1), calls=%async_computation.1 | async-start | bytes 3145728 | tf_op jit(solution)/shard_map/all_to_all | solution.py:525
  84.0 1.1 copy-start.1
  85.2 11.8 %copy-start.12 = (bf16[8,96,384]{2,1,0:T(8,128)(2,1)S(1)}, bf16[8,96,384]{2,1,0:T(8,128)(2,1)}, u32[]{:S(2)}) copy-start(bf16[8,96,384]{2,1,0:T(8,128)(2,1)} %get-tuple-element.79) | copy-start | bytes 1769476
  95.9 5.5 %copy-start.2 = (bf16[8,96,384]{2,1,0:T(8,128)(2,1)S(1)}, bf16[8,96,384]{2,1,0:T(8,128)(2,1)}, u32[]{:S(2)}) copy-start(bf16[8,96,384]{2,1,0:T(8,128)(2,1)} %get-tuple-element.85) | copy-start | bytes 1769476
  95.9 3.3 %collective-permute-start.13 = (bf16[512,768]{1,0:T(8,128)(2,1)}, bf16[512,768]{1,0:T(8,128)(2,1)S(1)}, u32[]{:S(2)}, u32[]{:S(2)}) collective-permute-start(bf16[512,768]{1,0:T(8,128)(2,1)} %get-tuple-element.81), channel_id=1, source_target_pairs={{0,8},{8,0},{16,24},{24,16},{32,40},{40,32},{48,56},{56,48},{64,72... | collective-permute-start | bytes 2359304 | tf_op jit(solution)/shard_map/ppermute | solution.py:614
  97.0 4.4 %collective-permute-start.12 = (bf16[8,96,384]{2,1,0:T(8,128)(2,1)S(1)}, bf16[8,96,384]{2,1,0:T(8,128)(2,1)S(1)}, u32[]{:S(2)}, u32[]{:S(2)}) collective-permute-start(bf16[8,96,384]{2,1,0:T(8,128)(2,1)S(1)} %copy-done.12), channel_id=1, source_target_pairs={{0,8},{8,0},{16,24},{24,16},{32,40},{40,32},{48,56},{56,48},{64,72... | collective-permute-start | bytes 1769480 | tf_op jit(solution)/shard_map/ppermute | solution.py:565
  101.6 12.8 %collective-permute-start.14 = (bf16[4,96,384]{2,1,0:T(8,128)(2,1)S(1)}, bf16[4,96,384]{2,1,0:T(8,128)(2,1)S(1)}, u32[]{:S(2)}, u32[]{:S(2)}) collective-permute-start(bf16[4,96,384]{2,1,0:T(8,128)(2,1)S(1)} %dynamic-slice_convert_fusion), channel_id=1, source_target_pairs={{0,16},{8,24},{16,0},{24,8},{32,48},{40,56},{48,32},{56,40},{64,80... | collective-permute-start | bytes 884744 | tf_op jit(solution)/shard_map/ppermute | solution.py:632
  102.3 29.4 %all-to-all-start.2 = ((bf16[64,8,768]{2,1,0:T(8,128)(2,1)}), bf16[64,8,768]{2,1,0:T(8,128)(2,1)S(1)}, u32[]{:S(2)}, u32[]{:S(2)}) async-start(bf16[64,8,768]{2,1,0:T(8,128)(2,1)} %fusion), calls=%async_computation.2 | async-start | bytes 1572864 | tf_op jit(solution)/shard_map/all_to_all | solution.py:619
  114.5 10.5 %collective-permute-start.17 = (bf16[96,384]{1,0:T(8,128)(2,1)S(1)}, bf16[96,384]{1,0:T(8,128)(2,1)S(1)}, u32[]{:S(2)}, u32[]{:S(2)}) collective-permute-start(bf16[96,384]{1,0:T(8,128)(2,1)S(1)} %get-tuple-element.88), channel_id=1, source_target_pairs={{0,96},{8,104},{16,112},{24,120},{32,0},{40,8},{48,16},{56,24},{64... | collective-permute-start | bytes 221192 | tf_op jit(solution)/shard_map/ppermute | solution.py:637
  117.0 8.3 %collective-permute-start.16 = (bf16[96,384]{1,0:T(8,128)(2,1)S(1)}, bf16[96,384]{1,0:T(8,128)(2,1)S(1)}, u32[]{:S(2)}, u32[]{:S(2)}) collective-permute-start(bf16[96,384]{1,0:T(8,128)(2,1)S(1)} %get-tuple-element.89), channel_id=1, source_target_pairs={{0,64},{8,72},{16,80},{24,88},{32,96},{40,104},{48,112},{56,120},{... | collective-permute-start | bytes 221192 | tf_op jit(solution)/shard_map/ppermute | solution.py:637
  117.3 13.6 %collective-permute-start.15 = (bf16[96,384]{1,0:T(8,128)(2,1)S(1)}, bf16[96,384]{1,0:T(8,128)(2,1)S(1)}, u32[]{:S(2)}, u32[]{:S(2)}) collective-permute-start(bf16[96,384]{1,0:T(8,128)(2,1)S(1)} %get-tuple-element.87), channel_id=1, source_target_pairs={{0,32},{8,40},{16,48},{24,56},{32,64},{40,72},{48,80},{56,88},{64,... | collective-permute-start | bytes 221192 | tf_op jit(solution)/shard_map/ppermute | solution.py:637

commit v6 on v5

--- a/solution.py
+++ b/solution.py
@@ -428,6 +428,10 @@
             to_ref[:, c * 128 : (c + 1) * 128] = line_ref[c].astype(BF16)
 
 
+def add_kernel(one_ref, other_ref, out_ref):
+    out_ref[...] = (one_ref[...].astype(F32) + other_ref[...].astype(F32)).astype(BF16)
+
+
 def shards(
     features, past_frames, upstream, query_weight, key_weight, value_weight, out_weight, conv_weight
 ):
@@ -612,7 +616,14 @@
     )
 
     taken = lax.ppermute(give, "dp", [(d, d ^ 1) for d in range(slots)])
-    chip = (keep.astype(F32) + taken.astype(F32)).astype(BF16)
+    chip = pl.pallas_call(
+        add_kernel,
+        out_shape=jax.ShapeDtypeStruct(keep.shape, BF16),
+        in_specs=whole(2),
+        out_specs=pl.BlockSpec(memory_space=pltpu.VMEM),
+        compiler_params=params(56),
+        name="add",
+    )(keep, taken)
     chip = chip.reshape(pairs * groups, 8, 2 * chans)
     same_core = [[d * groups + r for d in range(c, slots, 2) for r in range(groups)] for c in range(2)]
     conv_taken, chip, gb = lax.optimization_barrier((conv_taken, chip, gb))

time: 133 us -> 134 us (level)
  Pallas kernels: 49.9 us -> 52.3 us
  other arithmetic: 3.15 us -> 1.03 us
    pallas_call x0 -> x1, Pallas kernels: none -> 2.44 us  [shards(): pl.pallas_call(add_kernel, out_shape=jax.ShapeDtypeStruct(keep.shape, BF1...]
    reshape x1 -> x0, other arithmetic: 2.2 us -> none  [shards(): chip = chip.reshape(pairs * groups, 8, 2 * chans)]
    unnamed x32 -> x34, local copies, waits for them, and re-layouts: 4.09 us -> 4.97 us
  transfers between devices with their start and end apart: 21 -> 21, of which waited for: 8 -> 8; matrix products, arithmetic and copies ran while one was open for 3% -> 1% of each run, Pallas kernels for 30% -> 31%
where the time goes in v6:
time: 134 us
  Pallas kernels  52.3 us (39%)
  starting transfers between devices  48.9 us (36%)
  waiting for transfers between devices  24.9 us (19%)
  local copies, waits for them, and re-layouts  5.74 us (4%)
    pallas_call x1, Pallas kernels, shards(): pl.pallas_call(lambda *refs: forward_kernel(width, *refs), out_shape=(jax...  25.2 us
    all_to_all x1, starting transfers between devices, shards(): lax.all_to_all(chip, ('dp', 'rows'), 0, 0, axis_index_groups=same_core)  12 us
    pallas_call x1, Pallas kernels, shards(): pl.pallas_call(backward_kernel, out_shape=(jax.ShapeDtypeStruct((chans, c...  10.7 us
    ppermute x6, waiting for transfers between devices, along(): lax.ppermute(block, 'rows', [(r, (r + 2 * step) % groups) for r in range(...  10.3 us
    ppermute x6, starting transfers between devices, along(): lax.ppermute(block, 'rows', [(r, (r + 2 * step) % groups) for r in range(...  10.1 us
    ppermute x3, waiting for transfers between devices, shards(): lax.ppermute(sent, 'dp', [(d, (d + 4 * on) % slots) for d in range(slots)])  9.71 us
    ppermute x3, starting transfers between devices, shards(): lax.ppermute(w_near, 'dp', [(d, (d + 4 * back) % slots) for d in range(sl...  5.74 us
    unnamed x34, local copies, waits for them, and re-layouts  4.97 us
  transfers between devices with their start and end apart: 21, of which 8 were waited for; matrix products, arithmetic and copies ran while one was open for 1% of the time, Pallas kernels for 31%

profile of v6, /device:TPU:1, one launch (start us, length us, event | category | flops | bytes accessed | tf_op | source)
XLA Modules:
  0.0 133.8 jit_solution(15673732336607012567)
XLA Ops:
  0.6 3.8 %collective-permute-start.1 = (bf16[256,384]{1,0:T(8,128)(2,1)}, bf16[256,384]{1,0:T(8,128)(2,1)S(1)}, u32[]{:S(2)}, u32[]{:S(2)}) collective-permute-start(bf16[256,384]{1,0:T(8,128)(2,1)} %bitcast.31), channel_id=1, source_target_pairs={{0,1},{1,0},{2,3},{3,2},{4,5},{5,4},{6,7},{7,6},{8,9},{9,8},{10,11... | collective-permute-start | bytes 589832 | tf_op jit(solution)/shard_map/ppermute | solution.py:461
  4.5 1.2 collective-permute-start.2
  5.7 1.5 %collective-permute-start.3 = (bf16[256,384]{1,0:T(8,128)(2,1)}, bf16[256,384]{1,0:T(8,128)(2,1)S(1)}, u32[]{:S(2)}, u32[]{:S(2)}) collective-permute-start(bf16[256,384]{1,0:T(8,128)(2,1)} %bitcast.33), channel_id=1, source_target_pairs={{0,6},{1,7},{2,0},{3,1},{4,2},{5,3},{6,4},{7,5},{8,14},{9,15},{10,... | collective-permute-start | bytes 589832 | tf_op jit(solution)/shard_map/ppermute | solution.py:464
  7.1 3.0 %pack.1 = (bf16[8,480,256]{2,1,0:T(8,128)(2,1)}, bf16[3,16,384]{2,1,0:T(8,128)(2,1)}) custom-call(bf16[256,384]{1,0:T(8,128)(2,1)} %bitcast.39, bf16[2,256,384]{2,1,0:T(8,128)(2,1)} %bitcast.38, bf16[384,384]{1,0:T(8,128)(2,1)} %constant.51.clone.order_ref, bf16[3,27,384]{2,1,0:T(8,128)(2,1)} %conv_ref.1), custom_call_target="tpu_custom_call" | custom-call | tf_op jit(solution)/shard_map/pack/pallas_call | solution.py:469
  10.1 0.4 collective-permute-start
  10.5 2.6 %collective-permute-done = bf16[1,48,384]{2,1,0:T(8,128)(2,1)S(1)} collective-permute-done((bf16[1,48,384]{2,1,0:T(8,128)(2,1)}, bf16[1,48,384]{2,1,0:T(8,128)(2,1)S(1)}, u32[]{:S(2)}, u32[]{:S(2)}) %collective-permute-start) | collective-permute-done | bytes 36896 | tf_op jit(solution)/shard_map/ppermute | solution.py:482
  13.2 0.0 collective-permute-done.1.refs_3_
  13.2 0.7 copy-done.8
  13.9 3.6 %all-to-all-start = ((bf16[8,480,256]{2,1,0:T(8,128)(2,1)}), bf16[8,480,256]{2,1,0:T(8,128)(2,1)S(1)}, u32[]{:S(2)}, u32[]{:S(2)}) async-start(bf16[8,480,256]{2,1,0:T(8,128)(2,1)} %get-tuple-element.47), calls=%async_computation | async-start | bytes 3932160 | tf_op jit(solution)/shard_map/all_to_all | solution.py:489
  17.5 3.5 %prepare.1 = (bf16[1152,384]{1,0:T(8,128)(2,1)}, bf16[384,768]{1,0:T(8,128)(2,1)}, bf16[48,384]{1,0:T(8,128)(2,1)}, bf16[48,384]{1,0:T(8,128)(2,1)}, bf16[384,384]{1,0:T(8,128)(2,1)}) custom-call(s32[1]{0:T(128)} %bitcast.1.me_ref, bf16[384,384]{1,0:T(8,128)(2,1)} %wq_ref.3, bf16[384,384]{1,0:T(8,128)(2,1)} %wk_ref.3, bf16[384,384]{1,0:T(8,128)(2,1)} %wv_ref.3, ...), custom_call_target="tpu_custom_call" | custom-call | tf_op jit(solution)/shard_map/prepare/pallas_call | solution.py:490
  21.0 1.7 %collective-permute-start.4 = (bf16[2,48,384]{2,1,0:T(8,128)(2,1)S(1)}, bf16[2,48,384]{2,1,0:T(8,128)(2,1)S(1)}, u32[]{:S(2)}, u32[]{:S(2)}) collective-permute-start(bf16[2,48,384]{2,1,0:T(8,128)(2,1)S(1)} %pad_maximum_fusion), channel_id=1, source_target_pairs={{0,32},{8,40},{16,48},{24,56},{32,64},{40,72},{48,80},{56,88},{64,... | collective-permute-start | bytes 221192 | tf_op jit(solution)/shard_map/ppermute | solution.py:509
  22.7 3.3 %collective-permute-start.5 = (bf16[2,48,384]{2,1,0:T(8,128)(2,1)S(1)}, bf16[2,48,384]{2,1,0:T(8,128)(2,1)S(1)}, u32[]{:S(2)}, u32[]{:S(2)}) collective-permute-start(bf16[2,48,384]{2,1,0:T(8,128)(2,1)S(1)} %pad_maximum_fusion), channel_id=1, source_target_pairs={{0,64},{8,72},{16,80},{24,88},{32,96},{40,104},{48,112},{56,120},{... | collective-permute-start | bytes 221192 | tf_op jit(solution)/shard_map/ppermute | solution.py:509
  26.0 0.7 collective-permute-start.6
  26.8 2.6 %collective-permute-start.9 = (bf16[256,384]{1,0:T(8,128)(2,1)S(1)}, bf16[256,384]{1,0:T(8,128)(2,1)S(1)}, u32[]{:S(2)}, u32[]{:S(2)}) collective-permute-start(bf16[256,384]{1,0:T(8,128)(2,1)S(1)} %collective-permute-done.1.refs_3_), channel_id=1, source_target_pairs={{0,6},{1,7},{2,0},{3,1},{4,2},{5,3},{6,4},{7,5},{8,14},{9,15},{10,... | collective-permute-start | bytes 589832 | tf_op jit(solution)/shard_map/ppermute | solution.py:464
  29.4 0.1 collective-permute-done.6
  29.6 4.2 %collective-permute-start.7 = (bf16[8,48,384]{2,1,0:T(8,128)(2,1)S(1)}, bf16[8,48,384]{2,1,0:T(8,128)(2,1)S(1)}, u32[]{:S(2)}, u32[]{:S(2)}) collective-permute-start(bf16[8,48,384]{2,1,0:T(8,128)(2,1)S(1)} %constant_dynamic-update-slice_fusion.refs_2_), channel_id=1, source_target_pairs={{0,8},{8,0},{16,24},{24,16},{32,40},{40,32},{48,56},{56,48},{64,72... | collective-permute-start | bytes 884744 | tf_op jit(solution)/shard_map/ppermute | solution.py:511
  33.7 1.7 %collective-permute-start.8 = (bf16[256,384]{1,0:T(8,128)(2,1)S(1)}, bf16[256,384]{1,0:T(8,128)(2,1)S(1)}, u32[]{:S(2)}, u32[]{:S(2)}) collective-permute-start(bf16[256,384]{1,0:T(8,128)(2,1)S(1)} %collective-permute-done.1.refs_3_), channel_id=1, source_target_pairs={{0,2},{1,3},{2,4},{3,5},{4,6},{5,7},{6,0},{7,1},{8,10},{9,11},{10,... | collective-permute-start | bytes 589832 | tf_op jit(solution)/shard_map/ppermute | solution.py:464
  35.4 1.2 collective-permute-start.10
  36.6 7.8 %collective-permute-done.9.refs_7_ = bf16[256,384]{1,0:T(8,128)(2,1)S(1)} collective-permute-done((bf16[256,384]{1,0:T(8,128)(2,1)S(1)}, bf16[256,384]{1,0:T(8,128)(2,1)S(1)}, u32[]{:S(2)}, u32[]{:S(2)}) %collective-permute-start.9) | collective-permute-done | bytes 196640 | tf_op jit(solution)/shard_map/ppermute | solution.py:464
  44.4 2.0 %collective-permute-start.11 = (bf16[256,384]{1,0:T(8,128)(2,1)S(1)}, bf16[256,384]{1,0:T(8,128)(2,1)}, u32[]{:S(2)}, u32[]{:S(2)}) collective-permute-start(bf16[256,384]{1,0:T(8,128)(2,1)S(1)} %collective-permute-done.9.refs_7_), channel_id=1, source_target_pairs={{0,6},{1,7},{2,0},{3,1},{4,2},{5,3},{6,4},{7,5},{8,14},{9,15},{10,... | collective-permute-start | bytes 589832 | tf_op jit(solution)/shard_map/ppermute | solution.py:464
  46.4 0.7 copy-done.5
  47.1 0.7 copy-done
  47.8 4.3 %conv_input.1 = bf16[8,48,2048]{2,1,0:T(8,128)(2,1)} custom-call(s32[1]{0:T(128)} %bitcast.3.refs_0_, bf16[8,480,256]{2,1,0:T(8,128)(2,1)} %copy-done, bf16[8,48,384]{2,1,0:T(8,128)(2,1)} %copy-done.4, bf16[8,48,384]{2,1,0:T(8,128)(2,1)} %copy-done.5), custom_call_target="tpu_custom_call" | custom-call | tf_op jit(solution)/shard_map/conv_input/pallas_call | solution.py:513
  52.1 2.5 %collective-permute-done.10.refs_8_ = bf16[256,384]{1,0:T(8,128)(2,1)S(1)} collective-permute-done((bf16[256,384]{1,0:T(8,128)(2,1)S(1)}, bf16[256,384]{1,0:T(8,128)(2,1)S(1)}, u32[]{:S(2)}, u32[]{:S(2)}) %collective-permute-start.10) | collective-permute-done | bytes 196640 | tf_op jit(solution)/shard_map/ppermute | solution.py:464
  54.6 3.6 %all-to-all-start.1 = ((bf16[8,48,2048]{2,1,0:T(8,128)(2,1)}), bf16[8,48,2048]{2,1,0:T(8,128)(2,1)S(1)}, u32[]{:S(2)}, u32[]{:S(2)}) async-start(bf16[8,48,2048]{2,1,0:T(8,128)(2,1)} %conv_input.1), calls=%async_computation.1 | async-start | bytes 3145728 | tf_op jit(solution)/shard_map/all_to_all | solution.py:529
  58.2 0.7 pad_add_fusion.refs_0_.place_ref
  58.9 25.2 %forward.1 = (bf16[384,2048]{1,0:T(8,128)(2,1)}, bf16[384,2048]{1,0:T(8,128)(2,1)}, bf16[2048,384]{1,0:T(8,128)(2,1)}, bf16[2048,384]{1,0:T(8,128)(2,1)}, f32[38...) custom-call(s32[2]{0:T(128)} %pad_add_fusion.refs_0_.place_ref, ...), custom_call_target="tpu_custom_call" | custom-call | tf_op jit(solution)/shard_map/forward/pallas_call | solution.py:531
  84.1 1.1 copy-done.1
  85.3 10.7 %backward.1 = (bf16[384,256]{1,0:T(8,128)(2,1)}, bf16[384,256]{1,0:T(8,128)(2,1)}, bf16[384,256]{1,0:T(8,128)(2,1)}, bf16[384,256]{1,0:T(8,128)(2,1)}, bf16[512,...) custom-call(s32[2]{0:T(128)} %pad_add_fusion.refs_0_.place_ref, bf16[256,384]{1,0:T(8,128)(2,1)} %bitcast.35, ...), custom_call_target="tpu_custom_call" | custom-call | tf_op jit(solution)/shard_map/backward/pallas_call | solution.py:571
  96.0 1.1 collective-permute-start.13
  97.0 0.1 collective-permute-start.12
  97.1 2.1 %collective-permute-done.13.other_ref = bf16[512,768]{1,0:T(8,128)(2,1)S(1)} collective-permute-done((bf16[512,768]{1,0:T(8,128)(2,1)}, bf16[512,768]{1,0:T(8,128)(2,1)S(1)}, u32[]{:S(2)}, u32[]{:S(2)}) %collective-permute-start.13) | collective-permute-done | bytes 786464 | tf_op jit(solution)/shard_map/ppermute | solution.py:618
  99.3 0.9 copy-done.2
  100.2 2.4 %add.71 = bf16[512,768]{1,0:T(8,128)(2,1)} custom-call(bf16[512,768]{1,0:T(8,128)(2,1)} %get-tuple-element.80.one_ref, bf16[512,768]{1,0:T(8,128)(2,1)} %copy-done.2), custom_call_target="tpu_custom_call" | custom-call | tf_op jit(solution)/shard_map/add/pallas_call | solution.py:619
  102.6 0.1 convert_add_fusion
  102.8 0.8 collective-permute-start.14
  103.5 12.0 %all-to-all-start.2 = ((bf16[64,8,768]{2,1,0:T(8,128)(2,1)}), bf16[64,8,768]{2,1,0:T(8,128)(2,1)S(1)}, u32[]{:S(2)}, u32[]{:S(2)}) async-start(bf16[64,8,768]{2,1,0:T(8,128)(2,1)} %bitcast.8), calls=%async_computation.2 | async-start | bytes 1572864 | tf_op jit(solution)/shard_map/all_to_all | solution.py:630
  115.6 0.1 convert_add_fusion.1
  115.7 2.5 %collective-permute-start.17 = (bf16[96,384]{1,0:T(8,128)(2,1)S(1)}, bf16[96,384]{1,0:T(8,128)(2,1)S(1)}, u32[]{:S(2)}, u32[]{:S(2)}) collective-permute-start(bf16[96,384]{1,0:T(8,128)(2,1)S(1)} %get-tuple-element.88), channel_id=1, source_target_pairs={{0,96},{8,104},{16,112},{24,120},{32,0},{40,8},{48,16},{56,24},{64... | collective-permute-start | bytes 221192 | tf_op jit(solution)/shard_map/ppermute | solution.py:648
  118.2 0.4 collective-permute-start.16
  118.6 0.7 collective-permute-start.15
  119.2 3.2 %features.1 = bf16[256,384]{1,0:T(8,128)(2,1)} custom-call(bf16[256,384]{1,0:T(8,128)(2,1)} %bitcast.36, bf16[384,256]{1,0:T(8,128)(2,1)} %get-tuple-element.76.gq_ref, bf16[384,256]{1,0:T(8,128)(2,1)} %get-tuple-element.77.gk_ref, bf16[384,256]{1,0:T(8,128)(2,1)} %get-tuple-element.78.gv_ref, bf16[384,256]{1,0:T(8,128)(2,1)} %get-tuple-element.83.gb_ref, ...), custom_call_target="tpu_custom_call" | custom-call | tf_op jit(solution)/shard_map/features/pallas_call | solution.py:631
  122.4 3.8 %collective-permute-done.17 = bf16[96,384]{1,0:T(8,128)(2,1)S(1)} collective-permute-done((bf16[96,384]{1,0:T(8,128)(2,1)S(1)}, bf16[96,384]{1,0:T(8,128)(2,1)S(1)}, u32[]{:S(2)}, u32[]{:S(2)}) %collective-permute-start.17) | collective-permute-done | bytes 73760 | tf_op jit(solution)/shard_map/ppermute | solution.py:648
  126.2 0.3 collective-permute-done.16
  126.5 5.6 %collective-permute-done.15 = bf16[96,384]{1,0:T(8,128)(2,1)S(1)} collective-permute-done((bf16[96,384]{1,0:T(8,128)(2,1)S(1)}, bf16[96,384]{1,0:T(8,128)(2,1)S(1)}, u32[]{:S(2)}, u32[]{:S(2)}) %collective-permute-start.15) | collective-permute-done | bytes 73760 | tf_op jit(solution)/shard_map/ppermute | solution.py:648
  132.2 0.8 copy.14
  132.9 0.1 convert_reduce_fusion
  133.1 0.6 reshape.55
  (48 shorter events, 0.3 us)
Async XLA Ops:
  0.6 12.5 %collective-permute-start.1 = (bf16[256,384]{1,0:T(8,128)(2,1)}, bf16[256,384]{1,0:T(8,128)(2,1)S(1)}, u32[]{:S(2)}, u32[]{:S(2)}) collective-permute-start(bf16[256,384]{1,0:T(8,128)(2,1)} %bitcast.31), channel_id=1, source_target_pairs={{0,1},{1,0},{2,3},{3,2},{4,5},{5,4},{6,7},{7,6},{8,9},{9,8},{10,11... | collective-permute-start | bytes 589832 | tf_op jit(solution)/shard_map/ppermute | solution.py:461
  4.5 8.7 %collective-permute-start.2 = (bf16[256,384]{1,0:T(8,128)(2,1)}, bf16[256,384]{1,0:T(8,128)(2,1)S(1)}, u32[]{:S(2)}, u32[]{:S(2)}) collective-permute-start(bf16[256,384]{1,0:T(8,128)(2,1)} %bitcast.32), channel_id=1, source_target_pairs={{0,2},{1,3},{2,4},{3,5},{4,6},{5,7},{6,0},{7,1},{8,10},{9,11},{10,... | collective-permute-start | bytes 589832 | tf_op jit(solution)/shard_map/ppermute | solution.py:464
  5.7 7.5 %collective-permute-start.3 = (bf16[256,384]{1,0:T(8,128)(2,1)}, bf16[256,384]{1,0:T(8,128)(2,1)S(1)}, u32[]{:S(2)}, u32[]{:S(2)}) collective-permute-start(bf16[256,384]{1,0:T(8,128)(2,1)} %bitcast.33), channel_id=1, source_target_pairs={{0,6},{1,7},{2,0},{3,1},{4,2},{5,3},{6,4},{7,5},{8,14},{9,15},{10,... | collective-permute-start | bytes 589832 | tf_op jit(solution)/shard_map/ppermute | solution.py:464
  10.1 3.0 %collective-permute-start = (bf16[1,48,384]{2,1,0:T(8,128)(2,1)}, bf16[1,48,384]{2,1,0:T(8,128)(2,1)S(1)}, u32[]{:S(2)}, u32[]{:S(2)}) collective-permute-start(bf16[1,48,384]{2,1,0:T(8,128)(2,1)} %bitcast.42), channel_id=1, source_target_pairs={{0,16},{8,24},{16,0},{24,8},{32,48},{40,56},{48,32},{56,40},{64,80... | collective-permute-start | bytes 110600 | tf_op jit(solution)/shard_map/ppermute | solution.py:482
  13.2 20.6 %copy-start.6 = (bf16[256,384]{1,0:T(8,128)(2,1)}, bf16[256,384]{1,0:T(8,128)(2,1)S(1)}, u32[]{:S(2)}) copy-start(bf16[256,384]{1,0:T(8,128)(2,1)S(1)} %collective-permute-done.1.refs_3_) | copy-start | bytes 589828
  13.2 22.2 %copy-start.7 = (bf16[256,384]{1,0:T(8,128)(2,1)}, bf16[256,384]{1,0:T(8,128)(2,1)S(1)}, u32[]{:S(2)}) copy-start(bf16[256,384]{1,0:T(8,128)(2,1)S(1)} %collective-permute-done.2.refs_4_) | copy-start | bytes 589828
  13.2 0.7 copy-start.8
  13.2 4.3 %copy-start.12 = (bf16[3,16,384]{2,1,0:T(8,128)(2,1)S(1)}, bf16[3,16,384]{2,1,0:T(8,128)(2,1)}, u32[]{:S(2)}) copy-start(bf16[3,16,384]{2,1,0:T(8,128)(2,1)} %get-tuple-element.46) | copy-start | bytes 110596
  13.9 32.5 %all-to-all-start = ((bf16[8,480,256]{2,1,0:T(8,128)(2,1)}), bf16[8,480,256]{2,1,0:T(8,128)(2,1)S(1)}, u32[]{:S(2)}, u32[]{:S(2)}) async-start(bf16[8,480,256]{2,1,0:T(8,128)(2,1)} %get-tuple-element.47), calls=%async_computation | async-start | bytes 3932160 | tf_op jit(solution)/shard_map/all_to_all | solution.py:489
  21.0 8.3 %collective-permute-start.4 = (bf16[2,48,384]{2,1,0:T(8,128)(2,1)S(1)}, bf16[2,48,384]{2,1,0:T(8,128)(2,1)S(1)}, u32[]{:S(2)}, u32[]{:S(2)}) collective-permute-start(bf16[2,48,384]{2,1,0:T(8,128)(2,1)S(1)} %pad_maximum_fusion), channel_id=1, source_target_pairs={{0,32},{8,40},{16,48},{24,56},{32,64},{40,72},{48,80},{56,88},{64,... | collective-permute-start | bytes 221192 | tf_op jit(solution)/shard_map/ppermute | solution.py:509
  22.7 6.7 %collective-permute-start.5 = (bf16[2,48,384]{2,1,0:T(8,128)(2,1)S(1)}, bf16[2,48,384]{2,1,0:T(8,128)(2,1)S(1)}, u32[]{:S(2)}, u32[]{:S(2)}) collective-permute-start(bf16[2,48,384]{2,1,0:T(8,128)(2,1)S(1)} %pad_maximum_fusion), channel_id=1, source_target_pairs={{0,64},{8,72},{16,80},{24,88},{32,96},{40,104},{48,112},{56,120},{... | collective-permute-start | bytes 221192 | tf_op jit(solution)/shard_map/ppermute | solution.py:509
  26.0 3.5 %collective-permute-start.6 = (bf16[2,48,384]{2,1,0:T(8,128)(2,1)S(1)}, bf16[2,48,384]{2,1,0:T(8,128)(2,1)S(1)}, u32[]{:S(2)}, u32[]{:S(2)}) collective-permute-start(bf16[2,48,384]{2,1,0:T(8,128)(2,1)S(1)} %pad_maximum_fusion), channel_id=1, source_target_pairs={{0,96},{8,104},{16,112},{24,120},{32,0},{40,8},{48,16},{56,24},{64... | collective-permute-start | bytes 221192 | tf_op jit(solution)/shard_map/ppermute | solution.py:509
  26.8 17.6 %collective-permute-start.9 = (bf16[256,384]{1,0:T(8,128)(2,1)S(1)}, bf16[256,384]{1,0:T(8,128)(2,1)S(1)}, u32[]{:S(2)}, u32[]{:S(2)}) collective-permute-start(bf16[256,384]{1,0:T(8,128)(2,1)S(1)} %collective-permute-done.1.refs_3_), channel_id=1, source_target_pairs={{0,6},{1,7},{2,0},{3,1},{4,2},{5,3},{6,4},{7,5},{8,14},{9,15},{10,... | collective-permute-start | bytes 589832 | tf_op jit(solution)/shard_map/ppermute | solution.py:464
  29.6 16.8 %copy-start.4 = (bf16[8,48,384]{2,1,0:T(8,128)(2,1)}, bf16[8,48,384]{2,1,0:T(8,128)(2,1)S(1)}, u32[]{:S(2)}) copy-start(bf16[8,48,384]{2,1,0:T(8,128)(2,1)S(1)} %constant_dynamic-update-slice_fusion.refs_2_) | copy-start | bytes 884740
  29.6 16.8 %collective-permute-start.7 = (bf16[8,48,384]{2,1,0:T(8,128)(2,1)S(1)}, bf16[8,48,384]{2,1,0:T(8,128)(2,1)S(1)}, u32[]{:S(2)}, u32[]{:S(2)}) collective-permute-start(bf16[8,48,384]{2,1,0:T(8,128)(2,1)S(1)} %constant_dynamic-update-slice_fusion.refs_2_), channel_id=1, source_target_pairs={{0,8},{8,0},{16,24},{24,16},{32,40},{40,32},{48,56},{56,48},{64,72... | collective-permute-start | bytes 884744 | tf_op jit(solution)/shard_map/ppermute | solution.py:511
  33.7 18.3 %collective-permute-start.8 = (bf16[256,384]{1,0:T(8,128)(2,1)S(1)}, bf16[256,384]{1,0:T(8,128)(2,1)S(1)}, u32[]{:S(2)}, u32[]{:S(2)}) collective-permute-start(bf16[256,384]{1,0:T(8,128)(2,1)S(1)} %collective-permute-done.1.refs_3_), channel_id=1, source_target_pairs={{0,2},{1,3},{2,4},{3,5},{4,6},{5,7},{6,0},{7,1},{8,10},{9,11},{10,... | collective-permute-start | bytes 589832 | tf_op jit(solution)/shard_map/ppermute | solution.py:464
  35.4 19.2 %collective-permute-start.10 = (bf16[256,384]{1,0:T(8,128)(2,1)S(1)}, bf16[256,384]{1,0:T(8,128)(2,1)S(1)}, u32[]{:S(2)}, u32[]{:S(2)}) collective-permute-start(bf16[256,384]{1,0:T(8,128)(2,1)S(1)} %collective-permute-done.2.refs_4_), channel_id=1, source_target_pairs={{0,2},{1,3},{2,4},{3,5},{4,6},{5,7},{6,0},{7,1},{8,10},{9,11},{10,... | collective-permute-start | bytes 589832 | tf_op jit(solution)/shard_map/ppermute | solution.py:464
  44.4 14.5 %copy-start.9 = (bf16[256,384]{1,0:T(8,128)(2,1)}, bf16[256,384]{1,0:T(8,128)(2,1)S(1)}, u32[]{:S(2)}) copy-start(bf16[256,384]{1,0:T(8,128)(2,1)S(1)} %collective-permute-done.9.refs_7_) | copy-start | bytes 589828
  44.4 10.2 %collective-permute-start.11 = (bf16[256,384]{1,0:T(8,128)(2,1)S(1)}, bf16[256,384]{1,0:T(8,128)(2,1)}, u32[]{:S(2)}, u32[]{:S(2)}) collective-permute-start(bf16[256,384]{1,0:T(8,128)(2,1)S(1)} %collective-permute-done.9.refs_7_), channel_id=1, source_target_pairs={{0,6},{1,7},{2,0},{3,1},{4,2},{5,3},{6,4},{7,5},{8,14},{9,15},{10,... | collective-permute-start | bytes 589832 | tf_op jit(solution)/shard_map/ppermute | solution.py:464
  46.4 0.7 copy-start.5
  46.4 1.4 %copy-start = (bf16[8,480,256]{2,1,0:T(8,128)(2,1)}, bf16[8,480,256]{2,1,0:T(8,128)(2,1)S(1)}, u32[]{:S(2)}) copy-start(bf16[8,480,256]{2,1,0:T(8,128)(2,1)S(1)} %all-to-all-done.refs_1_) | copy-start | bytes 5898244
  52.1 6.1 %copy-start.10 = (bf16[256,384]{1,0:T(8,128)(2,1)}, bf16[256,384]{1,0:T(8,128)(2,1)S(1)}, u32[]{:S(2)}) copy-start(bf16[256,384]{1,0:T(8,128)(2,1)S(1)} %collective-permute-done.8.refs_5_) | copy-start | bytes 589828
  54.6 3.6 %copy-start.11 = (bf16[256,384]{1,0:T(8,128)(2,1)}, bf16[256,384]{1,0:T(8,128)(2,1)S(1)}, u32[]{:S(2)}) copy-start(bf16[256,384]{1,0:T(8,128)(2,1)S(1)} %collective-permute-done.10.refs_8_) | copy-start | bytes 589828
  54.6 29.5 %all-to-all-start.1 = ((bf16[8,48,2048]{2,1,0:T(8,128)(2,1)}), bf16[8,48,2048]{2,1,0:T(8,128)(2,1)S(1)}, u32[]{:S(2)}, u32[]{:S(2)}) async-start(bf16[8,48,2048]{2,1,0:T(8,128)(2,1)} %conv_input.1), calls=%async_computation.1 | async-start | bytes 3145728 | tf_op jit(solution)/shard_map/all_to_all | solution.py:529
  84.1 1.1 copy-start.1
  85.3 11.8 %copy-start.13 = (bf16[8,96,384]{2,1,0:T(8,128)(2,1)S(1)}, bf16[8,96,384]{2,1,0:T(8,128)(2,1)}, u32[]{:S(2)}) copy-start(bf16[8,96,384]{2,1,0:T(8,128)(2,1)} %get-tuple-element.79) | copy-start | bytes 1769476
  96.0 6.7 %copy-start.3 = (bf16[8,96,384]{2,1,0:T(8,128)(2,1)S(1)}, bf16[8,96,384]{2,1,0:T(8,128)(2,1)}, u32[]{:S(2)}) copy-start(bf16[8,96,384]{2,1,0:T(8,128)(2,1)} %get-tuple-element.85) | copy-start | bytes 1769476
  96.0 3.3 %collective-permute-start.13 = (bf16[512,768]{1,0:T(8,128)(2,1)}, bf16[512,768]{1,0:T(8,128)(2,1)S(1)}, u32[]{:S(2)}, u32[]{:S(2)}) collective-permute-start(bf16[512,768]{1,0:T(8,128)(2,1)} %get-tuple-element.81), channel_id=1, source_target_pairs={{0,8},{8,0},{16,24},{24,16},{32,40},{40,32},{48,56},{56,48},{64,72... | collective-permute-start | bytes 2359304 | tf_op jit(solution)/shard_map/ppermute | solution.py:618
  97.0 5.6 %collective-permute-start.12 = (bf16[8,96,384]{2,1,0:T(8,128)(2,1)S(1)}, bf16[8,96,384]{2,1,0:T(8,128)(2,1)S(1)}, u32[]{:S(2)}, u32[]{:S(2)}) collective-permute-start(bf16[8,96,384]{2,1,0:T(8,128)(2,1)S(1)} %copy-done.13), channel_id=1, source_target_pairs={{0,8},{8,0},{16,24},{24,16},{32,40},{40,32},{48,56},{56,48},{64,72... | collective-permute-start | bytes 1769480 | tf_op jit(solution)/shard_map/ppermute | solution.py:569
  99.3 0.9 copy-start.2
  102.8 12.8 %collective-permute-start.14 = (bf16[4,96,384]{2,1,0:T(8,128)(2,1)S(1)}, bf16[4,96,384]{2,1,0:T(8,128)(2,1)S(1)}, u32[]{:S(2)}, u32[]{:S(2)}) collective-permute-start(bf16[4,96,384]{2,1,0:T(8,128)(2,1)S(1)} %dynamic-slice_convert_fusion), channel_id=1, source_target_pairs={{0,16},{8,24},{16,0},{24,8},{32,48},{40,56},{48,32},{56,40},{64,80... | collective-permute-start | bytes 884744 | tf_op jit(solution)/shard_map/ppermute | solution.py:643
  103.5 29.4 %all-to-all-start.2 = ((bf16[64,8,768]{2,1,0:T(8,128)(2,1)}), bf16[64,8,768]{2,1,0:T(8,128)(2,1)S(1)}, u32[]{:S(2)}, u32[]{:S(2)}) async-start(bf16[64,8,768]{2,1,0:T(8,128)(2,1)} %bitcast.8), calls=%async_computation.2 | async-start | bytes 1572864 | tf_op jit(solution)/shard_map/all_to_all | solution.py:630
  115.7 10.5 %collective-permute-start.17 = (bf16[96,384]{1,0:T(8,128)(2,1)S(1)}, bf16[96,384]{1,0:T(8,128)(2,1)S(1)}, u32[]{:S(2)}, u32[]{:S(2)}) collective-permute-start(bf16[96,384]{1,0:T(8,128)(2,1)S(1)} %get-tuple-element.88), channel_id=1, source_target_pairs={{0,96},{8,104},{16,112},{24,120},{32,0},{40,8},{48,16},{56,24},{64... | collective-permute-start | bytes 221192 | tf_op jit(solution)/shard_map/ppermute | solution.py:648
  118.2 8.3 %collective-permute-start.16 = (bf16[96,384]{1,0:T(8,128)(2,1)S(1)}, bf16[96,384]{1,0:T(8,128)(2,1)S(1)}, u32[]{:S(2)}, u32[]{:S(2)}) collective-permute-start(bf16[96,384]{1,0:T(8,128)(2,1)S(1)} %get-tuple-element.89), channel_id=1, source_target_pairs={{0,64},{8,72},{16,80},{24,88},{32,96},{40,104},{48,112},{56,120},{... | collective-permute-start | bytes 221192 | tf_op jit(solution)/shard_map/ppermute | solution.py:648
  118.6 13.6 %collective-permute-start.15 = (bf16[96,384]{1,0:T(8,128)(2,1)S(1)}, bf16[96,384]{1,0:T(8,128)(2,1)S(1)}, u32[]{:S(2)}, u32[]{:S(2)}) collective-permute-start(bf16[96,384]{1,0:T(8,128)(2,1)S(1)} %get-tuple-element.87), channel_id=1, source_target_pairs={{0,32},{8,40},{16,48},{24,56},{32,64},{40,72},{48,80},{56,88},{64,... | collective-permute-start | bytes 221192 | tf_op jit(solution)/shard_map/ppermute | solution.py:648
